TPU v7x, 32 devices: a whole 2x2x4 slice. The times are simulated.
32 devices in a mesh: lon: 8 (over z, y), ch: 4 (over x, core).
Axes of the slice: x: 2, y: 2, z: 4, core: 2. Of those that a mesh axis runs over, the one named last changes fastest.
Arguments:
- features: bfloat16 [1024, 1, 144, 128], P('ch', None, 'lon'), may hold values from -6 to 6
- cotangent: bfloat16 [3, 256, 1, 144, 128], P(None, 'ch', None, 'lon'), may hold values from -6 to 6
- weights: bfloat16 [3, 3, 3, 256, 1024], P(None, None, None, 'ch'), may hold values from -0.0625 to 0.0625
Outputs:
- input_grad: bfloat16 [1024, 1, 144, 128], P('ch', None, 'lon')
- kernel_grad: float32 [3, 3, 3, 256, 1024], P(None, None, None, 'ch')
All inputs are finite; a program needn't handle non-finite values.
Results may differ from a plain program's by a relative error of at most 0.001.
Values may be sent and summed in bfloat16 or wider, within the bound.
No kernel may reach another device: no remote copies, remote signals or barrier semaphores. Data moves between devices by JAX's collectives and lax.ppermute only.
A program may use at most 256 MiB of HBM per device.

v0:
```python
import functools

import jax
import jax.numpy as jnp
from jax import lax
from jax.experimental import pallas as pl
from jax.experimental.pallas import tpu as pltpu
from jax.sharding import PartitionSpec as P

DILATIONS = (6, 12, 18)
TAPS = 9
GROUP = 8
REACH = 2.0**15.5
TINY = 1e-30
LEAST = 2.0**-125
MIB = 1024 * 1024
GRANT = 16 * MIB
PACE = 3e8
BLOCKS_AT = 2
ROWS_AT = 6


def cost(micros):
    return pl.CostEstimate(flops=int(micros * PACE), bytes_accessed=0, transcendentals=0)


def in_hbm(value):
    return pltpu.with_memory_space_constraint(value, pltpu.HBM)


def ring_order(count):
    return list(range(0, count, 2)) + list(range(count - 1, 0, -2))


def ring_position(index, count):
    return jnp.where(index % 2 == 0, index // 2, count - 1 - index // 2)


def bound_code(bound):
    return (bound * 1.01).astype(jnp.bfloat16)


def encode(value, bound):
    power = value * (REACH / bound.astype(jnp.float32))
    power = power * power
    power = power * power
    power = power * power
    return jnp.where(value < 0, -power, power).astype(jnp.bfloat16)


def decode(code, bound, norm):
    wide = code.astype(jnp.float32)
    fourth = lax.rsqrt(lax.rsqrt(jnp.maximum(jnp.abs(wide), LEAST)))
    root = fourth * lax.rsqrt(fourth) * (bound.astype(jnp.float32) * norm)
    return jnp.where(wide < 0, -root, root)


def direct(kernel, out_shapes, operands, name, table=None, micros=2):
    vmem = pl.BlockSpec(memory_space=pltpu.VMEM)
    smem = pl.BlockSpec(memory_space=pltpu.SMEM)
    return pl.pallas_call(
        kernel,
        in_specs=([] if table is None else [smem]) + [vmem] * len(operands),
        out_specs=[vmem] * len(out_shapes),
        out_shape=out_shapes,
        compiler_params=pltpu.CompilerParams(vmem_limit_bytes=GRANT),
        cost_estimate=cost(micros),
        name=name,
    )(*([] if table is None else [table]), *operands)


def edge_kernel(cot_ref, tail_ref, head_ref):
    cols = cot_ref.shape[1]
    start = 0
    for branch in range(3):
        dilation = DILATIONS[branch]
        tail_ref[start : start + dilation] = cot_ref[branch, cols - dilation :]
        head_ref[start : start + dilation] = cot_ref[branch, :dilation]
        start += dilation


def edges(cot):
    shape = (sum(DILATIONS),) + cot.shape[2:]
    return pl.pallas_call(
        edge_kernel,
        grid=(1,),
        in_specs=[pl.BlockSpec(cot.shape, lambda i: (0, 0, 0, 0))],
        out_specs=[pl.BlockSpec(shape, lambda i: (0, 0, 0))] * 2,
        out_shape=[jax.ShapeDtypeStruct(shape, cot.dtype)] * 2,
        compiler_params=pltpu.CompilerParams(vmem_limit_bytes=GRANT),
        cost_estimate=cost(1),
        name="edges",
    )(in_hbm(cot))


def spread_kernel(cot_ref, left_ref, right_ref, out_ref):
    cols, chans, rows = cot_ref.shape[1:]
    lane = lax.broadcasted_iota(jnp.int32, (chans, rows), 1)
    start = 0
    for branch in range(3):
        dilation = DILATIONS[branch]
        for place in range(-dilation, cols + dilation):
            if place < 0:
                column = left_ref[start + place + dilation]
            elif place >= cols:
                column = right_ref[start + place - cols]
            else:
                column = cot_ref[branch, place]
            wide = column.astype(jnp.float32)
            for lat_tap in range(3):
                shift = dilation * (lat_tap - 1)
                if shift == 0:
                    moved = column
                else:
                    keep = lane >= shift if shift > 0 else lane < rows + shift
                    moved = jnp.where(keep, pltpu.roll(wide, shift % rows, 1), 0.0)
                    moved = moved.astype(jnp.bfloat16)
                for lon_tap in range(3):
                    target = place + dilation * (lon_tap - 1)
                    if 0 <= target < cols:
                        low = (TAPS * branch + 3 * lat_tap + lon_tap) * chans
                        out_ref[low : low + chans, target * rows : (target + 1) * rows] = moved
        start += dilation


def spread(cot, left, right):
    branches, cols, chans, rows = cot.shape
    shape = jax.ShapeDtypeStruct((branches * TAPS * chans, cols * rows), jnp.bfloat16)
    return direct(spread_kernel, [shape], [cot, left, right], "spread")[0]


def flatten_kernel(place_ref, first_ref, second_ref, out_ref):
    cols, block, rows = first_ref.shape
    for ref, core in ((first_ref, place_ref[1]), (second_ref, 1 - place_ref[1])):
        at = pl.ds(pl.multiple_of(core * block, block), block)
        for col in range(cols):
            out_ref[col * rows : (col + 1) * rows, at] = jnp.transpose(ref[col])


def flatten(table, first, second):
    cols, block, rows = first.shape
    shape = jax.ShapeDtypeStruct((cols * rows, 2 * block), jnp.bfloat16)
    return direct(flatten_kernel, [shape], [first, second], "flatten", table)[0]


def kernel_terms_kernel(count, table_ref, grid_ref, feat_ref, out_ref, top_ref):
    chans = grid_ref.shape[0] // (3 * TAPS)
    parts = count // GROUP
    height = chans // GROUP
    width = feat_ref.shape[1] // parts
    deep = TAPS * chans
    top_ref[...] = jnp.full(top_ref.shape, TINY, jnp.float32)

    @pl.loop(0, 3)
    def _(branch):
        lines = grid_ref[pl.ds(pl.multiple_of(branch * deep, deep), deep)]
        sums = jnp.dot(lines, feat_ref[...], preferred_element_type=jnp.float32)
        top_ref[...] = jnp.maximum(top_ref[...], jnp.max(jnp.abs(sums)))
        for owner in range(count):
            at = lax.rem(owner - table_ref[0] + count, count)
            top = (owner % GROUP) * height
            side = (owner // GROUP) * width
            for tap in range(TAPS):
                low = tap * chans + top
                out_ref[at, branch * TAPS + tap] = sums[low : low + height, side : side + width]


def kernel_terms(table, grid, feat, count):
    wide = feat.shape[1]
    taps = 3 * TAPS
    tail = (grid.shape[0] // taps // GROUP, wide // (count // GROUP))
    shapes = [
        jax.ShapeDtypeStruct((count, taps) + tail, jnp.float32),
        jax.ShapeDtypeStruct((1,) + tail, jnp.float32),
    ]
    kernel = functools.partial(kernel_terms_kernel, count)
    return direct(kernel, shapes, [grid, feat], "kernel_terms", table, 6)


def input_terms_kernel(at, table_ref, weight_ref, grid_ref, added_ref, *out_refs):
    block, rows = out_refs[0].shape[1:]
    lines = weight_ref[pl.ds(pl.multiple_of(table_ref[at] * block, block), block)]
    done = 0
    for out_ref in out_refs:
        each = max(cols for cols in range(1, 7) if out_ref.shape[0] % cols == 0)
        for start in range(0, out_ref.shape[0], each):
            here = slice((done + start) * rows, (done + start + each) * rows)
            sums = jnp.dot(lines, grid_ref[:, here], preferred_element_type=jnp.float32)
            for col in range(each):
                part = sums[:, col * rows : (col + 1) * rows]
                if added_ref is not None:
                    part = part + added_ref[done + start + col]
                out_ref[start + col] = part
        done += out_ref.shape[0]


def input_terms(at, table, weight_rows, grid, added=None, *, block, spans, rows):
    shapes = [jax.ShapeDtypeStruct((cols, block, rows), jnp.float32) for cols in spans]
    operands = [weight_rows, grid] + ([] if added is None else [added])

    def kernel(table_ref, weight_ref, grid_ref, *refs):
        added_ref, out_refs = (None, refs) if added is None else (refs[0], refs[1:])
        input_terms_kernel(at, table_ref, weight_ref, grid_ref, added_ref, *out_refs)

    return direct(kernel, shapes, operands, "input_terms", table, 3.5)


def unfold_kernel(norm, places, table_ref, *refs):
    held = len(places)
    codes, (out_ref, plain_ref, sems) = refs[:held], refs[-3:]
    taps, height, width = plain_ref.shape[1:]
    copies = []
    for at, (row, col) in enumerate(places):
        plain_ref[at] = decode(codes[at][:taps], codes[at][taps:], norm)
        top = pl.ds(pl.multiple_of(table_ref[row] * height, height), height)
        side = pl.ds(pl.multiple_of(table_ref[col] * width, width), width)
        copies.append(
            pltpu.make_async_copy(plain_ref.at[at], out_ref.at[:, top, side], sems.at[at])
        )
        copies[-1].start()
    for copy in copies:
        copy.wait()


def unfold(places, norm, shape, table, codes, before=None):
    held = len(codes)
    vmem = pl.BlockSpec(memory_space=pltpu.VMEM)
    hbm = pl.BlockSpec(memory_space=pl.ANY)
    operands = codes + ([] if before is None else [before])
    return pl.pallas_call(
        functools.partial(unfold_kernel, norm, places),
        in_specs=[pl.BlockSpec(memory_space=pltpu.SMEM)]
        + [vmem] * held
        + ([] if before is None else [hbm]),
        out_specs=hbm,
        out_shape=pltpu.HBM(shape, jnp.float32),
        input_output_aliases={} if before is None else {held + 1: 0},
        scratch_shapes=[
            pltpu.VMEM((held, shape[0]) + codes[0].shape[1:], jnp.float32),
            pltpu.SemaphoreType.DMA((held,)),
        ],
        compiler_params=pltpu.CompilerParams(vmem_limit_bytes=GRANT),
        cost_estimate=cost(3),
        name="unfold",
    )(table, *operands)


def first_hop_kernel(cut, at, terms_ref, top_ref, up_ref, down_ref):
    taps = terms_ref.shape[1]
    bound = bound_code(top_ref[...])
    up_ref[:cut] = encode(terms_ref[at, :cut], bound)
    up_ref[cut:] = bound
    down_ref[: taps - cut] = encode(terms_ref[at, cut:], bound)
    down_ref[taps - cut :] = bound


def next_hop_kernel(cut, to_up, to_down, up_ref, down_ref, terms_ref, top_ref, up_out, down_out):
    taps = terms_ref.shape[1]
    top = top_ref[...]
    for ref, at, out_ref, low, high in (
        (up_ref, to_up, up_out, 0, cut),
        (down_ref, to_down, down_out, cut if cut < taps else 0, taps),
    ):
        arrived = ref[high - low :]
        bound = bound_code(arrived.astype(jnp.float32) + top)
        value = decode(ref[: high - low], arrived, 1.0 / REACH) + terms_ref[at, low:high]
        out_ref[low:high] = encode(value, bound)
        if low > 0:
            out_ref[:low] = encode(terms_ref[at, :low], bound)
        if high < taps:
            out_ref[high:taps] = encode(terms_ref[at, high:], bound)
        out_ref[taps:] = bound


def last_hop_kernel(up_ref, down_ref, own_ref, top_ref, out_ref):
    taps = own_ref.shape[1]
    up_bound, down_bound = up_ref[taps:], down_ref[taps:]
    bound = bound_code(
        up_bound.astype(jnp.float32) + down_bound.astype(jnp.float32) + top_ref[...]
    )
    value = own_ref[0] + decode(up_ref[:taps], up_bound, 1.0 / REACH)
    value = value + decode(down_ref[:taps], down_bound, 1.0 / REACH)
    out_ref[:taps] = encode(value, bound)
    out_ref[taps:] = bound


def hop_call(kernel, out_rows, operands, name):
    tail = operands[-1].shape[-2:]
    shapes = [jax.ShapeDtypeStruct((rows,) + tail, jnp.bfloat16) for rows in out_rows]
    return direct(kernel, shapes, operands, name)


class Order:
    def __init__(self):
        self.last = ()

    def gate(self, *values):
        if not self.last:
            return values
        return lax.optimization_barrier(values + self.last)[: len(values)]

    def pin(self, *values):
        values = self.gate(*values)
        self.last = (values[0],)
        return values

    def __call__(self, kernel, *values):
        result = kernel(*self.gate(*values))
        self.last = (jax.tree.leaves(result)[0],)
        return result


class Ring:
    def __init__(self, count, taps):
        order = ring_order(count)
        self.ahead = [(order[i], order[(i + 1) % count]) for i in range(count)]
        self.behind = [(b, a) for a, b in self.ahead]
        self.count, self.half = count, count // 2
        self.taps, self.cut = taps, (taps + 1) // 2

    def send(self, messages):
        up, down = messages
        return lax.ppermute(up, "lon", self.ahead), lax.ppermute(down, "lon", self.behind)

    def first(self, terms, top):
        kernel = functools.partial(first_hop_kernel, self.cut, self.half)
        rows = [self.cut + 1, self.taps - self.cut + 1]
        return hop_call(kernel, rows, [terms, top], "first_hop")

    def next(self, left, messages, terms, top):
        cut = self.cut if left == self.half else self.taps
        kernel = functools.partial(next_hop_kernel, cut, left - 1, self.count - left + 1)
        return hop_call(kernel, [self.taps + 1] * 2, [*messages, terms, top], "next_hop")

    def last(self, messages, terms, top):
        return hop_call(last_hop_kernel, [self.taps + 1], [*messages, terms, top], "last_hop")[0]


class Chain:
    def __init__(self, ring, order, side, terms, top):
        self.ring, self.order, self.side = ring, order, side
        self.terms, self.top, self.left = terms, top, ring.half
        self.out = order(ring.first, terms, top)
        self.codes = []

    def arrive(self):
        self.out = self.order.pin(*self.ring.send(self.out))

    def hop(self):
        run = functools.partial(self.ring.next, self.left)
        self.out = self.order(run, self.out, self.terms, self.top)
        self.left -= 1

    def last(self):
        own = self.order(self.ring.last, self.out, self.terms, self.top)
        self.out = (own, own)
        self.keep(0, own)

    def keep(self, ahead, code):
        count = self.ring.count
        self.codes.append(
            ((ROWS_AT + ahead, ROWS_AT + count + 2 * ahead + self.side), code)
        )

    def take(self):
        taken, self.codes = self.codes, []
        return taken

    def move(self):
        ring, (up, down) = self.ring, self.out
        if self.left < ring.half:
            self.out = self.order.pin(*ring.send((up, down)))
            self.keep(ring.count - self.left, self.out[0])
            self.keep(self.left, self.out[1])
        else:
            cut = ring.cut
            parts = self.order.pin(*ring.send((up[:cut], down[cut:])))
            self.keep(ring.half, jnp.concatenate(parts, axis=0))
        self.left += 1


def make_table(lon, ch, count):
    place_x, place_core = ch // 2, ch % 2
    spot = ring_position(lon, count)
    owners = (spot + jnp.arange(count, dtype=jnp.int32)) % count
    sides = jnp.stack([place_x, 1 - place_x]) * (count // GROUP)
    return jnp.concatenate(
        [
            jnp.stack([spot, place_core, 3 - ch, ch ^ 2, ch ^ 1, ch]),
            owners % GROUP,
            (owners[:, None] // GROUP + sides[None]).reshape(-1),
        ]
    ).astype(jnp.int32)


def local(features, cotangent, weights):
    block, _, cols, rows = features.shape
    chans = cotangent.shape[1]
    total = weights.shape[4]
    count = lax.axis_size("lon")
    cells = cols * count * rows

    feat = jnp.transpose(features.reshape(block, cols, rows), (1, 0, 2))
    cot = jnp.transpose(cotangent.reshape(3, chans, cols, rows), (0, 2, 1, 3))
    order = Order()

    tails, heads = order(edges, cot)
    left = lax.ppermute(tails, "lon", [(i, (i + 1) % count) for i in range(count)])
    right = lax.ppermute(heads, "lon", [((i + 1) % count, i) for i in range(count)])

    to_core = [(i, i ^ 1) for i in range(4)]
    to_x = [(i, i ^ 2) for i in range(4)]
    far = lax.ppermute(feat, "ch", to_x)
    near = lax.ppermute(feat, "ch", to_core)

    norm = 1.0 / (REACH * cells**0.5)
    ring = Ring(count, 3 * TAPS)
    table = order(
        functools.partial(make_table, count=count), lax.axis_index("lon"), lax.axis_index("ch")
    )
    weight_rows = order(jnp.transpose, weights.reshape(-1, total))
    flat_near = order(flatten, table, feat, near)
    left, right, far = order.gate(left, right, far)
    grid = order(spread, cot, left, right)
    far_near = lax.ppermute(far, "ch", to_core)

    def terms_of(which, spans, *added):
        run = functools.partial(
            input_terms, BLOCKS_AT + which, block=block, spans=spans, rows=rows
        )
        return order(run, table, weight_rows, grid, *added)

    def features_with(flat):
        return order(functools.partial(kernel_terms, count=count), table, grid, flat)

    half = ring.half
    most, whole = (cols * 5 // 6, cols // 6), (cols,)
    shape = (3 * TAPS, chans, total)
    written = []

    def write(*chains):
        taken = [item for chain in chains for item in chain.take()]
        places, codes = zip(*taken)
        run = functools.partial(unfold, places, norm, shape)
        written[:] = [order(run, table, list(codes), *written)]

    near = Chain(ring, order, 0, *features_with(flat_near))
    flat_far = order(flatten, table, far, far_near)
    (away,) = terms_of(0, whole)
    near.arrive()
    near.hop()
    away = lax.ppermute(order.gate(away)[0], "ch", to_core)
    far = Chain(ring, order, 1, *features_with(flat_far))
    across = list(terms_of(1, most, away))
    near.arrive()
    near.hop()
    far.arrive()
    far.hop()
    across[0] = lax.ppermute(order.gate(across[0])[0], "ch", to_x)
    (beside,) = terms_of(2, whole)
    for _ in range(half - 4):
        near.arrive()
        near.hop()
        far.arrive()
        far.hop()
    near.arrive()
    near.hop()
    far.arrive()
    far.hop()
    (mine,) = terms_of(3, whole)
    near.arrive()
    near.last()
    far.arrive()
    far.hop()
    near.move()
    far.arrive()
    far.last()
    write(near)
    near.move()
    far.move()
    for _ in range(half - 4):
        near.move()
        far.move()
    write(near, far)
    near.move()
    far.move()
    across[0] = order.pin(across[0])[0]
    across[1] = lax.ppermute(order.gate(across[1])[0], "ch", to_x)
    write(near, far)
    near.move()
    beside = lax.ppermute(order.gate(beside)[0], "ch", to_core)
    far.move()
    write(near, far)
    across = jnp.concatenate(across, axis=0)
    input_grad = order(lambda *parts: sum(parts).astype(jnp.bfloat16), mine, beside, across)
    far.move()
    write(far)
    kernel_grad = written[0]

    input_grad = jnp.transpose(input_grad, (1, 0, 2)).reshape(block, 1, cols, rows)
    return (input_grad, kernel_grad.reshape(3, 3, 3, chans, total))


def solution(mesh):
    return jax.shard_map(
        local,
        mesh=mesh,
        in_specs=(
            P("ch", None, "lon", None),
            P(None, "ch", None, "lon", None),
            P(None, None, None, "ch", None),
        ),
        out_specs=(P("ch", None, "lon", None), P(None, None, None, "ch", None)),
        check_vma=False,
    )
```

profile of v0, /device:TPU:0, one launch (start us, length us, event | category | flops | bytes accessed | tf_op | source)
XLA Modules:
  0.0 139.5 jit_solution(12390096348833539477)
XLA Ops:
  1.1 2.6 %collective-permute-start.2 = (bf16[18,256,128]{2,1,0:T(8,128)(2,1)}, bf16[18,256,128]{2,1,0:T(8,128)(2,1)S(1)}, u32[]{:S(2)}, u32[]{:S(2)}) collective-permute-start(bf16[18,256,128]{2,1,0:T(8,128)(2,1)} %bitcast.25), channel_id=1, source_target_pairs={{0,2},{1,3},{2,0},{3,1},{4,6},{5,7},{6,4},{7,5},{8,10},{9,11},{10,... | collective-permute-start | bytes 3538952 | tf_op jit(solution)/shard_map/ppermute | solution.py:413
  3.7 2.3 %edges.1 = (bf16[36,64,128]{2,1,0:T(8,128)(2,1)}, bf16[36,64,128]{2,1,0:T(8,128)(2,1)}) custom-call(bf16[3,18,64,128]{3,2,1,0:T(8,128)(2,1)} %bitcast.27), custom_call_target="tpu_custom_call" | custom-call | flops 300000000 | tf_op jit(solution)/shard_map/edges/pallas_call | solution.py:84
  6.0 4.6 %collective-permute-start.1 = (bf16[36,64,128]{2,1,0:T(8,128)(2,1)}, bf16[36,64,128]{2,1,0:T(8,128)(2,1)}, u32[]{:S(2)}, u32[]{:S(2)}) collective-permute-start(bf16[36,64,128]{2,1,0:T(8,128)(2,1)} %get-tuple-element.165), channel_id=1, source_target_pairs={{4,0},{8,4},{12,8},{16,12},{20,16},{24,20},{28,24},{0,28},{5,1},{9... | collective-permute-start | bytes 1769480 | tf_op jit(solution)/shard_map/ppermute | solution.py:409
  11.0 5.9 %copy.10 = bf16[1728,1024]{0,1:T(8,128)(2,1)} copy(bf16[1728,1024]{1,0:T(8,128)(2,1)} %bitcast.30) | data formatting | bytes 7077888 | tf_op jit(solution)/shard_map/optimization_barrier | solution.py:300
  16.8 1.2 flatten.2.feat_ref
  18.0 16.3 %collective-permute-done.1.right_ref = bf16[36,64,128]{2,1,0:T(8,128)(2,1)} collective-permute-done((bf16[36,64,128]{2,1,0:T(8,128)(2,1)}, bf16[36,64,128]{2,1,0:T(8,128)(2,1)}, u32[]{:S(2)}, u32[]{:S(2)}) %collective-permute-start.1) | collective-permute-done | bytes 589856 | tf_op jit(solution)/shard_map/ppermute | solution.py:409
  34.4 2.5 %spread.1.grid_ref = bf16[1728,2304]{1,0:T(8,128)(2,1)S(1)} custom-call(bf16[3,18,64,128]{3,2,1,0:T(8,128)(2,1)S(1)} %bitcast.28, bf16[36,64,128]{2,1,0:T(8,128)(2,1)} %collective-permute-done.left_ref, bf16[36,64,128]{2,1,0:T(8,128)(2,1)} %collective-permute-done.1.right_ref), custom_call_target="tpu_custom_call" | custom-call | flops 600000000 | tf_op jit(solution)/shard_map/spread/pallas_call | solution.py:61
  36.9 5.6 %kernel_terms.2 = (f32[8,27,8,512]{3,2,1,0:T(8,128)S(1)}, f32[1,8,512]{2,1,0:T(8,128)S(1)}) custom-call(s32[30]{0:T(128)S(1)} %concatenate.12.place_ref.table_ref, bf16[1728,2304]{1,0:T(8,128)(2,1)S(1)} %spread.1.grid_ref, bf16[2304,512]{1,0:T(8,128)(2,1)S(1)} %flatten.2.feat_ref), custom_call_target="tpu_custom_call" | custom-call | flops 1800000000 | tf_op jit(solution)/shard_map/kernel_terms/pallas_call | solution.py:61
  42.6 2.5 %collective-permute-start.6 = (bf16[14,8,512]{2,1,0:T(8,128)(2,1)S(1)}, bf16[14,8,512]{2,1,0:T(8,128)(2,1)S(1)}, u32[]{:S(2)}, u32[]{:S(2)}) collective-permute-start(bf16[14,8,512]{2,1,0:T(8,128)(2,1)S(1)} %get-tuple-element.186), channel_id=1, source_target_pairs={{8,0},{16,8},{24,16},{28,24},{20,28},{12,20},{4,12},{0,4},{9,1},{1... | collective-permute-start | bytes 344072 | tf_op jit(solution)/shard_map/ppermute | solution.py:323
  45.1 1.2 flatten.3.feat_ref
  46.4 0.8 copy-done
  47.2 2.8 %input_terms.4 = f32[18,256,128]{2,1,0:T(8,128)S(1)} custom-call(s32[30]{0:T(128)S(1)} %concatenate.12.place_ref.table_ref, bf16[1024,1728]{1,0:T(8,128)(2,1)S(1)} %bitcast.20, bf16[1728,2304]{1,0:T(8,128)(2,1)S(1)} %spread.1.grid_ref), custom_call_target="tpu_custom_call" | custom-call | flops 1050000000 | tf_op jit(solution)/shard_map/input_terms/pallas_call | solution.py:61
  51.4 1.7 %collective-permute-start.10 = (bf16[28,8,512]{2,1,0:T(8,128)(2,1)S(1)}, bf16[28,8,512]{2,1,0:T(8,128)(2,1)S(1)}, u32[]{:S(2)}, u32[]{:S(2)}) collective-permute-start(bf16[28,8,512]{2,1,0:T(8,128)(2,1)S(1)} %get-tuple-element.206), channel_id=1, source_target_pairs={{8,0},{16,8},{24,16},{28,24},{20,28},{12,20},{4,12},{0,4},{9,1},{1... | collective-permute-start | bytes 688136 | tf_op jit(solution)/shard_map/ppermute | solution.py:323
  53.2 5.6 %kernel_terms.3 = (f32[8,27,8,512]{3,2,1,0:T(8,128)S(1)}, f32[1,8,512]{2,1,0:T(8,128)S(1)}) custom-call(s32[30]{0:T(128)S(1)} %concatenate.12.place_ref.table_ref, bf16[1728,2304]{1,0:T(8,128)(2,1)S(1)} %spread.1.grid_ref, bf16[2304,512]{1,0:T(8,128)(2,1)S(1)} %flatten.3.feat_ref), custom_call_target="tpu_custom_call" | custom-call | flops 1800000000 | tf_op jit(solution)/shard_map/kernel_terms/pallas_call | solution.py:61
  58.9 1.0 collective-permute-start.8
  59.9 1.1 collective-permute-start.7
  61.0 3.4 %input_terms.5 = (f32[15,256,128]{2,1,0:T(8,128)S(1)}, f32[3,256,128]{2,1,0:T(8,128)S(1)}) custom-call(s32[30]{0:T(128)S(1)} %concatenate.12.place_ref.table_ref, bf16[1024,1728]{1,0:T(8,128)(2,1)S(1)} %bitcast.21, bf16[1728,2304]{1,0:T(8,128)(2,1)S(1)} %spread.1.grid_ref, f32[18,256,128]{2,1,0:T(8,128)S(1)} %collective-permute-done.11.refs_0_), custom_call_target="tpu_custom_call" | custom-call | flops 1050000000 | tf_op jit(solution)/shard_map/input_terms/pallas_call | solution.py:61
  64.4 0.6 next_hop.7
  66.1 1.3 collective-permute-start.15
  67.4 0.7 collective-permute-start.14
  68.1 1.3 collective-permute-start.13
  69.4 0.7 collective-permute-start.12
  70.2 2.8 %input_terms.6 = f32[18,256,128]{2,1,0:T(8,128)S(1)} custom-call(s32[30]{0:T(128)S(1)} %concatenate.12.place_ref.table_ref, bf16[1024,1728]{1,0:T(8,128)(2,1)S(1)} %bitcast.22, bf16[1728,2304]{1,0:T(8,128)(2,1)S(1)} %spread.1.grid_ref), custom_call_target="tpu_custom_call" | custom-call | flops 1050000000 | tf_op jit(solution)/shard_map/input_terms/pallas_call | solution.py:61
  73.0 1.6 %collective-permute-done.15.down_ref = bf16[28,8,512]{2,1,0:T(8,128)(2,1)S(1)} collective-permute-done((bf16[28,8,512]{2,1,0:T(8,128)(2,1)S(1)}, bf16[28,8,512]{2,1,0:T(8,128)(2,1)S(1)}, u32[]{:S(2)}, u32[]{:S(2)}) %collective-permute-start.15) | collective-permute-done | bytes 229408 | tf_op jit(solution)/shard_map/ppermute | solution.py:323
  74.7 1.3 collective-permute-done.14.up_ref
  76.5 1.4 %collective-permute-start.17 = (bf16[28,8,512]{2,1,0:T(8,128)(2,1)S(1)}, bf16[28,8,512]{2,1,0:T(8,128)(2,1)S(1)}, u32[]{:S(2)}, u32[]{:S(2)}) collective-permute-start(bf16[28,8,512]{2,1,0:T(8,128)(2,1)S(1)} %get-tuple-element.249), channel_id=1, source_target_pairs={{8,0},{16,8},{24,16},{28,24},{20,28},{12,20},{4,12},{0,4},{9,1},{1... | collective-permute-start | bytes 688136 | tf_op jit(solution)/shard_map/ppermute | solution.py:323
  78.0 0.6 collective-permute-start.16
  78.6 0.9 collective-permute-done.13.down_ref
  79.6 1.3 collective-permute-done.12.up_ref
  81.5 1.4 %collective-permute-start.21 = (bf16[28,8,512]{2,1,0:T(8,128)(2,1)S(1)}, bf16[28,8,512]{2,1,0:T(8,128)(2,1)S(1)}, u32[]{:S(2)}, u32[]{:S(2)}) collective-permute-start(bf16[28,8,512]{2,1,0:T(8,128)(2,1)S(1)} %get-tuple-element.256), channel_id=1, source_target_pairs={{8,0},{16,8},{24,16},{28,24},{20,28},{12,20},{4,12},{0,4},{9,1},{1... | collective-permute-start | bytes 688136 | tf_op jit(solution)/shard_map/ppermute | solution.py:323
  82.9 0.6 collective-permute-start.20
  83.5 2.8 %input_terms.7 = f32[18,256,128]{2,1,0:T(8,128)S(1)} custom-call(s32[30]{0:T(128)S(1)} %concatenate.12.place_ref.table_ref, bf16[1024,1728]{1,0:T(8,128)(2,1)S(1)} %bitcast.23, bf16[1728,2304]{1,0:T(8,128)(2,1)S(1)} %spread.1.grid_ref), custom_call_target="tpu_custom_call" | custom-call | flops 1050000000 | tf_op jit(solution)/shard_map/input_terms/pallas_call | solution.py:61
  86.9 1.4 %collective-permute-start.19 = (bf16[28,8,512]{2,1,0:T(8,128)(2,1)S(1)}, bf16[28,8,512]{2,1,0:T(8,128)(2,1)S(1)}, u32[]{:S(2)}, u32[]{:S(2)}) collective-permute-start(bf16[28,8,512]{2,1,0:T(8,128)(2,1)S(1)} %last_hop.2.refs_0_), channel_id=1, source_target_pairs={{8,0},{16,8},{24,16},{28,24},{20,28},{12,20},{4,12},{0,4},{9,1},{1... | collective-permute-start | bytes 688136 | tf_op jit(solution)/shard_map/ppermute | solution.py:323
  88.3 0.6 collective-permute-start.18
  89.0 1.1 collective-permute-done.21.down_ref
  91.3 1.5 %collective-permute-start.25 = (bf16[28,8,512]{2,1,0:T(8,128)(2,1)S(1)}, bf16[28,8,512]{2,1,0:T(8,128)(2,1)S(1)}, u32[]{:S(2)}, u32[]{:S(2)}) collective-permute-start(bf16[28,8,512]{2,1,0:T(8,128)(2,1)S(1)} %get-tuple-element.266), channel_id=1, source_target_pairs={{8,0},{16,8},{24,16},{28,24},{20,28},{12,20},{4,12},{0,4},{9,1},{1... | collective-permute-start | bytes 688136 | tf_op jit(solution)/shard_map/ppermute | solution.py:323
  93.3 1.4 %collective-permute-done.19.refs_2_ = bf16[28,8,512]{2,1,0:T(8,128)(2,1)S(1)} collective-permute-done((bf16[28,8,512]{2,1,0:T(8,128)(2,1)S(1)}, bf16[28,8,512]{2,1,0:T(8,128)(2,1)S(1)}, u32[]{:S(2)}, u32[]{:S(2)}) %collective-permute-start.19) | collective-permute-done | bytes 229408 | tf_op jit(solution)/shard_map/ppermute | solution.py:323
  94.8 2.1 %collective-permute-done.18.refs_1_ = bf16[28,8,512]{2,1,0:T(8,128)(2,1)S(1)} collective-permute-done((bf16[28,8,512]{2,1,0:T(8,128)(2,1)S(1)}, bf16[28,8,512]{2,1,0:T(8,128)(2,1)S(1)}, u32[]{:S(2)}, u32[]{:S(2)}) %collective-permute-start.18) | collective-permute-done | bytes 229408 | tf_op jit(solution)/shard_map/ppermute | solution.py:323
  96.9 0.6 collective-permute-start.22
  97.8 2.5 %collective-permute-done.24.up_ref = bf16[28,8,512]{2,1,0:T(8,128)(2,1)S(1)} collective-permute-done((bf16[28,8,512]{2,1,0:T(8,128)(2,1)S(1)}, bf16[28,8,512]{2,1,0:T(8,128)(2,1)S(1)}, u32[]{:S(2)}, u32[]{:S(2)}) %collective-permute-start.24) | collective-permute-done | bytes 229408 | tf_op jit(solution)/shard_map/ppermute | solution.py:323
  100.3 1.6 %collective-permute-start.23 = (bf16[28,8,512]{2,1,0:T(8,128)(2,1)S(1)}, bf16[28,8,512]{2,1,0:T(8,128)(2,1)S(1)}, u32[]{:S(2)}, u32[]{:S(2)}) collective-permute-start(bf16[28,8,512]{2,1,0:T(8,128)(2,1)S(1)} %collective-permute-done.19.refs_2_), channel_id=1, source_target_pairs={{8,0},{16,8},{24,16},{28,24},{20,28},{12,20},{4,12},{0,4},{9,1},{1... | collective-permute-start | bytes 688136 | tf_op jit(solution)/shard_map/ppermute | solution.py:323
  102.4 2.0 %collective-permute-start.29 = (bf16[28,8,512]{2,1,0:T(8,128)(2,1)S(1)}, bf16[28,8,512]{2,1,0:T(8,128)(2,1)S(1)}, u32[]{:S(2)}, u32[]{:S(2)}) collective-permute-start(bf16[28,8,512]{2,1,0:T(8,128)(2,1)S(1)} %last_hop.3.refs_2_), channel_id=1, source_target_pairs={{8,0},{16,8},{24,16},{28,24},{20,28},{12,20},{4,12},{0,4},{9,1},{1... | collective-permute-start | bytes 688136 | tf_op jit(solution)/shard_map/ppermute | solution.py:323
  104.5 1.9 %unfold.5.refs_5_ = f32[27,64,1024]{2,1,0:T(8,128)} custom-call(s32[30]{0:T(128)S(1)} %concatenate.12.place_ref.table_ref, bf16[28,8,512]{2,1,0:T(8,128)(2,1)S(1)} %last_hop.2.refs_0_, bf16[28,8,512]{2,1,0:T(8,128)(2,1)S(1)} %collective-permute-done.18.refs_1_, bf16[28,8,512]{2,1,0:T(8,128)(2,1)S(1)} %collective-permute-done.19.refs_2_), custom_call_target="tpu_custom_call" | custom-call | flops 900000000 | tf_op jit(solution)/shard_map/unfold/pallas_call | solution.py:230
  106.3 1.4 collective-permute-done.23.refs_1_
  107.7 1.7 %collective-permute-start.27 = (bf16[28,8,512]{2,1,0:T(8,128)(2,1)S(1)}, bf16[28,8,512]{2,1,0:T(8,128)(2,1)S(1)}, u32[]{:S(2)}, u32[]{:S(2)}) collective-permute-start(bf16[28,8,512]{2,1,0:T(8,128)(2,1)S(1)} %collective-permute-done.23.refs_1_), channel_id=1, source_target_pairs={{8,0},{16,8},{24,16},{28,24},{20,28},{12,20},{4,12},{0,4},{9,1},{1... | collective-permute-start | bytes 688136 | tf_op jit(solution)/shard_map/ppermute | solution.py:323
  109.8 2.0 %collective-permute-done.29.refs_4_ = bf16[28,8,512]{2,1,0:T(8,128)(2,1)S(1)} collective-permute-done((bf16[28,8,512]{2,1,0:T(8,128)(2,1)S(1)}, bf16[28,8,512]{2,1,0:T(8,128)(2,1)S(1)}, u32[]{:S(2)}, u32[]{:S(2)}) %collective-permute-start.29) | collective-permute-done | bytes 229408 | tf_op jit(solution)/shard_map/ppermute | solution.py:323
  111.7 1.0 collective-permute-done.28.refs_3_
  112.8 0.9 collective-permute-start.32
  113.7 1.1 collective-permute-start.33
  114.8 2.2 %unfold.6.refs_4_ = f32[27,64,1024]{2,1,0:T(8,128)} custom-call(s32[30]{0:T(128)S(1)} %concatenate.12.place_ref.table_ref, bf16[28,8,512]{2,1,0:T(8,128)(2,1)S(1)} %collective-permute-done.22.refs_0_, bf16[28,8,512]{2,1,0:T(8,128)(2,1)S(1)} %collective-permute-done.23.refs_1_, ...), custom_call_target="tpu_custom_call", output_to_operand_aliasing={{}: (6, {})} | custom-call | flops 900000000 | tf_op jit(solution)/shard_map/unfold/pallas_call | solution.py:230
  117.1 1.0 collective-permute-start.30
  118.1 1.1 collective-permute-start.31
  119.7 2.0 %unfold.7.refs_3_ = f32[27,64,1024]{2,1,0:T(8,128)} custom-call(s32[30]{0:T(128)S(1)} %concatenate.12.place_ref.table_ref, bf16[28,8,512]{2,1,0:T(8,128)(2,1)S(1)} %collective-permute-done.26.refs_0_, bf16[28,8,512]{2,1,0:T(8,128)(2,1)S(1)} %collective-permute-done.27.refs_1_, ...), custom_call_target="tpu_custom_call", output_to_operand_aliasing={{}: (5, {})} | custom-call | flops 900000000 | tf_op jit(solution)/shard_map/unfold/pallas_call | solution.py:230
  121.9 0.9 collective-permute-done.31
  122.9 1.1 collective-permute-start.38
  124.0 0.9 collective-permute-start.37
  124.9 1.5 %collective-permute-start.36 = (f32[3,256,128]{2,1,0:T(8,128)S(1)}, f32[3,256,128]{2,1,0:T(8,128)S(1)}, u32[]{:S(2)}, u32[]{:S(2)}) collective-permute-start(f32[3,256,128]{2,1,0:T(8,128)S(1)} %get-tuple-element.303), channel_id=1, source_target_pairs={{0,2},{1,3},{2,0},{3,1},{4,6},{5,7},{6,4},{7,5},{8,10},{9,11},{10,... | collective-permute-start | bytes 1179656 | tf_op jit(solution)/shard_map/ppermute | solution.py:488
  126.4 4.5 %collective-permute-done.38.refs_2_ = bf16[28,8,512]{2,1,0:T(8,128)(2,1)S(1)} collective-permute-done((bf16[28,8,512]{2,1,0:T(8,128)(2,1)S(1)}, bf16[28,8,512]{2,1,0:T(8,128)(2,1)S(1)}, u32[]{:S(2)}, u32[]{:S(2)}) %collective-permute-start.38) | collective-permute-done | bytes 229408 | tf_op jit(solution)/shard_map/ppermute | solution.py:323
  130.9 0.8 collective-permute-done.37.refs_1_
  131.8 1.3 collective-permute-start.40
  133.0 0.8 collective-permute-start.39
  133.8 1.9 %unfold.8.refs_1_ = f32[27,64,1024]{2,1,0:T(8,128)} custom-call(s32[30]{0:T(128)S(1)} %concatenate.12.place_ref.table_ref, bf16[28,8,512]{2,1,0:T(8,128)(2,1)S(1)} %pad_maximum_fusion.1.refs_0_, bf16[28,8,512]{2,1,0:T(8,128)(2,1)S(1)} %collective-permute-done.37.refs_1_, ...), custom_call_target="tpu_custom_call", output_to_operand_aliasing={{}: (4, {})} | custom-call | flops 900000000 | tf_op jit(solution)/shard_map/unfold/pallas_call | solution.py:230
  136.0 1.6 %add_convert_fusion = bf16[18,256,128]{2,1,0:T(8,128)(2,1)} fusion(f32[18,256,128]{2,1,0:T(8,128)S(1)} %pad_maximum_fusion, f32[18,256,128]{2,1,0:T(8,128)S(1)} %input_terms.7, f32[18,256,128]{2,1,0:T(8,128)S(1)} %collective-permute-done.35), kind=kLoop, calls=%fused_computation.1 | loop fusion | flops 1769472 | bytes 8257536 | tf_op jit(solution)/shard_map/convert_element_type | solution.py:495
  137.8 1.5 %unfold.9 = f32[27,64,1024]{2,1,0:T(8,128)} custom-call(s32[30]{0:T(128)S(1)} %concatenate.12.place_ref.table_ref, bf16[28,8,512]{2,1,0:T(8,128)(2,1)S(1)} %pad_maximum_fusion.2.refs_0_, f32[27,64,1024]{2,1,0:T(8,128)} %unfold.8.refs_1_), custom_call_target="tpu_custom_call", output_to_operand_aliasing={{}: (2, {})} | custom-call | flops 900000000 | tf_op jit(solution)/shard_map/unfold/pallas_call | solution.py:230
  (64 shorter events, 9.6 us)
Async XLA Ops:
  0.6 16.2 %collective-permute-start.3 = (bf16[18,256,128]{2,1,0:T(8,128)(2,1)}, bf16[18,256,128]{2,1,0:T(8,128)(2,1)S(1)}, u32[]{:S(2)}, u32[]{:S(2)}) collective-permute-start(bf16[18,256,128]{2,1,0:T(8,128)(2,1)} %bitcast.24), channel_id=1, source_target_pairs={{0,1},{1,0},{2,3},{3,2},{4,5},{5,4},{6,7},{7,6},{8,9},{9,8},{10,11... | collective-permute-start | bytes 3538952 | tf_op jit(solution)/shard_map/ppermute | solution.py:414
  1.1 33.2 %collective-permute-start.2 = (bf16[18,256,128]{2,1,0:T(8,128)(2,1)}, bf16[18,256,128]{2,1,0:T(8,128)(2,1)S(1)}, u32[]{:S(2)}, u32[]{:S(2)}) collective-permute-start(bf16[18,256,128]{2,1,0:T(8,128)(2,1)} %bitcast.25), channel_id=1, source_target_pairs={{0,2},{1,3},{2,0},{3,1},{4,6},{5,7},{6,4},{7,5},{8,10},{9,11},{10,... | collective-permute-start | bytes 3538952 | tf_op jit(solution)/shard_map/ppermute | solution.py:413
  6.0 28.4 %collective-permute-start.1 = (bf16[36,64,128]{2,1,0:T(8,128)(2,1)}, bf16[36,64,128]{2,1,0:T(8,128)(2,1)}, u32[]{:S(2)}, u32[]{:S(2)}) collective-permute-start(bf16[36,64,128]{2,1,0:T(8,128)(2,1)} %get-tuple-element.165), channel_id=1, source_target_pairs={{4,0},{8,4},{12,8},{16,12},{20,16},{24,20},{28,24},{0,28},{5,1},{9... | collective-permute-start | bytes 1769480 | tf_op jit(solution)/shard_map/ppermute | solution.py:409
  10.6 23.8 %collective-permute-start = (bf16[36,64,128]{2,1,0:T(8,128)(2,1)}, bf16[36,64,128]{2,1,0:T(8,128)(2,1)}, u32[]{:S(2)}, u32[]{:S(2)}) collective-permute-start(bf16[36,64,128]{2,1,0:T(8,128)(2,1)} %get-tuple-element.161), channel_id=1, source_target_pairs={{0,4},{4,8},{8,12},{12,16},{16,20},{20,24},{24,28},{28,0},{1,5},{5... | collective-permute-start | bytes 1769480 | tf_op jit(solution)/shard_map/ppermute | solution.py:408
  10.9 5.9 %copy-start.1 = (bf16[256,1,18,128]{3,0,2,1:T(8,128)(2,1)S(1)}, bf16[256,1,18,128]{3,0,2,1:T(8,128)(2,1)}, u32[]{:S(2)}) copy-start(bf16[256,1,18,128]{3,0,2,1:T(8,128)(2,1)} %param.3) | copy-start | bytes 3538948
  16.8 17.6 %copy-start.2 = (bf16[3,64,1,18,128]{4,1,3,2,0:T(8,128)(2,1)S(1)}, bf16[3,64,1,18,128]{4,1,3,2,0:T(8,128)(2,1)}, u32[]{:S(2)}) copy-start(bf16[3,64,1,18,128]{4,1,3,2,0:T(8,128)(2,1)} %param.4) | copy-start | bytes 2654212
  34.4 10.8 %collective-permute-start.4 = (bf16[18,256,128]{2,1,0:T(8,128)(2,1)S(1)}, bf16[18,256,128]{2,1,0:T(8,128)(2,1)S(1)}, u32[]{:S(2)}, u32[]{:S(2)}) collective-permute-start(bf16[18,256,128]{2,1,0:T(8,128)(2,1)S(1)} %collective-permute-done.2.first_ref), channel_id=1, source_target_pairs={{0,1},{1,0},{2,3},{3,2},{4,5},{5,4},{6,7},{7,6},{8,9},{9,8},{10,11... | collective-permute-start | bytes 3538952 | tf_op jit(solution)/shard_map/ppermute | solution.py:425
  42.6 7.4 %collective-permute-start.6 = (bf16[14,8,512]{2,1,0:T(8,128)(2,1)S(1)}, bf16[14,8,512]{2,1,0:T(8,128)(2,1)S(1)}, u32[]{:S(2)}, u32[]{:S(2)}) collective-permute-start(bf16[14,8,512]{2,1,0:T(8,128)(2,1)S(1)} %get-tuple-element.186), channel_id=1, source_target_pairs={{8,0},{16,8},{24,16},{28,24},{20,28},{12,20},{4,12},{0,4},{9,1},{1... | collective-permute-start | bytes 344072 | tf_op jit(solution)/shard_map/ppermute | solution.py:323
  45.1 2.0 %copy-start = (bf16[1728,1024]{0,1:T(8,128)(2,1)S(1)}, bf16[1728,1024]{0,1:T(8,128)(2,1)}, u32[]{:S(2)}) copy-start(bf16[1728,1024]{0,1:T(8,128)(2,1)} %copy.10) | copy-start | bytes 10616836
  45.1 5.4 %collective-permute-start.5 = (bf16[15,8,512]{2,1,0:T(8,128)(2,1)S(1)}, bf16[15,8,512]{2,1,0:T(8,128)(2,1)S(1)}, u32[]{:S(2)}, u32[]{:S(2)}) collective-permute-start(bf16[15,8,512]{2,1,0:T(8,128)(2,1)S(1)} %get-tuple-element.182), channel_id=1, source_target_pairs={{0,8},{8,16},{16,24},{24,28},{28,20},{20,12},{12,4},{4,0},{1,9},{9... | collective-permute-start | bytes 368648 | tf_op jit(solution)/shard_map/ppermute | solution.py:323
  51.0 10.0 %collective-permute-start.11 = (f32[18,256,128]{2,1,0:T(8,128)S(1)}, f32[18,256,128]{2,1,0:T(8,128)S(1)}, u32[]{:S(2)}, u32[]{:S(2)}) collective-permute-start(f32[18,256,128]{2,1,0:T(8,128)S(1)} %input_terms.4), channel_id=1, source_target_pairs={{0,1},{1,0},{2,3},{3,2},{4,5},{5,4},{6,7},{7,6},{8,9},{9,8},{10,11... | collective-permute-start | bytes 7077896 | tf_op jit(solution)/shard_map/ppermute | solution.py:452
  51.1 13.3 %collective-permute-start.9 = (bf16[28,8,512]{2,1,0:T(8,128)(2,1)S(1)}, bf16[28,8,512]{2,1,0:T(8,128)(2,1)S(1)}, u32[]{:S(2)}, u32[]{:S(2)}) collective-permute-start(bf16[28,8,512]{2,1,0:T(8,128)(2,1)S(1)} %get-tuple-element.196), channel_id=1, source_target_pairs={{0,8},{8,16},{16,24},{24,28},{28,20},{20,12},{12,4},{4,0},{1,9},{9... | collective-permute-start | bytes 688136 | tf_op jit(solution)/shard_map/ppermute | solution.py:323
  51.4 13.0 %collective-permute-start.10 = (bf16[28,8,512]{2,1,0:T(8,128)(2,1)S(1)}, bf16[28,8,512]{2,1,0:T(8,128)(2,1)S(1)}, u32[]{:S(2)}, u32[]{:S(2)}) collective-permute-start(bf16[28,8,512]{2,1,0:T(8,128)(2,1)S(1)} %get-tuple-element.206), channel_id=1, source_target_pairs={{8,0},{16,8},{24,16},{28,24},{20,28},{12,20},{4,12},{0,4},{9,1},{1... | collective-permute-start | bytes 688136 | tf_op jit(solution)/shard_map/ppermute | solution.py:323
  58.9 6.1 %collective-permute-start.8 = (bf16[14,8,512]{2,1,0:T(8,128)(2,1)S(1)}, bf16[14,8,512]{2,1,0:T(8,128)(2,1)S(1)}, u32[]{:S(2)}, u32[]{:S(2)}) collective-permute-start(bf16[14,8,512]{2,1,0:T(8,128)(2,1)S(1)} %get-tuple-element.205), channel_id=1, source_target_pairs={{8,0},{16,8},{24,16},{28,24},{20,28},{12,20},{4,12},{0,4},{9,1},{1... | collective-permute-start | bytes 344072 | tf_op jit(solution)/shard_map/ppermute | solution.py:323
  59.9 5.2 %collective-permute-start.7 = (bf16[15,8,512]{2,1,0:T(8,128)(2,1)S(1)}, bf16[15,8,512]{2,1,0:T(8,128)(2,1)S(1)}, u32[]{:S(2)}, u32[]{:S(2)}) collective-permute-start(bf16[15,8,512]{2,1,0:T(8,128)(2,1)S(1)} %get-tuple-element.204), channel_id=1, source_target_pairs={{0,8},{8,16},{16,24},{24,28},{28,20},{20,12},{12,4},{4,0},{1,9},{9... | collective-permute-start | bytes 368648 | tf_op jit(solution)/shard_map/ppermute | solution.py:323
  65.5 54.2 %collective-permute-start.34 = (f32[15,256,128]{2,1,0:T(8,128)S(1)}, f32[15,256,128]{2,1,0:T(8,128)S(1)}, u32[]{:S(2)}, u32[]{:S(2)}) collective-permute-start(f32[15,256,128]{2,1,0:T(8,128)S(1)} %get-tuple-element.292), channel_id=1, source_target_pairs={{0,2},{1,3},{2,0},{3,1},{4,6},{5,7},{6,4},{7,5},{8,10},{9,11},{10,... | collective-permute-start | bytes 5898248 | tf_op jit(solution)/shard_map/ppermute | solution.py:459
  66.1 8.5 %collective-permute-start.15 = (bf16[28,8,512]{2,1,0:T(8,128)(2,1)S(1)}, bf16[28,8,512]{2,1,0:T(8,128)(2,1)S(1)}, u32[]{:S(2)}, u32[]{:S(2)}) collective-permute-start(bf16[28,8,512]{2,1,0:T(8,128)(2,1)S(1)} %get-tuple-element.228), channel_id=1, source_target_pairs={{8,0},{16,8},{24,16},{28,24},{20,28},{12,20},{4,12},{0,4},{9,1},{1... | collective-permute-start | bytes 688136 | tf_op jit(solution)/shard_map/ppermute | solution.py:323
  67.4 8.5 %collective-permute-start.14 = (bf16[28,8,512]{2,1,0:T(8,128)(2,1)S(1)}, bf16[28,8,512]{2,1,0:T(8,128)(2,1)S(1)}, u32[]{:S(2)}, u32[]{:S(2)}) collective-permute-start(bf16[28,8,512]{2,1,0:T(8,128)(2,1)S(1)} %get-tuple-element.219), channel_id=1, source_target_pairs={{0,8},{8,16},{16,24},{24,28},{28,20},{20,12},{12,4},{4,0},{1,9},{9... | collective-permute-start | bytes 688136 | tf_op jit(solution)/shard_map/ppermute | solution.py:323
  68.1 11.4 %collective-permute-start.13 = (bf16[28,8,512]{2,1,0:T(8,128)(2,1)S(1)}, bf16[28,8,512]{2,1,0:T(8,128)(2,1)S(1)}, u32[]{:S(2)}, u32[]{:S(2)}) collective-permute-start(bf16[28,8,512]{2,1,0:T(8,128)(2,1)S(1)} %get-tuple-element.227), channel_id=1, source_target_pairs={{8,0},{16,8},{24,16},{28,24},{20,28},{12,20},{4,12},{0,4},{9,1},{1... | collective-permute-start | bytes 688136 | tf_op jit(solution)/shard_map/ppermute | solution.py:323
  69.4 11.4 %collective-permute-start.12 = (bf16[28,8,512]{2,1,0:T(8,128)(2,1)S(1)}, bf16[28,8,512]{2,1,0:T(8,128)(2,1)S(1)}, u32[]{:S(2)}, u32[]{:S(2)}) collective-permute-start(bf16[28,8,512]{2,1,0:T(8,128)(2,1)S(1)} %get-tuple-element.226), channel_id=1, source_target_pairs={{0,8},{8,16},{16,24},{24,28},{28,20},{20,12},{12,4},{4,0},{1,9},{9... | collective-permute-start | bytes 688136 | tf_op jit(solution)/shard_map/ppermute | solution.py:323
  76.5 9.8 %collective-permute-start.17 = (bf16[28,8,512]{2,1,0:T(8,128)(2,1)S(1)}, bf16[28,8,512]{2,1,0:T(8,128)(2,1)S(1)}, u32[]{:S(2)}, u32[]{:S(2)}) collective-permute-start(bf16[28,8,512]{2,1,0:T(8,128)(2,1)S(1)} %get-tuple-element.249), channel_id=1, source_target_pairs={{8,0},{16,8},{24,16},{28,24},{20,28},{12,20},{4,12},{0,4},{9,1},{1... | collective-permute-start | bytes 688136 | tf_op jit(solution)/shard_map/ppermute | solution.py:323
  78.0 8.4 %collective-permute-start.16 = (bf16[28,8,512]{2,1,0:T(8,128)(2,1)S(1)}, bf16[28,8,512]{2,1,0:T(8,128)(2,1)S(1)}, u32[]{:S(2)}, u32[]{:S(2)}) collective-permute-start(bf16[28,8,512]{2,1,0:T(8,128)(2,1)S(1)} %get-tuple-element.238), channel_id=1, source_target_pairs={{0,8},{8,16},{16,24},{24,28},{28,20},{20,12},{12,4},{4,0},{1,9},{9... | collective-permute-start | bytes 688136 | tf_op jit(solution)/shard_map/ppermute | solution.py:323
  81.5 8.6 %collective-permute-start.21 = (bf16[28,8,512]{2,1,0:T(8,128)(2,1)S(1)}, bf16[28,8,512]{2,1,0:T(8,128)(2,1)S(1)}, u32[]{:S(2)}, u32[]{:S(2)}) collective-permute-start(bf16[28,8,512]{2,1,0:T(8,128)(2,1)S(1)} %get-tuple-element.256), channel_id=1, source_target_pairs={{8,0},{16,8},{24,16},{28,24},{20,28},{12,20},{4,12},{0,4},{9,1},{1... | collective-permute-start | bytes 688136 | tf_op jit(solution)/shard_map/ppermute | solution.py:323
  82.9 7.8 %collective-permute-start.20 = (bf16[28,8,512]{2,1,0:T(8,128)(2,1)S(1)}, bf16[28,8,512]{2,1,0:T(8,128)(2,1)S(1)}, u32[]{:S(2)}, u32[]{:S(2)}) collective-permute-start(bf16[28,8,512]{2,1,0:T(8,128)(2,1)S(1)} %get-tuple-element.245), channel_id=1, source_target_pairs={{0,8},{8,16},{16,24},{24,28},{28,20},{20,12},{12,4},{4,0},{1,9},{9... | collective-permute-start | bytes 688136 | tf_op jit(solution)/shard_map/ppermute | solution.py:323
  86.9 7.9 %collective-permute-start.19 = (bf16[28,8,512]{2,1,0:T(8,128)(2,1)S(1)}, bf16[28,8,512]{2,1,0:T(8,128)(2,1)S(1)}, u32[]{:S(2)}, u32[]{:S(2)}) collective-permute-start(bf16[28,8,512]{2,1,0:T(8,128)(2,1)S(1)} %last_hop.2.refs_0_), channel_id=1, source_target_pairs={{8,0},{16,8},{24,16},{28,24},{20,28},{12,20},{4,12},{0,4},{9,1},{1... | collective-permute-start | bytes 688136 | tf_op jit(solution)/shard_map/ppermute | solution.py:323
  88.3 8.5 %collective-permute-start.18 = (bf16[28,8,512]{2,1,0:T(8,128)(2,1)S(1)}, bf16[28,8,512]{2,1,0:T(8,128)(2,1)S(1)}, u32[]{:S(2)}, u32[]{:S(2)}) collective-permute-start(bf16[28,8,512]{2,1,0:T(8,128)(2,1)S(1)} %last_hop.2.refs_0_), channel_id=1, source_target_pairs={{0,8},{8,16},{16,24},{24,28},{28,20},{20,12},{12,4},{4,0},{1,9},{9... | collective-permute-start | bytes 688136 | tf_op jit(solution)/shard_map/ppermute | solution.py:323
  91.3 6.6 %collective-permute-start.25 = (bf16[28,8,512]{2,1,0:T(8,128)(2,1)S(1)}, bf16[28,8,512]{2,1,0:T(8,128)(2,1)S(1)}, u32[]{:S(2)}, u32[]{:S(2)}) collective-permute-start(bf16[28,8,512]{2,1,0:T(8,128)(2,1)S(1)} %get-tuple-element.266), channel_id=1, source_target_pairs={{8,0},{16,8},{24,16},{28,24},{20,28},{12,20},{4,12},{0,4},{9,1},{1... | collective-permute-start | bytes 688136 | tf_op jit(solution)/shard_map/ppermute | solution.py:323
  92.7 7.6 %collective-permute-start.24 = (bf16[28,8,512]{2,1,0:T(8,128)(2,1)S(1)}, bf16[28,8,512]{2,1,0:T(8,128)(2,1)S(1)}, u32[]{:S(2)}, u32[]{:S(2)}) collective-permute-start(bf16[28,8,512]{2,1,0:T(8,128)(2,1)S(1)} %get-tuple-element.263), channel_id=1, source_target_pairs={{0,8},{8,16},{16,24},{24,28},{28,20},{20,12},{12,4},{4,0},{1,9},{9... | collective-permute-start | bytes 688136 | tf_op jit(solution)/shard_map/ppermute | solution.py:323
  96.9 10.9 %collective-permute-start.22 = (bf16[28,8,512]{2,1,0:T(8,128)(2,1)S(1)}, bf16[28,8,512]{2,1,0:T(8,128)(2,1)S(1)}, u32[]{:S(2)}, u32[]{:S(2)}) collective-permute-start(bf16[28,8,512]{2,1,0:T(8,128)(2,1)S(1)} %collective-permute-done.18.refs_1_), channel_id=1, source_target_pairs={{0,8},{8,16},{16,24},{24,28},{28,20},{20,12},{12,4},{4,0},{1,9},{9... | collective-permute-start | bytes 688136 | tf_op jit(solution)/shard_map/ppermute | solution.py:323
  100.3 7.4 %collective-permute-start.23 = (bf16[28,8,512]{2,1,0:T(8,128)(2,1)S(1)}, bf16[28,8,512]{2,1,0:T(8,128)(2,1)S(1)}, u32[]{:S(2)}, u32[]{:S(2)}) collective-permute-start(bf16[28,8,512]{2,1,0:T(8,128)(2,1)S(1)} %collective-permute-done.19.refs_2_), channel_id=1, source_target_pairs={{8,0},{16,8},{24,16},{28,24},{20,28},{12,20},{4,12},{0,4},{9,1},{1... | collective-permute-start | bytes 688136 | tf_op jit(solution)/shard_map/ppermute | solution.py:323
  102.4 9.3 %collective-permute-start.29 = (bf16[28,8,512]{2,1,0:T(8,128)(2,1)S(1)}, bf16[28,8,512]{2,1,0:T(8,128)(2,1)S(1)}, u32[]{:S(2)}, u32[]{:S(2)}) collective-permute-start(bf16[28,8,512]{2,1,0:T(8,128)(2,1)S(1)} %last_hop.3.refs_2_), channel_id=1, source_target_pairs={{8,0},{16,8},{24,16},{28,24},{20,28},{12,20},{4,12},{0,4},{9,1},{1... | collective-permute-start | bytes 688136 | tf_op jit(solution)/shard_map/ppermute | solution.py:323
  104.4 8.4 %collective-permute-start.28 = (bf16[28,8,512]{2,1,0:T(8,128)(2,1)S(1)}, bf16[28,8,512]{2,1,0:T(8,128)(2,1)S(1)}, u32[]{:S(2)}, u32[]{:S(2)}) collective-permute-start(bf16[28,8,512]{2,1,0:T(8,128)(2,1)S(1)} %last_hop.3.refs_2_), channel_id=1, source_target_pairs={{0,8},{8,16},{16,24},{24,28},{28,20},{20,12},{12,4},{4,0},{1,9},{9... | collective-permute-start | bytes 688136 | tf_op jit(solution)/shard_map/ppermute | solution.py:323
  107.7 9.3 %collective-permute-start.27 = (bf16[28,8,512]{2,1,0:T(8,128)(2,1)S(1)}, bf16[28,8,512]{2,1,0:T(8,128)(2,1)S(1)}, u32[]{:S(2)}, u32[]{:S(2)}) collective-permute-start(bf16[28,8,512]{2,1,0:T(8,128)(2,1)S(1)} %collective-permute-done.23.refs_1_), channel_id=1, source_target_pairs={{8,0},{16,8},{24,16},{28,24},{20,28},{12,20},{4,12},{0,4},{9,1},{1... | collective-permute-start | bytes 688136 | tf_op jit(solution)/shard_map/ppermute | solution.py:323
  109.5 7.6 %collective-permute-start.26 = (bf16[28,8,512]{2,1,0:T(8,128)(2,1)S(1)}, bf16[28,8,512]{2,1,0:T(8,128)(2,1)S(1)}, u32[]{:S(2)}, u32[]{:S(2)}) collective-permute-start(bf16[28,8,512]{2,1,0:T(8,128)(2,1)S(1)} %collective-permute-done.22.refs_0_), channel_id=1, source_target_pairs={{0,8},{8,16},{16,24},{24,28},{28,20},{20,12},{12,4},{4,0},{1,9},{9... | collective-permute-start | bytes 688136 | tf_op jit(solution)/shard_map/ppermute | solution.py:323
  112.8 6.4 %collective-permute-start.32 = (bf16[28,8,512]{2,1,0:T(8,128)(2,1)S(1)}, bf16[28,8,512]{2,1,0:T(8,128)(2,1)S(1)}, u32[]{:S(2)}, u32[]{:S(2)}) collective-permute-start(bf16[28,8,512]{2,1,0:T(8,128)(2,1)S(1)} %collective-permute-done.28.refs_3_), channel_id=1, source_target_pairs={{0,8},{8,16},{16,24},{24,28},{28,20},{20,12},{12,4},{4,0},{1,9},{9... | collective-permute-start | bytes 688136 | tf_op jit(solution)/shard_map/ppermute | solution.py:323
  113.7 6.0 %collective-permute-start.33 = (bf16[28,8,512]{2,1,0:T(8,128)(2,1)S(1)}, bf16[28,8,512]{2,1,0:T(8,128)(2,1)S(1)}, u32[]{:S(2)}, u32[]{:S(2)}) collective-permute-start(bf16[28,8,512]{2,1,0:T(8,128)(2,1)S(1)} %collective-permute-done.29.refs_4_), channel_id=1, source_target_pairs={{8,0},{16,8},{24,16},{28,24},{20,28},{12,20},{4,12},{0,4},{9,1},{1... | collective-permute-start | bytes 688136 | tf_op jit(solution)/shard_map/ppermute | solution.py:323
  117.1 4.8 %collective-permute-start.30 = (bf16[14,8,512]{2,1,0:T(8,128)(2,1)S(1)}, bf16[14,8,512]{2,1,0:T(8,128)(2,1)S(1)}, u32[]{:S(2)}, u32[]{:S(2)}) collective-permute-start(bf16[14,8,512]{2,1,0:T(8,128)(2,1)S(1)} %slice.12), channel_id=1, source_target_pairs={{0,8},{8,16},{16,24},{24,28},{28,20},{20,12},{12,4},{4,0},{1,9},{9... | collective-permute-start | bytes 344072 | tf_op jit(solution)/shard_map/ppermute | solution.py:323
  118.1 4.8 %collective-permute-start.31 = (bf16[14,8,512]{2,1,0:T(8,128)(2,1)S(1)}, bf16[14,8,512]{2,1,0:T(8,128)(2,1)S(1)}, u32[]{:S(2)}, u32[]{:S(2)}) collective-permute-start(bf16[14,8,512]{2,1,0:T(8,128)(2,1)S(1)} %slice.13), channel_id=1, source_target_pairs={{8,0},{16,8},{24,16},{28,24},{20,28},{12,20},{4,12},{0,4},{9,1},{1... | collective-permute-start | bytes 344072 | tf_op jit(solution)/shard_map/ppermute | solution.py:323
  122.9 13.2 %collective-permute-start.35 = (f32[18,256,128]{2,1,0:T(8,128)S(1)}, f32[18,256,128]{2,1,0:T(8,128)S(1)}, u32[]{:S(2)}, u32[]{:S(2)}) collective-permute-start(f32[18,256,128]{2,1,0:T(8,128)S(1)} %input_terms.6), channel_id=1, source_target_pairs={{0,1},{1,0},{2,3},{3,2},{4,5},{5,4},{6,7},{7,6},{8,9},{9,8},{10,11... | collective-permute-start | bytes 7077896 | tf_op jit(solution)/shard_map/ppermute | solution.py:491
  122.9 8.0 %collective-permute-start.38 = (bf16[28,8,512]{2,1,0:T(8,128)(2,1)S(1)}, bf16[28,8,512]{2,1,0:T(8,128)(2,1)S(1)}, u32[]{:S(2)}, u32[]{:S(2)}) collective-permute-start(bf16[28,8,512]{2,1,0:T(8,128)(2,1)S(1)} %collective-permute-done.33.refs_3_), channel_id=1, source_target_pairs={{8,0},{16,8},{24,16},{28,24},{20,28},{12,20},{4,12},{0,4},{9,1},{1... | collective-permute-start | bytes 688136 | tf_op jit(solution)/shard_map/ppermute | solution.py:323
  124.0 7.7 %collective-permute-start.37 = (bf16[28,8,512]{2,1,0:T(8,128)(2,1)S(1)}, bf16[28,8,512]{2,1,0:T(8,128)(2,1)S(1)}, u32[]{:S(2)}, u32[]{:S(2)}) collective-permute-start(bf16[28,8,512]{2,1,0:T(8,128)(2,1)S(1)} %collective-permute-done.32.refs_2_), channel_id=1, source_target_pairs={{0,8},{8,16},{16,24},{24,28},{28,20},{20,12},{12,4},{4,0},{1,9},{9... | collective-permute-start | bytes 688136 | tf_op jit(solution)/shard_map/ppermute | solution.py:323
  124.9 11.0 %collective-permute-start.36 = (f32[3,256,128]{2,1,0:T(8,128)S(1)}, f32[3,256,128]{2,1,0:T(8,128)S(1)}, u32[]{:S(2)}, u32[]{:S(2)}) collective-permute-start(f32[3,256,128]{2,1,0:T(8,128)S(1)} %get-tuple-element.303), channel_id=1, source_target_pairs={{0,2},{1,3},{2,0},{3,1},{4,6},{5,7},{6,4},{7,5},{8,10},{9,11},{10,... | collective-permute-start | bytes 1179656 | tf_op jit(solution)/shard_map/ppermute | solution.py:488
  131.8 5.9 %collective-permute-start.40 = (bf16[14,8,512]{2,1,0:T(8,128)(2,1)S(1)}, bf16[14,8,512]{2,1,0:T(8,128)(2,1)S(1)}, u32[]{:S(2)}, u32[]{:S(2)}) collective-permute-start(bf16[14,8,512]{2,1,0:T(8,128)(2,1)S(1)} %slice.15), channel_id=1, source_target_pairs={{8,0},{16,8},{24,16},{28,24},{20,28},{12,20},{4,12},{0,4},{9,1},{1... | collective-permute-start | bytes 344072 | tf_op jit(solution)/shard_map/ppermute | solution.py:323
  133.0 4.8 %collective-permute-start.39 = (bf16[14,8,512]{2,1,0:T(8,128)(2,1)S(1)}, bf16[14,8,512]{2,1,0:T(8,128)(2,1)S(1)}, u32[]{:S(2)}, u32[]{:S(2)}) collective-permute-start(bf16[14,8,512]{2,1,0:T(8,128)(2,1)S(1)} %slice.14), channel_id=1, source_target_pairs={{0,8},{8,16},{16,24},{24,28},{28,20},{20,12},{12,4},{4,0},{1,9},{9... | collective-permute-start | bytes 344072 | tf_op jit(solution)/shard_map/ppermute | solution.py:323
where the time goes:
time: 140 us
  Pallas kernels  44.4 us (32%)
  starting transfers between devices  43.4 us (31%)
  waiting for transfers between devices  41.8 us (30%)
  local copies, waits for them, and re-layouts  6.91 us (5%)
  other arithmetic  1.99 us (1%)
    pallas_call x19, Pallas kernels, direct(): pl.pallas_call(kernel, in_specs=([] if table is None else [smem]) + [vmem...  32.6 us
    ppermute x16, starting transfers between devices, send(): lax.ppermute(down, 'lon', self.behind)  23.4 us
    ppermute x1, waiting for transfers between devices, local(): lax.ppermute(heads, 'lon', [((i + 1) % count, i) for i in range(count)])  16.3 us
    ppermute x16, waiting for transfers between devices, send(): lax.ppermute(down, 'lon', self.behind)  14.8 us
    ppermute x16, waiting for transfers between devices, send(): lax.ppermute(up, 'lon', self.ahead)  10.5 us
    ppermute x16, starting transfers between devices, send(): lax.ppermute(up, 'lon', self.ahead)  10.1 us
    pallas_call x5, Pallas kernels, unfold(): pl.pallas_call(functools.partial(unfold_kernel, norm, places), in_specs=[...  9.48 us
    optimization_barrier x1, local copies, waits for them, and re-layouts, gate(): return lax.optimization_barrier(values + self.last)[:len(values)]  5.87 us
  transfers between devices with their start and end apart: 41, of which 22 were waited for; matrix products, arithmetic and copies ran while one was open for 6% of the time, Pallas kernels for 30%

commit v1 on v0

--- a/solution.py
+++ b/solution.py
@@ -452,17 +452,19 @@
     away = lax.ppermute(order.gate(away)[0], "ch", to_core)
     far = Chain(ring, order, 1, *features_with(flat_far))
     across = list(terms_of(1, most, away))
+    far.arrive()
+    far.hop()
     near.arrive()
     near.hop()
-    far.arrive()
-    far.hop()
     across[0] = lax.ppermute(order.gate(across[0])[0], "ch", to_x)
     (beside,) = terms_of(2, whole)
     for _ in range(half - 4):
+        far.arrive()
+        far.hop()
         near.arrive()
         near.hop()
-        far.arrive()
-        far.hop()
+    far.arrive()
+    far.hop()
     near.arrive()
     near.hop()
     far.arrive()
@@ -470,8 +472,6 @@
     (mine,) = terms_of(3, whole)
     near.arrive()
     near.last()
-    far.arrive()
-    far.hop()
     near.move()
     far.arrive()
     far.last()

time: 140 us -> 142 us (1.014)
    ppermute x16, starting transfers between devices: 23.4 us -> 27.6 us  [send(): lax.ppermute(down, 'lon', self.behind)]
    ppermute x16, starting transfers between devices: 10.1 us -> 6.06 us  [send(): lax.ppermute(up, 'lon', self.ahead)]
    ppermute x16, waiting for transfers between devices: 10.5 us -> 12.8 us  [send(): lax.ppermute(up, 'lon', self.ahead)]
  transfers between devices with their start and end apart: 41 -> 41, of which waited for: 22 -> 20; matrix products, arithmetic and copies ran while one was open for 6% -> 6% of each run, Pallas kernels for 30% -> 30%
where the time goes in v1:
time: 142 us; the launch traced here: 141 us
  Pallas kernels  44.4 us (31%)
  starting transfers between devices  43.5 us (31%)
  waiting for transfers between devices  43.2 us (30%)
  local copies, waits for them, and re-layouts  6.91 us (5%)
  other arithmetic  1.99 us (1%)
    pallas_call x19, Pallas kernels, direct(): pl.pallas_call(kernel, in_specs=([] if table is None else [smem]) + [vmem...  32.6 us
    ppermute x16, starting transfers between devices, send(): lax.ppermute(down, 'lon', self.behind)  27.6 us
    ppermute x1, waiting for transfers between devices, local(): lax.ppermute(heads, 'lon', [((i + 1) % count, i) for i in range(count)])  16.3 us
    ppermute x16, waiting for transfers between devices, send(): lax.ppermute(down, 'lon', self.behind)  14.1 us
    ppermute x16, waiting for transfers between devices, send(): lax.ppermute(up, 'lon', self.ahead)  12.8 us
    pallas_call x5, Pallas kernels, unfold(): pl.pallas_call(functools.partial(unfold_kernel, norm, places), in_specs=[...  9.48 us
    ppermute x16, starting transfers between devices, send(): lax.ppermute(up, 'lon', self.ahead)  6.06 us
    optimization_barrier x1, local copies, waits for them, and re-layouts, gate(): return lax.optimization_barrier(values + self.last)[:len(values)]  5.87 us
  transfers between devices with their start and end apart: 41, of which 20 were waited for; matrix products, arithmetic and copies ran while one was open for 6% of the time, Pallas kernels for 30%

profile of v1, /device:TPU:0, one launch (start us, length us, event | category | flops | bytes accessed | tf_op | source)
XLA Modules:
  0.0 141.2 jit_solution(16834501555154039438)
XLA Ops:
  1.1 2.6 %collective-permute-start.2 = (bf16[18,256,128]{2,1,0:T(8,128)(2,1)}, bf16[18,256,128]{2,1,0:T(8,128)(2,1)S(1)}, u32[]{:S(2)}, u32[]{:S(2)}) collective-permute-start(bf16[18,256,128]{2,1,0:T(8,128)(2,1)} %bitcast.25), channel_id=1, source_target_pairs={{0,2},{1,3},{2,0},{3,1},{4,6},{5,7},{6,4},{7,5},{8,10},{9,11},{10,... | collective-permute-start | bytes 3538952 | tf_op jit(solution)/shard_map/ppermute | solution.py:413
  3.7 2.3 %edges.1 = (bf16[36,64,128]{2,1,0:T(8,128)(2,1)}, bf16[36,64,128]{2,1,0:T(8,128)(2,1)}) custom-call(bf16[3,18,64,128]{3,2,1,0:T(8,128)(2,1)} %bitcast.27), custom_call_target="tpu_custom_call" | custom-call | flops 300000000 | tf_op jit(solution)/shard_map/edges/pallas_call | solution.py:84
  6.0 4.6 %collective-permute-start.1 = (bf16[36,64,128]{2,1,0:T(8,128)(2,1)}, bf16[36,64,128]{2,1,0:T(8,128)(2,1)}, u32[]{:S(2)}, u32[]{:S(2)}) collective-permute-start(bf16[36,64,128]{2,1,0:T(8,128)(2,1)} %get-tuple-element.165), channel_id=1, source_target_pairs={{4,0},{8,4},{12,8},{16,12},{20,16},{24,20},{28,24},{0,28},{5,1},{9... | collective-permute-start | bytes 1769480 | tf_op jit(solution)/shard_map/ppermute | solution.py:409
  11.0 5.9 %copy.10 = bf16[1728,1024]{0,1:T(8,128)(2,1)} copy(bf16[1728,1024]{1,0:T(8,128)(2,1)} %bitcast.30) | data formatting | bytes 7077888 | tf_op jit(solution)/shard_map/optimization_barrier | solution.py:300
  16.8 1.2 flatten.2.feat_ref
  18.0 16.3 %collective-permute-done.1.right_ref = bf16[36,64,128]{2,1,0:T(8,128)(2,1)} collective-permute-done((bf16[36,64,128]{2,1,0:T(8,128)(2,1)}, bf16[36,64,128]{2,1,0:T(8,128)(2,1)}, u32[]{:S(2)}, u32[]{:S(2)}) %collective-permute-start.1) | collective-permute-done | bytes 589856 | tf_op jit(solution)/shard_map/ppermute | solution.py:409
  34.4 2.5 %spread.1.grid_ref = bf16[1728,2304]{1,0:T(8,128)(2,1)S(1)} custom-call(bf16[3,18,64,128]{3,2,1,0:T(8,128)(2,1)S(1)} %bitcast.28, bf16[36,64,128]{2,1,0:T(8,128)(2,1)} %collective-permute-done.left_ref, bf16[36,64,128]{2,1,0:T(8,128)(2,1)} %collective-permute-done.1.right_ref), custom_call_target="tpu_custom_call" | custom-call | flops 600000000 | tf_op jit(solution)/shard_map/spread/pallas_call | solution.py:61
  36.9 5.6 %kernel_terms.2 = (f32[8,27,8,512]{3,2,1,0:T(8,128)S(1)}, f32[1,8,512]{2,1,0:T(8,128)S(1)}) custom-call(s32[30]{0:T(128)S(1)} %concatenate.12.place_ref.table_ref, bf16[1728,2304]{1,0:T(8,128)(2,1)S(1)} %spread.1.grid_ref, bf16[2304,512]{1,0:T(8,128)(2,1)S(1)} %flatten.2.feat_ref), custom_call_target="tpu_custom_call" | custom-call | flops 1800000000 | tf_op jit(solution)/shard_map/kernel_terms/pallas_call | solution.py:61
  42.6 2.5 %collective-permute-start.6 = (bf16[14,8,512]{2,1,0:T(8,128)(2,1)S(1)}, bf16[14,8,512]{2,1,0:T(8,128)(2,1)S(1)}, u32[]{:S(2)}, u32[]{:S(2)}) collective-permute-start(bf16[14,8,512]{2,1,0:T(8,128)(2,1)S(1)} %get-tuple-element.186), channel_id=1, source_target_pairs={{8,0},{16,8},{24,16},{28,24},{20,28},{12,20},{4,12},{0,4},{9,1},{1... | collective-permute-start | bytes 344072 | tf_op jit(solution)/shard_map/ppermute | solution.py:323
  45.1 1.2 flatten.3.feat_ref
  46.4 0.8 copy-done
  47.2 2.8 %input_terms.4 = f32[18,256,128]{2,1,0:T(8,128)S(1)} custom-call(s32[30]{0:T(128)S(1)} %concatenate.12.place_ref.table_ref, bf16[1024,1728]{1,0:T(8,128)(2,1)S(1)} %bitcast.20, bf16[1728,2304]{1,0:T(8,128)(2,1)S(1)} %spread.1.grid_ref), custom_call_target="tpu_custom_call" | custom-call | flops 1050000000 | tf_op jit(solution)/shard_map/input_terms/pallas_call | solution.py:61
  51.4 1.7 %collective-permute-start.13 = (bf16[28,8,512]{2,1,0:T(8,128)(2,1)S(1)}, bf16[28,8,512]{2,1,0:T(8,128)(2,1)S(1)}, u32[]{:S(2)}, u32[]{:S(2)}) collective-permute-start(bf16[28,8,512]{2,1,0:T(8,128)(2,1)S(1)} %get-tuple-element.220), channel_id=1, source_target_pairs={{8,0},{16,8},{24,16},{28,24},{20,28},{12,20},{4,12},{0,4},{9,1},{1... | collective-permute-start | bytes 688136 | tf_op jit(solution)/shard_map/ppermute | solution.py:323
  53.2 5.6 %kernel_terms.3 = (f32[8,27,8,512]{3,2,1,0:T(8,128)S(1)}, f32[1,8,512]{2,1,0:T(8,128)S(1)}) custom-call(s32[30]{0:T(128)S(1)} %concatenate.12.place_ref.table_ref, bf16[1728,2304]{1,0:T(8,128)(2,1)S(1)} %spread.1.grid_ref, bf16[2304,512]{1,0:T(8,128)(2,1)S(1)} %flatten.3.feat_ref), custom_call_target="tpu_custom_call" | custom-call | flops 1800000000 | tf_op jit(solution)/shard_map/kernel_terms/pallas_call | solution.py:61
  59.3 1.7 %collective-permute-start.8 = (bf16[14,8,512]{2,1,0:T(8,128)(2,1)S(1)}, bf16[14,8,512]{2,1,0:T(8,128)(2,1)S(1)}, u32[]{:S(2)}, u32[]{:S(2)}) collective-permute-start(bf16[14,8,512]{2,1,0:T(8,128)(2,1)S(1)} %get-tuple-element.205), channel_id=1, source_target_pairs={{8,0},{16,8},{24,16},{28,24},{20,28},{12,20},{4,12},{0,4},{9,1},{1... | collective-permute-start | bytes 344072 | tf_op jit(solution)/shard_map/ppermute | solution.py:323
  61.0 3.4 %input_terms.5 = (f32[15,256,128]{2,1,0:T(8,128)S(1)}, f32[3,256,128]{2,1,0:T(8,128)S(1)}) custom-call(s32[30]{0:T(128)S(1)} %concatenate.12.place_ref.table_ref, bf16[1024,1728]{1,0:T(8,128)(2,1)S(1)} %bitcast.21, bf16[1728,2304]{1,0:T(8,128)(2,1)S(1)} %spread.1.grid_ref, f32[18,256,128]{2,1,0:T(8,128)S(1)} %collective-permute-done.9.refs_0_), custom_call_target="tpu_custom_call" | custom-call | flops 1050000000 | tf_op jit(solution)/shard_map/input_terms/pallas_call | solution.py:61
  64.9 0.6 next_hop.8
  66.1 1.4 collective-permute-start.11
  67.5 0.6 collective-permute-start.10
  68.1 0.8 collective-permute-start.16
  68.9 1.3 collective-permute-start.17
  70.2 2.8 %input_terms.6 = f32[18,256,128]{2,1,0:T(8,128)S(1)} custom-call(s32[30]{0:T(128)S(1)} %concatenate.12.place_ref.table_ref, bf16[1024,1728]{1,0:T(8,128)(2,1)S(1)} %bitcast.22, bf16[1728,2304]{1,0:T(8,128)(2,1)S(1)} %spread.1.grid_ref), custom_call_target="tpu_custom_call" | custom-call | flops 1050000000 | tf_op jit(solution)/shard_map/input_terms/pallas_call | solution.py:61
  73.0 1.6 %collective-permute-done.11.down_ref = bf16[28,8,512]{2,1,0:T(8,128)(2,1)S(1)} collective-permute-done((bf16[28,8,512]{2,1,0:T(8,128)(2,1)S(1)}, bf16[28,8,512]{2,1,0:T(8,128)(2,1)S(1)}, u32[]{:S(2)}, u32[]{:S(2)}) %collective-permute-start.11) | collective-permute-done | bytes 229408 | tf_op jit(solution)/shard_map/ppermute | solution.py:323
  74.7 1.1 collective-permute-done.10.up_ref
  75.7 0.6 next_hop.9
  76.4 1.4 %collective-permute-start.15 = (bf16[28,8,512]{2,1,0:T(8,128)(2,1)S(1)}, bf16[28,8,512]{2,1,0:T(8,128)(2,1)S(1)}, u32[]{:S(2)}, u32[]{:S(2)}) collective-permute-start(bf16[28,8,512]{2,1,0:T(8,128)(2,1)S(1)} %get-tuple-element.238), channel_id=1, source_target_pairs={{8,0},{16,8},{24,16},{28,24},{20,28},{12,20},{4,12},{0,4},{9,1},{1... | collective-permute-start | bytes 688136 | tf_op jit(solution)/shard_map/ppermute | solution.py:323
  77.8 0.6 collective-permute-start.14
  78.4 1.1 collective-permute-done.17.down_ref
  79.6 1.1 collective-permute-done.16.up_ref
  80.7 0.6 next_hop.10
  81.3 1.4 %collective-permute-start.19 = (bf16[28,8,512]{2,1,0:T(8,128)(2,1)S(1)}, bf16[28,8,512]{2,1,0:T(8,128)(2,1)S(1)}, u32[]{:S(2)}, u32[]{:S(2)}) collective-permute-start(bf16[28,8,512]{2,1,0:T(8,128)(2,1)S(1)} %get-tuple-element.257), channel_id=1, source_target_pairs={{8,0},{16,8},{24,16},{28,24},{20,28},{12,20},{4,12},{0,4},{9,1},{1... | collective-permute-start | bytes 688136 | tf_op jit(solution)/shard_map/ppermute | solution.py:323
  82.7 0.6 collective-permute-start.18
  83.3 1.6 %collective-permute-done.15.down_ref = bf16[28,8,512]{2,1,0:T(8,128)(2,1)S(1)} collective-permute-done((bf16[28,8,512]{2,1,0:T(8,128)(2,1)S(1)}, bf16[28,8,512]{2,1,0:T(8,128)(2,1)S(1)}, u32[]{:S(2)}, u32[]{:S(2)}) %collective-permute-start.15) | collective-permute-done | bytes 229408 | tf_op jit(solution)/shard_map/ppermute | solution.py:323
  84.9 0.6 collective-permute-done.14.up_ref
  85.6 0.6 next_hop.11
  86.2 2.8 %input_terms.7 = f32[18,256,128]{2,1,0:T(8,128)S(1)} custom-call(s32[30]{0:T(128)S(1)} %concatenate.12.place_ref.table_ref, bf16[1024,1728]{1,0:T(8,128)(2,1)S(1)} %bitcast.23, bf16[1728,2304]{1,0:T(8,128)(2,1)S(1)} %spread.1.grid_ref), custom_call_target="tpu_custom_call" | custom-call | flops 1050000000 | tf_op jit(solution)/shard_map/input_terms/pallas_call | solution.py:61
  89.6 1.6 %collective-permute-start.21 = (bf16[28,8,512]{2,1,0:T(8,128)(2,1)S(1)}, bf16[28,8,512]{2,1,0:T(8,128)(2,1)S(1)}, u32[]{:S(2)}, u32[]{:S(2)}) collective-permute-start(bf16[28,8,512]{2,1,0:T(8,128)(2,1)S(1)} %last_hop.2.refs_0_), channel_id=1, source_target_pairs={{8,0},{16,8},{24,16},{28,24},{20,28},{12,20},{4,12},{0,4},{9,1},{1... | collective-permute-start | bytes 688136 | tf_op jit(solution)/shard_map/ppermute | solution.py:323
  91.6 1.6 %collective-permute-start.25 = (bf16[28,8,512]{2,1,0:T(8,128)(2,1)S(1)}, bf16[28,8,512]{2,1,0:T(8,128)(2,1)S(1)}, u32[]{:S(2)}, u32[]{:S(2)}) collective-permute-start(bf16[28,8,512]{2,1,0:T(8,128)(2,1)S(1)} %get-tuple-element.266), channel_id=1, source_target_pairs={{8,0},{16,8},{24,16},{28,24},{20,28},{12,20},{4,12},{0,4},{9,1},{1... | collective-permute-start | bytes 688136 | tf_op jit(solution)/shard_map/ppermute | solution.py:323
  93.7 3.0 %collective-permute-done.21.refs_2_ = bf16[28,8,512]{2,1,0:T(8,128)(2,1)S(1)} collective-permute-done((bf16[28,8,512]{2,1,0:T(8,128)(2,1)S(1)}, bf16[28,8,512]{2,1,0:T(8,128)(2,1)S(1)}, u32[]{:S(2)}, u32[]{:S(2)}) %collective-permute-start.21) | collective-permute-done | bytes 229408 | tf_op jit(solution)/shard_map/ppermute | solution.py:323
  96.7 1.7 %collective-permute-done.20.refs_1_ = bf16[28,8,512]{2,1,0:T(8,128)(2,1)S(1)} collective-permute-done((bf16[28,8,512]{2,1,0:T(8,128)(2,1)S(1)}, bf16[28,8,512]{2,1,0:T(8,128)(2,1)S(1)}, u32[]{:S(2)}, u32[]{:S(2)}) %collective-permute-start.20) | collective-permute-done | bytes 229408 | tf_op jit(solution)/shard_map/ppermute | solution.py:323
  98.4 2.2 %collective-permute-start.23 = (bf16[28,8,512]{2,1,0:T(8,128)(2,1)S(1)}, bf16[28,8,512]{2,1,0:T(8,128)(2,1)S(1)}, u32[]{:S(2)}, u32[]{:S(2)}) collective-permute-start(bf16[28,8,512]{2,1,0:T(8,128)(2,1)S(1)} %collective-permute-done.21.refs_2_), channel_id=1, source_target_pairs={{8,0},{16,8},{24,16},{28,24},{20,28},{12,20},{4,12},{0,4},{9,1},{1... | collective-permute-start | bytes 688136 | tf_op jit(solution)/shard_map/ppermute | solution.py:323
  100.6 1.0 collective-permute-done.25.down_ref
  101.6 1.7 %collective-permute-done.24.up_ref = bf16[28,8,512]{2,1,0:T(8,128)(2,1)S(1)} collective-permute-done((bf16[28,8,512]{2,1,0:T(8,128)(2,1)S(1)}, bf16[28,8,512]{2,1,0:T(8,128)(2,1)S(1)}, u32[]{:S(2)}, u32[]{:S(2)}) %collective-permute-start.24) | collective-permute-done | bytes 229408 | tf_op jit(solution)/shard_map/ppermute | solution.py:323
  103.8 2.3 %collective-permute-start.29 = (bf16[28,8,512]{2,1,0:T(8,128)(2,1)S(1)}, bf16[28,8,512]{2,1,0:T(8,128)(2,1)S(1)}, u32[]{:S(2)}, u32[]{:S(2)}) collective-permute-start(bf16[28,8,512]{2,1,0:T(8,128)(2,1)S(1)} %last_hop.3.refs_2_), channel_id=1, source_target_pairs={{8,0},{16,8},{24,16},{28,24},{20,28},{12,20},{4,12},{0,4},{9,1},{1... | collective-permute-start | bytes 688136 | tf_op jit(solution)/shard_map/ppermute | solution.py:323
  106.1 1.9 %unfold.5.refs_5_ = f32[27,64,1024]{2,1,0:T(8,128)} custom-call(s32[30]{0:T(128)S(1)} %concatenate.12.place_ref.table_ref, bf16[28,8,512]{2,1,0:T(8,128)(2,1)S(1)} %last_hop.2.refs_0_, bf16[28,8,512]{2,1,0:T(8,128)(2,1)S(1)} %collective-permute-done.20.refs_1_, bf16[28,8,512]{2,1,0:T(8,128)(2,1)S(1)} %collective-permute-done.21.refs_2_), custom_call_target="tpu_custom_call" | custom-call | flops 900000000 | tf_op jit(solution)/shard_map/unfold/pallas_call | solution.py:230
  107.9 1.2 collective-permute-done.22.refs_0_
  109.1 1.3 collective-permute-start.27
  110.4 0.7 collective-permute-start.26
  111.2 1.2 collective-permute-done.29.refs_4_
  112.4 2.2 %collective-permute-done.28.refs_3_ = bf16[28,8,512]{2,1,0:T(8,128)(2,1)S(1)} collective-permute-done((bf16[28,8,512]{2,1,0:T(8,128)(2,1)S(1)}, bf16[28,8,512]{2,1,0:T(8,128)(2,1)S(1)}, u32[]{:S(2)}, u32[]{:S(2)}) %collective-permute-start.28) | collective-permute-done | bytes 229408 | tf_op jit(solution)/shard_map/ppermute | solution.py:323
  114.6 2.0 %collective-permute-start.33 = (bf16[28,8,512]{2,1,0:T(8,128)(2,1)S(1)}, bf16[28,8,512]{2,1,0:T(8,128)(2,1)S(1)}, u32[]{:S(2)}, u32[]{:S(2)}) collective-permute-start(bf16[28,8,512]{2,1,0:T(8,128)(2,1)S(1)} %collective-permute-done.29.refs_4_), channel_id=1, source_target_pairs={{8,0},{16,8},{24,16},{28,24},{20,28},{12,20},{4,12},{0,4},{9,1},{1... | collective-permute-start | bytes 688136 | tf_op jit(solution)/shard_map/ppermute | solution.py:323
  116.6 2.2 %unfold.6.refs_4_ = f32[27,64,1024]{2,1,0:T(8,128)} custom-call(s32[30]{0:T(128)S(1)} %concatenate.12.place_ref.table_ref, bf16[28,8,512]{2,1,0:T(8,128)(2,1)S(1)} %collective-permute-done.22.refs_0_, bf16[28,8,512]{2,1,0:T(8,128)(2,1)S(1)} %collective-permute-done.23.refs_1_, ...), custom_call_target="tpu_custom_call", output_to_operand_aliasing={{}: (6, {})} | custom-call | flops 900000000 | tf_op jit(solution)/shard_map/unfold/pallas_call | solution.py:230
  119.0 2.0 %collective-permute-start.31 = (bf16[14,8,512]{2,1,0:T(8,128)(2,1)S(1)}, bf16[14,8,512]{2,1,0:T(8,128)(2,1)S(1)}, u32[]{:S(2)}, u32[]{:S(2)}) collective-permute-start(bf16[14,8,512]{2,1,0:T(8,128)(2,1)S(1)} %slice.13), channel_id=1, source_target_pairs={{8,0},{16,8},{24,16},{28,24},{20,28},{12,20},{4,12},{0,4},{9,1},{1... | collective-permute-start | bytes 344072 | tf_op jit(solution)/shard_map/ppermute | solution.py:323
  121.0 2.0 %unfold.7.refs_3_ = f32[27,64,1024]{2,1,0:T(8,128)} custom-call(s32[30]{0:T(128)S(1)} %concatenate.12.place_ref.table_ref, bf16[28,8,512]{2,1,0:T(8,128)(2,1)S(1)} %collective-permute-done.26.refs_0_, bf16[28,8,512]{2,1,0:T(8,128)(2,1)S(1)} %collective-permute-done.27.refs_1_, ...), custom_call_target="tpu_custom_call", output_to_operand_aliasing={{}: (5, {})} | custom-call | flops 900000000 | tf_op jit(solution)/shard_map/unfold/pallas_call | solution.py:230
  123.0 0.7 collective-permute-done.30
  123.8 2.0 %collective-permute-start.38 = (bf16[28,8,512]{2,1,0:T(8,128)(2,1)S(1)}, bf16[28,8,512]{2,1,0:T(8,128)(2,1)S(1)}, u32[]{:S(2)}, u32[]{:S(2)}) collective-permute-start(bf16[28,8,512]{2,1,0:T(8,128)(2,1)S(1)} %collective-permute-done.33.refs_3_), channel_id=1, source_target_pairs={{8,0},{16,8},{24,16},{28,24},{20,28},{12,20},{4,12},{0,4},{9,1},{1... | collective-permute-start | bytes 688136 | tf_op jit(solution)/shard_map/ppermute | solution.py:323
  125.8 1.5 %collective-permute-start.36 = (f32[3,256,128]{2,1,0:T(8,128)S(1)}, f32[3,256,128]{2,1,0:T(8,128)S(1)}, u32[]{:S(2)}, u32[]{:S(2)}) collective-permute-start(f32[3,256,128]{2,1,0:T(8,128)S(1)} %get-tuple-element.303), channel_id=1, source_target_pairs={{0,2},{1,3},{2,0},{3,1},{4,6},{5,7},{6,4},{7,5},{8,10},{9,11},{10,... | collective-permute-start | bytes 1179656 | tf_op jit(solution)/shard_map/ppermute | solution.py:488
  127.4 4.5 %collective-permute-done.38.refs_2_ = bf16[28,8,512]{2,1,0:T(8,128)(2,1)S(1)} collective-permute-done((bf16[28,8,512]{2,1,0:T(8,128)(2,1)S(1)}, bf16[28,8,512]{2,1,0:T(8,128)(2,1)S(1)}, u32[]{:S(2)}, u32[]{:S(2)}) %collective-permute-start.38) | collective-permute-done | bytes 229408 | tf_op jit(solution)/shard_map/ppermute | solution.py:323
  131.8 1.7 %collective-permute-done.37.refs_1_ = bf16[28,8,512]{2,1,0:T(8,128)(2,1)S(1)} collective-permute-done((bf16[28,8,512]{2,1,0:T(8,128)(2,1)S(1)}, bf16[28,8,512]{2,1,0:T(8,128)(2,1)S(1)}, u32[]{:S(2)}, u32[]{:S(2)}) %collective-permute-start.37) | collective-permute-done | bytes 229408 | tf_op jit(solution)/shard_map/ppermute | solution.py:323
  133.6 1.1 collective-permute-start.40
  134.7 0.9 collective-permute-start.39
  135.7 1.9 %unfold.8.refs_1_ = f32[27,64,1024]{2,1,0:T(8,128)} custom-call(s32[30]{0:T(128)S(1)} %concatenate.12.place_ref.table_ref, bf16[28,8,512]{2,1,0:T(8,128)(2,1)S(1)} %pad_maximum_fusion.1.refs_0_, bf16[28,8,512]{2,1,0:T(8,128)(2,1)S(1)} %collective-permute-done.37.refs_1_, ...), custom_call_target="tpu_custom_call", output_to_operand_aliasing={{}: (4, {})} | custom-call | flops 900000000 | tf_op jit(solution)/shard_map/unfold/pallas_call | solution.py:230
  137.7 1.6 %add_convert_fusion = bf16[18,256,128]{2,1,0:T(8,128)(2,1)} fusion(f32[18,256,128]{2,1,0:T(8,128)S(1)} %pad_maximum_fusion, f32[18,256,128]{2,1,0:T(8,128)S(1)} %input_terms.7, f32[18,256,128]{2,1,0:T(8,128)S(1)} %collective-permute-done.35), kind=kLoop, calls=%fused_computation.1 | loop fusion | flops 1769472 | bytes 8257536 | tf_op jit(solution)/shard_map/convert_element_type | solution.py:495
  139.5 1.5 %unfold.9 = f32[27,64,1024]{2,1,0:T(8,128)} custom-call(s32[30]{0:T(128)S(1)} %concatenate.12.place_ref.table_ref, bf16[28,8,512]{2,1,0:T(8,128)(2,1)S(1)} %pad_maximum_fusion.2.refs_0_, f32[27,64,1024]{2,1,0:T(8,128)} %unfold.8.refs_1_), custom_call_target="tpu_custom_call", output_to_operand_aliasing={{}: (2, {})} | custom-call | flops 900000000 | tf_op jit(solution)/shard_map/unfold/pallas_call | solution.py:230
  (64 shorter events, 6.5 us)
Async XLA Ops:
  0.6 16.2 %collective-permute-start.3 = (bf16[18,256,128]{2,1,0:T(8,128)(2,1)}, bf16[18,256,128]{2,1,0:T(8,128)(2,1)S(1)}, u32[]{:S(2)}, u32[]{:S(2)}) collective-permute-start(bf16[18,256,128]{2,1,0:T(8,128)(2,1)} %bitcast.24), channel_id=1, source_target_pairs={{0,1},{1,0},{2,3},{3,2},{4,5},{5,4},{6,7},{7,6},{8,9},{9,8},{10,11... | collective-permute-start | bytes 3538952 | tf_op jit(solution)/shard_map/ppermute | solution.py:414
  1.1 33.2 %collective-permute-start.2 = (bf16[18,256,128]{2,1,0:T(8,128)(2,1)}, bf16[18,256,128]{2,1,0:T(8,128)(2,1)S(1)}, u32[]{:S(2)}, u32[]{:S(2)}) collective-permute-start(bf16[18,256,128]{2,1,0:T(8,128)(2,1)} %bitcast.25), channel_id=1, source_target_pairs={{0,2},{1,3},{2,0},{3,1},{4,6},{5,7},{6,4},{7,5},{8,10},{9,11},{10,... | collective-permute-start | bytes 3538952 | tf_op jit(solution)/shard_map/ppermute | solution.py:413
  6.0 28.4 %collective-permute-start.1 = (bf16[36,64,128]{2,1,0:T(8,128)(2,1)}, bf16[36,64,128]{2,1,0:T(8,128)(2,1)}, u32[]{:S(2)}, u32[]{:S(2)}) collective-permute-start(bf16[36,64,128]{2,1,0:T(8,128)(2,1)} %get-tuple-element.165), channel_id=1, source_target_pairs={{4,0},{8,4},{12,8},{16,12},{20,16},{24,20},{28,24},{0,28},{5,1},{9... | collective-permute-start | bytes 1769480 | tf_op jit(solution)/shard_map/ppermute | solution.py:409
  10.6 23.8 %collective-permute-start = (bf16[36,64,128]{2,1,0:T(8,128)(2,1)}, bf16[36,64,128]{2,1,0:T(8,128)(2,1)}, u32[]{:S(2)}, u32[]{:S(2)}) collective-permute-start(bf16[36,64,128]{2,1,0:T(8,128)(2,1)} %get-tuple-element.161), channel_id=1, source_target_pairs={{0,4},{4,8},{8,12},{12,16},{16,20},{20,24},{24,28},{28,0},{1,5},{5... | collective-permute-start | bytes 1769480 | tf_op jit(solution)/shard_map/ppermute | solution.py:408
  10.9 5.9 %copy-start.1 = (bf16[256,1,18,128]{3,0,2,1:T(8,128)(2,1)S(1)}, bf16[256,1,18,128]{3,0,2,1:T(8,128)(2,1)}, u32[]{:S(2)}) copy-start(bf16[256,1,18,128]{3,0,2,1:T(8,128)(2,1)} %param.3) | copy-start | bytes 3538948
  16.8 17.6 %copy-start.2 = (bf16[3,64,1,18,128]{4,1,3,2,0:T(8,128)(2,1)S(1)}, bf16[3,64,1,18,128]{4,1,3,2,0:T(8,128)(2,1)}, u32[]{:S(2)}) copy-start(bf16[3,64,1,18,128]{4,1,3,2,0:T(8,128)(2,1)} %param.4) | copy-start | bytes 2654212
  34.4 10.8 %collective-permute-start.4 = (bf16[18,256,128]{2,1,0:T(8,128)(2,1)S(1)}, bf16[18,256,128]{2,1,0:T(8,128)(2,1)S(1)}, u32[]{:S(2)}, u32[]{:S(2)}) collective-permute-start(bf16[18,256,128]{2,1,0:T(8,128)(2,1)S(1)} %collective-permute-done.2.first_ref), channel_id=1, source_target_pairs={{0,1},{1,0},{2,3},{3,2},{4,5},{5,4},{6,7},{7,6},{8,9},{9,8},{10,11... | collective-permute-start | bytes 3538952 | tf_op jit(solution)/shard_map/ppermute | solution.py:425
  42.6 7.4 %collective-permute-start.6 = (bf16[14,8,512]{2,1,0:T(8,128)(2,1)S(1)}, bf16[14,8,512]{2,1,0:T(8,128)(2,1)S(1)}, u32[]{:S(2)}, u32[]{:S(2)}) collective-permute-start(bf16[14,8,512]{2,1,0:T(8,128)(2,1)S(1)} %get-tuple-element.186), channel_id=1, source_target_pairs={{8,0},{16,8},{24,16},{28,24},{20,28},{12,20},{4,12},{0,4},{9,1},{1... | collective-permute-start | bytes 344072 | tf_op jit(solution)/shard_map/ppermute | solution.py:323
  45.1 2.0 %copy-start = (bf16[1728,1024]{0,1:T(8,128)(2,1)S(1)}, bf16[1728,1024]{0,1:T(8,128)(2,1)}, u32[]{:S(2)}) copy-start(bf16[1728,1024]{0,1:T(8,128)(2,1)} %copy.10) | copy-start | bytes 10616836
  45.1 5.4 %collective-permute-start.5 = (bf16[15,8,512]{2,1,0:T(8,128)(2,1)S(1)}, bf16[15,8,512]{2,1,0:T(8,128)(2,1)S(1)}, u32[]{:S(2)}, u32[]{:S(2)}) collective-permute-start(bf16[15,8,512]{2,1,0:T(8,128)(2,1)S(1)} %get-tuple-element.182), channel_id=1, source_target_pairs={{0,8},{8,16},{16,24},{24,28},{28,20},{20,12},{12,4},{4,0},{1,9},{9... | collective-permute-start | bytes 368648 | tf_op jit(solution)/shard_map/ppermute | solution.py:323
  51.0 10.0 %collective-permute-start.9 = (f32[18,256,128]{2,1,0:T(8,128)S(1)}, f32[18,256,128]{2,1,0:T(8,128)S(1)}, u32[]{:S(2)}, u32[]{:S(2)}) collective-permute-start(f32[18,256,128]{2,1,0:T(8,128)S(1)} %input_terms.4), channel_id=1, source_target_pairs={{0,1},{1,0},{2,3},{3,2},{4,5},{5,4},{6,7},{7,6},{8,9},{9,8},{10,11... | collective-permute-start | bytes 7077896 | tf_op jit(solution)/shard_map/ppermute | solution.py:452
  51.1 13.8 %collective-permute-start.12 = (bf16[28,8,512]{2,1,0:T(8,128)(2,1)S(1)}, bf16[28,8,512]{2,1,0:T(8,128)(2,1)S(1)}, u32[]{:S(2)}, u32[]{:S(2)}) collective-permute-start(bf16[28,8,512]{2,1,0:T(8,128)(2,1)S(1)} %get-tuple-element.196), channel_id=1, source_target_pairs={{0,8},{8,16},{16,24},{24,28},{28,20},{20,12},{12,4},{4,0},{1,9},{9... | collective-permute-start | bytes 688136 | tf_op jit(solution)/shard_map/ppermute | solution.py:323
  51.4 13.4 %collective-permute-start.13 = (bf16[28,8,512]{2,1,0:T(8,128)(2,1)S(1)}, bf16[28,8,512]{2,1,0:T(8,128)(2,1)S(1)}, u32[]{:S(2)}, u32[]{:S(2)}) collective-permute-start(bf16[28,8,512]{2,1,0:T(8,128)(2,1)S(1)} %get-tuple-element.220), channel_id=1, source_target_pairs={{8,0},{16,8},{24,16},{28,24},{20,28},{12,20},{4,12},{0,4},{9,1},{1... | collective-permute-start | bytes 688136 | tf_op jit(solution)/shard_map/ppermute | solution.py:323
  58.9 5.5 %collective-permute-start.7 = (bf16[15,8,512]{2,1,0:T(8,128)(2,1)S(1)}, bf16[15,8,512]{2,1,0:T(8,128)(2,1)S(1)}, u32[]{:S(2)}, u32[]{:S(2)}) collective-permute-start(bf16[15,8,512]{2,1,0:T(8,128)(2,1)S(1)} %get-tuple-element.204), channel_id=1, source_target_pairs={{0,8},{8,16},{16,24},{24,28},{28,20},{20,12},{12,4},{4,0},{1,9},{9... | collective-permute-start | bytes 368648 | tf_op jit(solution)/shard_map/ppermute | solution.py:323
  59.3 5.1 %collective-permute-start.8 = (bf16[14,8,512]{2,1,0:T(8,128)(2,1)S(1)}, bf16[14,8,512]{2,1,0:T(8,128)(2,1)S(1)}, u32[]{:S(2)}, u32[]{:S(2)}) collective-permute-start(bf16[14,8,512]{2,1,0:T(8,128)(2,1)S(1)} %get-tuple-element.205), channel_id=1, source_target_pairs={{8,0},{16,8},{24,16},{28,24},{20,28},{12,20},{4,12},{0,4},{9,1},{1... | collective-permute-start | bytes 344072 | tf_op jit(solution)/shard_map/ppermute | solution.py:323
  65.5 55.5 %collective-permute-start.34 = (f32[15,256,128]{2,1,0:T(8,128)S(1)}, f32[15,256,128]{2,1,0:T(8,128)S(1)}, u32[]{:S(2)}, u32[]{:S(2)}) collective-permute-start(f32[15,256,128]{2,1,0:T(8,128)S(1)} %get-tuple-element.292), channel_id=1, source_target_pairs={{0,2},{1,3},{2,0},{3,1},{4,6},{5,7},{6,4},{7,5},{8,10},{9,11},{10,... | collective-permute-start | bytes 5898248 | tf_op jit(solution)/shard_map/ppermute | solution.py:459
  66.1 8.5 %collective-permute-start.11 = (bf16[28,8,512]{2,1,0:T(8,128)(2,1)S(1)}, bf16[28,8,512]{2,1,0:T(8,128)(2,1)S(1)}, u32[]{:S(2)}, u32[]{:S(2)}) collective-permute-start(bf16[28,8,512]{2,1,0:T(8,128)(2,1)S(1)} %get-tuple-element.219), channel_id=1, source_target_pairs={{8,0},{16,8},{24,16},{28,24},{20,28},{12,20},{4,12},{0,4},{9,1},{1... | collective-permute-start | bytes 688136 | tf_op jit(solution)/shard_map/ppermute | solution.py:323
  67.5 8.3 %collective-permute-start.10 = (bf16[28,8,512]{2,1,0:T(8,128)(2,1)S(1)}, bf16[28,8,512]{2,1,0:T(8,128)(2,1)S(1)}, u32[]{:S(2)}, u32[]{:S(2)}) collective-permute-start(bf16[28,8,512]{2,1,0:T(8,128)(2,1)S(1)} %get-tuple-element.218), channel_id=1, source_target_pairs={{0,8},{8,16},{16,24},{24,28},{28,20},{20,12},{12,4},{4,0},{1,9},{9... | collective-permute-start | bytes 688136 | tf_op jit(solution)/shard_map/ppermute | solution.py:323
  68.1 12.5 %collective-permute-start.16 = (bf16[28,8,512]{2,1,0:T(8,128)(2,1)S(1)}, bf16[28,8,512]{2,1,0:T(8,128)(2,1)S(1)}, u32[]{:S(2)}, u32[]{:S(2)}) collective-permute-start(bf16[28,8,512]{2,1,0:T(8,128)(2,1)S(1)} %get-tuple-element.227), channel_id=1, source_target_pairs={{0,8},{8,16},{16,24},{24,28},{28,20},{20,12},{12,4},{4,0},{1,9},{9... | collective-permute-start | bytes 688136 | tf_op jit(solution)/shard_map/ppermute | solution.py:323
  68.9 10.7 %collective-permute-start.17 = (bf16[28,8,512]{2,1,0:T(8,128)(2,1)S(1)}, bf16[28,8,512]{2,1,0:T(8,128)(2,1)S(1)}, u32[]{:S(2)}, u32[]{:S(2)}) collective-permute-start(bf16[28,8,512]{2,1,0:T(8,128)(2,1)S(1)} %get-tuple-element.239), channel_id=1, source_target_pairs={{8,0},{16,8},{24,16},{28,24},{20,28},{12,20},{4,12},{0,4},{9,1},{1... | collective-permute-start | bytes 688136 | tf_op jit(solution)/shard_map/ppermute | solution.py:323
  76.4 8.6 %collective-permute-start.15 = (bf16[28,8,512]{2,1,0:T(8,128)(2,1)S(1)}, bf16[28,8,512]{2,1,0:T(8,128)(2,1)S(1)}, u32[]{:S(2)}, u32[]{:S(2)}) collective-permute-start(bf16[28,8,512]{2,1,0:T(8,128)(2,1)S(1)} %get-tuple-element.238), channel_id=1, source_target_pairs={{8,0},{16,8},{24,16},{28,24},{20,28},{12,20},{4,12},{0,4},{9,1},{1... | collective-permute-start | bytes 688136 | tf_op jit(solution)/shard_map/ppermute | solution.py:323
  77.8 7.8 %collective-permute-start.14 = (bf16[28,8,512]{2,1,0:T(8,128)(2,1)S(1)}, bf16[28,8,512]{2,1,0:T(8,128)(2,1)S(1)}, u32[]{:S(2)}, u32[]{:S(2)}) collective-permute-start(bf16[28,8,512]{2,1,0:T(8,128)(2,1)S(1)} %get-tuple-element.237), channel_id=1, source_target_pairs={{0,8},{8,16},{16,24},{24,28},{28,20},{20,12},{12,4},{4,0},{1,9},{9... | collective-permute-start | bytes 688136 | tf_op jit(solution)/shard_map/ppermute | solution.py:323
  81.3 7.8 %collective-permute-start.19 = (bf16[28,8,512]{2,1,0:T(8,128)(2,1)S(1)}, bf16[28,8,512]{2,1,0:T(8,128)(2,1)S(1)}, u32[]{:S(2)}, u32[]{:S(2)}) collective-permute-start(bf16[28,8,512]{2,1,0:T(8,128)(2,1)S(1)} %get-tuple-element.257), channel_id=1, source_target_pairs={{8,0},{16,8},{24,16},{28,24},{20,28},{12,20},{4,12},{0,4},{9,1},{1... | collective-permute-start | bytes 688136 | tf_op jit(solution)/shard_map/ppermute | solution.py:323
  82.7 6.3 %collective-permute-start.18 = (bf16[28,8,512]{2,1,0:T(8,128)(2,1)S(1)}, bf16[28,8,512]{2,1,0:T(8,128)(2,1)S(1)}, u32[]{:S(2)}, u32[]{:S(2)}) collective-permute-start(bf16[28,8,512]{2,1,0:T(8,128)(2,1)S(1)} %get-tuple-element.246), channel_id=1, source_target_pairs={{0,8},{8,16},{16,24},{24,28},{28,20},{20,12},{12,4},{4,0},{1,9},{9... | collective-permute-start | bytes 688136 | tf_op jit(solution)/shard_map/ppermute | solution.py:323
  89.6 7.1 %collective-permute-start.21 = (bf16[28,8,512]{2,1,0:T(8,128)(2,1)S(1)}, bf16[28,8,512]{2,1,0:T(8,128)(2,1)S(1)}, u32[]{:S(2)}, u32[]{:S(2)}) collective-permute-start(bf16[28,8,512]{2,1,0:T(8,128)(2,1)S(1)} %last_hop.2.refs_0_), channel_id=1, source_target_pairs={{8,0},{16,8},{24,16},{28,24},{20,28},{12,20},{4,12},{0,4},{9,1},{1... | collective-permute-start | bytes 688136 | tf_op jit(solution)/shard_map/ppermute | solution.py:323
  91.2 7.2 %collective-permute-start.20 = (bf16[28,8,512]{2,1,0:T(8,128)(2,1)S(1)}, bf16[28,8,512]{2,1,0:T(8,128)(2,1)S(1)}, u32[]{:S(2)}, u32[]{:S(2)}) collective-permute-start(bf16[28,8,512]{2,1,0:T(8,128)(2,1)S(1)} %last_hop.2.refs_0_), channel_id=1, source_target_pairs={{0,8},{8,16},{16,24},{24,28},{28,20},{20,12},{12,4},{4,0},{1,9},{9... | collective-permute-start | bytes 688136 | tf_op jit(solution)/shard_map/ppermute | solution.py:323
  91.6 9.9 %collective-permute-start.25 = (bf16[28,8,512]{2,1,0:T(8,128)(2,1)S(1)}, bf16[28,8,512]{2,1,0:T(8,128)(2,1)S(1)}, u32[]{:S(2)}, u32[]{:S(2)}) collective-permute-start(bf16[28,8,512]{2,1,0:T(8,128)(2,1)S(1)} %get-tuple-element.266), channel_id=1, source_target_pairs={{8,0},{16,8},{24,16},{28,24},{20,28},{12,20},{4,12},{0,4},{9,1},{1... | collective-permute-start | bytes 688136 | tf_op jit(solution)/shard_map/ppermute | solution.py:323
  93.2 10.1 %collective-permute-start.24 = (bf16[28,8,512]{2,1,0:T(8,128)(2,1)S(1)}, bf16[28,8,512]{2,1,0:T(8,128)(2,1)S(1)}, u32[]{:S(2)}, u32[]{:S(2)}) collective-permute-start(bf16[28,8,512]{2,1,0:T(8,128)(2,1)S(1)} %get-tuple-element.253), channel_id=1, source_target_pairs={{0,8},{8,16},{16,24},{24,28},{28,20},{20,12},{12,4},{4,0},{1,9},{9... | collective-permute-start | bytes 688136 | tf_op jit(solution)/shard_map/ppermute | solution.py:323
  98.4 9.6 %collective-permute-start.23 = (bf16[28,8,512]{2,1,0:T(8,128)(2,1)S(1)}, bf16[28,8,512]{2,1,0:T(8,128)(2,1)S(1)}, u32[]{:S(2)}, u32[]{:S(2)}) collective-permute-start(bf16[28,8,512]{2,1,0:T(8,128)(2,1)S(1)} %collective-permute-done.21.refs_2_), channel_id=1, source_target_pairs={{8,0},{16,8},{24,16},{28,24},{20,28},{12,20},{4,12},{0,4},{9,1},{1... | collective-permute-start | bytes 688136 | tf_op jit(solution)/shard_map/ppermute | solution.py:323
  100.6 8.5 %collective-permute-start.22 = (bf16[28,8,512]{2,1,0:T(8,128)(2,1)S(1)}, bf16[28,8,512]{2,1,0:T(8,128)(2,1)S(1)}, u32[]{:S(2)}, u32[]{:S(2)}) collective-permute-start(bf16[28,8,512]{2,1,0:T(8,128)(2,1)S(1)} %collective-permute-done.20.refs_1_), channel_id=1, source_target_pairs={{0,8},{8,16},{16,24},{24,28},{28,20},{20,12},{12,4},{4,0},{1,9},{9... | collective-permute-start | bytes 688136 | tf_op jit(solution)/shard_map/ppermute | solution.py:323
  103.8 8.6 %collective-permute-start.29 = (bf16[28,8,512]{2,1,0:T(8,128)(2,1)S(1)}, bf16[28,8,512]{2,1,0:T(8,128)(2,1)S(1)}, u32[]{:S(2)}, u32[]{:S(2)}) collective-permute-start(bf16[28,8,512]{2,1,0:T(8,128)(2,1)S(1)} %last_hop.3.refs_2_), channel_id=1, source_target_pairs={{8,0},{16,8},{24,16},{28,24},{20,28},{12,20},{4,12},{0,4},{9,1},{1... | collective-permute-start | bytes 688136 | tf_op jit(solution)/shard_map/ppermute | solution.py:323
  106.1 8.5 %collective-permute-start.28 = (bf16[28,8,512]{2,1,0:T(8,128)(2,1)S(1)}, bf16[28,8,512]{2,1,0:T(8,128)(2,1)S(1)}, u32[]{:S(2)}, u32[]{:S(2)}) collective-permute-start(bf16[28,8,512]{2,1,0:T(8,128)(2,1)S(1)} %last_hop.3.refs_2_), channel_id=1, source_target_pairs={{0,8},{8,16},{16,24},{24,28},{28,20},{20,12},{12,4},{4,0},{1,9},{9... | collective-permute-start | bytes 688136 | tf_op jit(solution)/shard_map/ppermute | solution.py:323
  109.1 9.7 %collective-permute-start.27 = (bf16[28,8,512]{2,1,0:T(8,128)(2,1)S(1)}, bf16[28,8,512]{2,1,0:T(8,128)(2,1)S(1)}, u32[]{:S(2)}, u32[]{:S(2)}) collective-permute-start(bf16[28,8,512]{2,1,0:T(8,128)(2,1)S(1)} %collective-permute-done.23.refs_1_), channel_id=1, source_target_pairs={{8,0},{16,8},{24,16},{28,24},{20,28},{12,20},{4,12},{0,4},{9,1},{1... | collective-permute-start | bytes 688136 | tf_op jit(solution)/shard_map/ppermute | solution.py:323
  110.4 8.4 %collective-permute-start.26 = (bf16[28,8,512]{2,1,0:T(8,128)(2,1)S(1)}, bf16[28,8,512]{2,1,0:T(8,128)(2,1)S(1)}, u32[]{:S(2)}, u32[]{:S(2)}) collective-permute-start(bf16[28,8,512]{2,1,0:T(8,128)(2,1)S(1)} %collective-permute-done.22.refs_0_), channel_id=1, source_target_pairs={{0,8},{8,16},{16,24},{24,28},{28,20},{20,12},{12,4},{4,0},{1,9},{9... | collective-permute-start | bytes 688136 | tf_op jit(solution)/shard_map/ppermute | solution.py:323
  114.6 6.4 %collective-permute-start.32 = (bf16[28,8,512]{2,1,0:T(8,128)(2,1)S(1)}, bf16[28,8,512]{2,1,0:T(8,128)(2,1)S(1)}, u32[]{:S(2)}, u32[]{:S(2)}) collective-permute-start(bf16[28,8,512]{2,1,0:T(8,128)(2,1)S(1)} %collective-permute-done.28.refs_3_), channel_id=1, source_target_pairs={{0,8},{8,16},{16,24},{24,28},{28,20},{20,12},{12,4},{4,0},{1,9},{9... | collective-permute-start | bytes 688136 | tf_op jit(solution)/shard_map/ppermute | solution.py:323
  114.6 6.4 %collective-permute-start.33 = (bf16[28,8,512]{2,1,0:T(8,128)(2,1)S(1)}, bf16[28,8,512]{2,1,0:T(8,128)(2,1)S(1)}, u32[]{:S(2)}, u32[]{:S(2)}) collective-permute-start(bf16[28,8,512]{2,1,0:T(8,128)(2,1)S(1)} %collective-permute-done.29.refs_4_), channel_id=1, source_target_pairs={{8,0},{16,8},{24,16},{28,24},{20,28},{12,20},{4,12},{0,4},{9,1},{1... | collective-permute-start | bytes 688136 | tf_op jit(solution)/shard_map/ppermute | solution.py:323
  118.9 4.8 %collective-permute-start.30 = (bf16[14,8,512]{2,1,0:T(8,128)(2,1)S(1)}, bf16[14,8,512]{2,1,0:T(8,128)(2,1)S(1)}, u32[]{:S(2)}, u32[]{:S(2)}) collective-permute-start(bf16[14,8,512]{2,1,0:T(8,128)(2,1)S(1)} %slice.12), channel_id=1, source_target_pairs={{0,8},{8,16},{16,24},{24,28},{28,20},{20,12},{12,4},{4,0},{1,9},{9... | collective-permute-start | bytes 344072 | tf_op jit(solution)/shard_map/ppermute | solution.py:323
  119.0 4.8 %collective-permute-start.31 = (bf16[14,8,512]{2,1,0:T(8,128)(2,1)S(1)}, bf16[14,8,512]{2,1,0:T(8,128)(2,1)S(1)}, u32[]{:S(2)}, u32[]{:S(2)}) collective-permute-start(bf16[14,8,512]{2,1,0:T(8,128)(2,1)S(1)} %slice.13), channel_id=1, source_target_pairs={{8,0},{16,8},{24,16},{28,24},{20,28},{12,20},{4,12},{0,4},{9,1},{1... | collective-permute-start | bytes 344072 | tf_op jit(solution)/shard_map/ppermute | solution.py:323
  123.8 13.9 %collective-permute-start.35 = (f32[18,256,128]{2,1,0:T(8,128)S(1)}, f32[18,256,128]{2,1,0:T(8,128)S(1)}, u32[]{:S(2)}, u32[]{:S(2)}) collective-permute-start(f32[18,256,128]{2,1,0:T(8,128)S(1)} %input_terms.6), channel_id=1, source_target_pairs={{0,1},{1,0},{2,3},{3,2},{4,5},{5,4},{6,7},{7,6},{8,9},{9,8},{10,11... | collective-permute-start | bytes 7077896 | tf_op jit(solution)/shard_map/ppermute | solution.py:491
  123.8 8.0 %collective-permute-start.38 = (bf16[28,8,512]{2,1,0:T(8,128)(2,1)S(1)}, bf16[28,8,512]{2,1,0:T(8,128)(2,1)S(1)}, u32[]{:S(2)}, u32[]{:S(2)}) collective-permute-start(bf16[28,8,512]{2,1,0:T(8,128)(2,1)S(1)} %collective-permute-done.33.refs_3_), channel_id=1, source_target_pairs={{8,0},{16,8},{24,16},{28,24},{20,28},{12,20},{4,12},{0,4},{9,1},{1... | collective-permute-start | bytes 688136 | tf_op jit(solution)/shard_map/ppermute | solution.py:323
  125.8 7.7 %collective-permute-start.37 = (bf16[28,8,512]{2,1,0:T(8,128)(2,1)S(1)}, bf16[28,8,512]{2,1,0:T(8,128)(2,1)S(1)}, u32[]{:S(2)}, u32[]{:S(2)}) collective-permute-start(bf16[28,8,512]{2,1,0:T(8,128)(2,1)S(1)} %collective-permute-done.32.refs_2_), channel_id=1, source_target_pairs={{0,8},{8,16},{16,24},{24,28},{28,20},{20,12},{12,4},{4,0},{1,9},{9... | collective-permute-start | bytes 688136 | tf_op jit(solution)/shard_map/ppermute | solution.py:323
  125.8 11.7 %collective-permute-start.36 = (f32[3,256,128]{2,1,0:T(8,128)S(1)}, f32[3,256,128]{2,1,0:T(8,128)S(1)}, u32[]{:S(2)}, u32[]{:S(2)}) collective-permute-start(f32[3,256,128]{2,1,0:T(8,128)S(1)} %get-tuple-element.303), channel_id=1, source_target_pairs={{0,2},{1,3},{2,0},{3,1},{4,6},{5,7},{6,4},{7,5},{8,10},{9,11},{10,... | collective-permute-start | bytes 1179656 | tf_op jit(solution)/shard_map/ppermute | solution.py:488
  133.6 5.7 %collective-permute-start.40 = (bf16[14,8,512]{2,1,0:T(8,128)(2,1)S(1)}, bf16[14,8,512]{2,1,0:T(8,128)(2,1)S(1)}, u32[]{:S(2)}, u32[]{:S(2)}) collective-permute-start(bf16[14,8,512]{2,1,0:T(8,128)(2,1)S(1)} %slice.15), channel_id=1, source_target_pairs={{8,0},{16,8},{24,16},{28,24},{20,28},{12,20},{4,12},{0,4},{9,1},{1... | collective-permute-start | bytes 344072 | tf_op jit(solution)/shard_map/ppermute | solution.py:323
  134.7 4.8 %collective-permute-start.39 = (bf16[14,8,512]{2,1,0:T(8,128)(2,1)S(1)}, bf16[14,8,512]{2,1,0:T(8,128)(2,1)S(1)}, u32[]{:S(2)}, u32[]{:S(2)}) collective-permute-start(bf16[14,8,512]{2,1,0:T(8,128)(2,1)S(1)} %slice.14), channel_id=1, source_target_pairs={{0,8},{8,16},{16,24},{24,28},{28,20},{20,12},{12,4},{4,0},{1,9},{9... | collective-permute-start | bytes 344072 | tf_op jit(solution)/shard_map/ppermute | solution.py:323

commit v2 on v1

--- a/solution.py
+++ b/solution.py
@@ -434,7 +434,7 @@
         return order(functools.partial(kernel_terms, count=count), table, grid, flat)
 
     half = ring.half
-    most, whole = (cols * 5 // 6, cols // 6), (cols,)
+    whole = (cols,)
     shape = (3 * TAPS, chans, total)
     written = []
 
@@ -451,12 +451,12 @@
     near.hop()
     away = lax.ppermute(order.gate(away)[0], "ch", to_core)
     far = Chain(ring, order, 1, *features_with(flat_far))
-    across = list(terms_of(1, most, away))
+    (across,) = terms_of(1, whole, away)
     far.arrive()
     far.hop()
     near.arrive()
     near.hop()
-    across[0] = lax.ppermute(order.gate(across[0])[0], "ch", to_x)
+    across = lax.ppermute(order.gate(across)[0], "ch", to_x)
     (beside,) = terms_of(2, whole)
     for _ in range(half - 4):
         far.arrive()
@@ -472,29 +472,27 @@
     (mine,) = terms_of(3, whole)
     near.arrive()
     near.last()
-    near.move()
     far.arrive()
     far.last()
+    near.move()
     write(near)
+    far.move()
+    write(far)
     near.move()
+    for _ in range(half - 4):
+        far.move()
+        near.move()
     far.move()
-    for _ in range(half - 4):
-        near.move()
-        far.move()
     write(near, far)
     near.move()
+    across = order.pin(across)[0]
     far.move()
-    across[0] = order.pin(across[0])[0]
-    across[1] = lax.ppermute(order.gate(across[1])[0], "ch", to_x)
+    beside = lax.ppermute(order.gate(beside)[0], "ch", to_core)
     write(near, far)
-    near.move()
-    beside = lax.ppermute(order.gate(beside)[0], "ch", to_core)
-    far.move()
-    write(near, far)
-    across = jnp.concatenate(across, axis=0)
     input_grad = order(lambda *parts: sum(parts).astype(jnp.bfloat16), mine, beside, across)
     far.move()
-    write(far)
+    near.move()
+    write(near, far)
     kernel_grad = written[0]
 
     input_grad = jnp.transpose(input_grad, (1, 0, 2)).reshape(block, 1, cols, rows)

time: 142 us -> 134 us (0.944)
  waiting for transfers between devices: 43.2 us -> 38.9 us
  starting transfers between devices: 43.5 us -> 41.7 us
    ppermute x16, starting transfers between devices: 27.6 us -> 20.6 us  [send(): lax.ppermute(down, 'lon', self.behind)]
    ppermute x16, starting transfers between devices: 6.06 us -> 12.7 us  [send(): lax.ppermute(up, 'lon', self.ahead)]
    ppermute x16, waiting for transfers between devices: 14.1 us -> 8.92 us  [send(): lax.ppermute(down, 'lon', self.behind)]
    ppermute x2 -> x1, starting transfers between devices: 2.11 us -> 0.6 us  [local(): across = lax.ppermute(order.gate(across)[0], 'ch', to_x)]
  transfers between devices with their start and end apart: 41 -> 40, of which waited for: 20 -> 21; matrix products, arithmetic and copies ran while one was open for 6% -> 6% of each run, Pallas kernels for 30% -> 31%
where the time goes in v2:
time: 134 us
  Pallas kernels  43.8 us (33%)
  starting transfers between devices  41.7 us (31%)
  waiting for transfers between devices  38.9 us (29%)
  local copies, waits for them, and re-layouts  6.91 us (5%)
  other arithmetic  1.69 us (1%)
    pallas_call x19, Pallas kernels, direct(): pl.pallas_call(kernel, in_specs=([] if table is None else [smem]) + [vmem...  32 us
    ppermute x16, starting transfers between devices, send(): lax.ppermute(down, 'lon', self.behind)  20.6 us
    ppermute x1, waiting for transfers between devices, local(): lax.ppermute(heads, 'lon', [((i + 1) % count, i) for i in range(count)])  16.3 us
    ppermute x16, waiting for transfers between devices, send(): lax.ppermute(up, 'lon', self.ahead)  13.7 us
    ppermute x16, starting transfers between devices, send(): lax.ppermute(up, 'lon', self.ahead)  12.7 us
    pallas_call x5, Pallas kernels, unfold(): pl.pallas_call(functools.partial(unfold_kernel, norm, places), in_specs=[...  9.48 us
    ppermute x16, waiting for transfers between devices, send(): lax.ppermute(down, 'lon', self.behind)  8.92 us
    optimization_barrier x1, local copies, waits for them, and re-layouts, gate(): return lax.optimization_barrier(values + self.last)[:len(values)]  5.87 us
  transfers between devices with their start and end apart: 40, of which 21 were waited for; matrix products, arithmetic and copies ran while one was open for 6% of the time, Pallas kernels for 31%

profile of v2, /device:TPU:0, one launch (start us, length us, event | category | flops | bytes accessed | tf_op | source)
XLA Modules:
  0.0 134.1 jit_solution(14212126536510595024)
XLA Ops:
  1.1 2.6 %collective-permute-start.2 = (bf16[18,256,128]{2,1,0:T(8,128)(2,1)}, bf16[18,256,128]{2,1,0:T(8,128)(2,1)S(1)}, u32[]{:S(2)}, u32[]{:S(2)}) collective-permute-start(bf16[18,256,128]{2,1,0:T(8,128)(2,1)} %bitcast.25), channel_id=1, source_target_pairs={{0,2},{1,3},{2,0},{3,1},{4,6},{5,7},{6,4},{7,5},{8,10},{9,11},{10,... | collective-permute-start | bytes 3538952 | tf_op jit(solution)/shard_map/ppermute | solution.py:413
  3.7 2.3 %edges.1 = (bf16[36,64,128]{2,1,0:T(8,128)(2,1)}, bf16[36,64,128]{2,1,0:T(8,128)(2,1)}) custom-call(bf16[3,18,64,128]{3,2,1,0:T(8,128)(2,1)} %bitcast.27), custom_call_target="tpu_custom_call" | custom-call | flops 300000000 | tf_op jit(solution)/shard_map/edges/pallas_call | solution.py:84
  6.0 4.6 %collective-permute-start.1 = (bf16[36,64,128]{2,1,0:T(8,128)(2,1)}, bf16[36,64,128]{2,1,0:T(8,128)(2,1)}, u32[]{:S(2)}, u32[]{:S(2)}) collective-permute-start(bf16[36,64,128]{2,1,0:T(8,128)(2,1)} %get-tuple-element.162), channel_id=1, source_target_pairs={{4,0},{8,4},{12,8},{16,12},{20,16},{24,20},{28,24},{0,28},{5,1},{9... | collective-permute-start | bytes 1769480 | tf_op jit(solution)/shard_map/ppermute | solution.py:409
  10.9 5.9 %copy.10 = bf16[1728,1024]{0,1:T(8,128)(2,1)} copy(bf16[1728,1024]{1,0:T(8,128)(2,1)} %bitcast.30) | data formatting | bytes 7077888 | tf_op jit(solution)/shard_map/optimization_barrier | solution.py:300
  16.8 1.2 flatten.2.feat_ref
  18.0 16.3 %collective-permute-done.1.right_ref = bf16[36,64,128]{2,1,0:T(8,128)(2,1)} collective-permute-done((bf16[36,64,128]{2,1,0:T(8,128)(2,1)}, bf16[36,64,128]{2,1,0:T(8,128)(2,1)}, u32[]{:S(2)}, u32[]{:S(2)}) %collective-permute-start.1) | collective-permute-done | bytes 589856 | tf_op jit(solution)/shard_map/ppermute | solution.py:409
  34.4 2.5 %spread.1.grid_ref = bf16[1728,2304]{1,0:T(8,128)(2,1)S(1)} custom-call(bf16[3,18,64,128]{3,2,1,0:T(8,128)(2,1)S(1)} %bitcast.28, bf16[36,64,128]{2,1,0:T(8,128)(2,1)} %collective-permute-done.left_ref, bf16[36,64,128]{2,1,0:T(8,128)(2,1)} %collective-permute-done.1.right_ref), custom_call_target="tpu_custom_call" | custom-call | flops 600000000 | tf_op jit(solution)/shard_map/spread/pallas_call | solution.py:61
  36.9 5.6 %kernel_terms.2 = (f32[8,27,8,512]{3,2,1,0:T(8,128)S(1)}, f32[1,8,512]{2,1,0:T(8,128)S(1)}) custom-call(s32[30]{0:T(128)S(1)} %concatenate.9.place_ref.table_ref, bf16[1728,2304]{1,0:T(8,128)(2,1)S(1)} %spread.1.grid_ref, bf16[2304,512]{1,0:T(8,128)(2,1)S(1)} %flatten.2.feat_ref), custom_call_target="tpu_custom_call" | custom-call | flops 1800000000 | tf_op jit(solution)/shard_map/kernel_terms/pallas_call | solution.py:61
  42.6 2.5 %collective-permute-start.6 = (bf16[14,8,512]{2,1,0:T(8,128)(2,1)S(1)}, bf16[14,8,512]{2,1,0:T(8,128)(2,1)S(1)}, u32[]{:S(2)}, u32[]{:S(2)}) collective-permute-start(bf16[14,8,512]{2,1,0:T(8,128)(2,1)S(1)} %get-tuple-element.183), channel_id=1, source_target_pairs={{8,0},{16,8},{24,16},{28,24},{20,28},{12,20},{4,12},{0,4},{9,1},{1... | collective-permute-start | bytes 344072 | tf_op jit(solution)/shard_map/ppermute | solution.py:323
  45.1 1.2 flatten.3.feat_ref
  46.3 0.8 copy-done
  47.2 2.8 %input_terms.4 = f32[18,256,128]{2,1,0:T(8,128)S(1)} custom-call(s32[30]{0:T(128)S(1)} %concatenate.9.place_ref.table_ref, bf16[1024,1728]{1,0:T(8,128)(2,1)S(1)} %bitcast.20, bf16[1728,2304]{1,0:T(8,128)(2,1)S(1)} %spread.1.grid_ref), custom_call_target="tpu_custom_call" | custom-call | flops 1050000000 | tf_op jit(solution)/shard_map/input_terms/pallas_call | solution.py:61
  51.4 1.7 %collective-permute-start.13 = (bf16[28,8,512]{2,1,0:T(8,128)(2,1)S(1)}, bf16[28,8,512]{2,1,0:T(8,128)(2,1)S(1)}, u32[]{:S(2)}, u32[]{:S(2)}) collective-permute-start(bf16[28,8,512]{2,1,0:T(8,128)(2,1)S(1)} %get-tuple-element.216), channel_id=1, source_target_pairs={{8,0},{16,8},{24,16},{28,24},{20,28},{12,20},{4,12},{0,4},{9,1},{1... | collective-permute-start | bytes 688136 | tf_op jit(solution)/shard_map/ppermute | solution.py:323
  53.2 5.6 %kernel_terms.3 = (f32[8,27,8,512]{3,2,1,0:T(8,128)S(1)}, f32[1,8,512]{2,1,0:T(8,128)S(1)}) custom-call(s32[30]{0:T(128)S(1)} %concatenate.9.place_ref.table_ref, bf16[1728,2304]{1,0:T(8,128)(2,1)S(1)} %spread.1.grid_ref, bf16[2304,512]{1,0:T(8,128)(2,1)S(1)} %flatten.3.feat_ref), custom_call_target="tpu_custom_call" | custom-call | flops 1800000000 | tf_op jit(solution)/shard_map/kernel_terms/pallas_call | solution.py:61
  59.3 1.7 %collective-permute-start.8 = (bf16[14,8,512]{2,1,0:T(8,128)(2,1)S(1)}, bf16[14,8,512]{2,1,0:T(8,128)(2,1)S(1)}, u32[]{:S(2)}, u32[]{:S(2)}) collective-permute-start(bf16[14,8,512]{2,1,0:T(8,128)(2,1)S(1)} %get-tuple-element.202), channel_id=1, source_target_pairs={{8,0},{16,8},{24,16},{28,24},{20,28},{12,20},{4,12},{0,4},{9,1},{1... | collective-permute-start | bytes 344072 | tf_op jit(solution)/shard_map/ppermute | solution.py:323
  61.0 2.8 %input_terms.5 = f32[18,256,128]{2,1,0:T(8,128)S(1)} custom-call(s32[30]{0:T(128)S(1)} %concatenate.9.place_ref.table_ref, bf16[1024,1728]{1,0:T(8,128)(2,1)S(1)} %bitcast.21, bf16[1728,2304]{1,0:T(8,128)(2,1)S(1)} %spread.1.grid_ref, f32[18,256,128]{2,1,0:T(8,128)S(1)} %collective-permute-done.9.refs_0_), custom_call_target="tpu_custom_call" | custom-call | flops 1050000000 | tf_op jit(solution)/shard_map/input_terms/pallas_call | solution.py:61
  64.6 0.6 next_hop.8
  65.8 1.7 %collective-permute-start.11 = (bf16[28,8,512]{2,1,0:T(8,128)(2,1)S(1)}, bf16[28,8,512]{2,1,0:T(8,128)(2,1)S(1)}, u32[]{:S(2)}, u32[]{:S(2)}) collective-permute-start(bf16[28,8,512]{2,1,0:T(8,128)(2,1)S(1)} %get-tuple-element.215), channel_id=1, source_target_pairs={{8,0},{16,8},{24,16},{28,24},{20,28},{12,20},{4,12},{0,4},{9,1},{1... | collective-permute-start | bytes 688136 | tf_op jit(solution)/shard_map/ppermute | solution.py:323
  67.8 1.1 collective-permute-start.16
  68.9 0.9 collective-permute-start.17
  69.8 2.8 %input_terms.6 = f32[18,256,128]{2,1,0:T(8,128)S(1)} custom-call(s32[30]{0:T(128)S(1)} %concatenate.9.place_ref.table_ref, bf16[1024,1728]{1,0:T(8,128)(2,1)S(1)} %bitcast.22, bf16[1728,2304]{1,0:T(8,128)(2,1)S(1)} %spread.1.grid_ref), custom_call_target="tpu_custom_call" | custom-call | flops 1050000000 | tf_op jit(solution)/shard_map/input_terms/pallas_call | solution.py:61
  72.7 1.6 %collective-permute-done.11.down_ref = bf16[28,8,512]{2,1,0:T(8,128)(2,1)S(1)} collective-permute-done((bf16[28,8,512]{2,1,0:T(8,128)(2,1)S(1)}, bf16[28,8,512]{2,1,0:T(8,128)(2,1)S(1)}, u32[]{:S(2)}, u32[]{:S(2)}) %collective-permute-start.11) | collective-permute-done | bytes 229408 | tf_op jit(solution)/shard_map/ppermute | solution.py:323
  74.3 1.7 %collective-permute-done.10.up_ref = bf16[28,8,512]{2,1,0:T(8,128)(2,1)S(1)} collective-permute-done((bf16[28,8,512]{2,1,0:T(8,128)(2,1)S(1)}, bf16[28,8,512]{2,1,0:T(8,128)(2,1)S(1)}, u32[]{:S(2)}, u32[]{:S(2)}) %collective-permute-start.10) | collective-permute-done | bytes 229408 | tf_op jit(solution)/shard_map/ppermute | solution.py:323
  76.0 0.6 next_hop.9
  76.6 1.0 collective-permute-start.15
  77.6 1.1 collective-permute-start.14
  79.2 1.7 %collective-permute-done.16.up_ref = bf16[28,8,512]{2,1,0:T(8,128)(2,1)S(1)} collective-permute-done((bf16[28,8,512]{2,1,0:T(8,128)(2,1)S(1)}, bf16[28,8,512]{2,1,0:T(8,128)(2,1)S(1)}, u32[]{:S(2)}, u32[]{:S(2)}) %collective-permute-start.16) | collective-permute-done | bytes 229408 | tf_op jit(solution)/shard_map/ppermute | solution.py:323
  81.6 1.0 collective-permute-start.21
  82.5 1.1 collective-permute-start.20
  83.6 1.6 %collective-permute-done.15.down_ref = bf16[28,8,512]{2,1,0:T(8,128)(2,1)S(1)} collective-permute-done((bf16[28,8,512]{2,1,0:T(8,128)(2,1)S(1)}, bf16[28,8,512]{2,1,0:T(8,128)(2,1)S(1)}, u32[]{:S(2)}, u32[]{:S(2)}) %collective-permute-start.15) | collective-permute-done | bytes 229408 | tf_op jit(solution)/shard_map/ppermute | solution.py:323
  85.2 0.9 collective-permute-done.14.up_ref
  86.8 0.9 collective-permute-start.19
  87.6 1.2 collective-permute-start.18
  88.8 2.8 %input_terms.7 = f32[18,256,128]{2,1,0:T(8,128)S(1)} custom-call(s32[30]{0:T(128)S(1)} %concatenate.9.place_ref.table_ref, bf16[1024,1728]{1,0:T(8,128)(2,1)S(1)} %bitcast.23, bf16[1728,2304]{1,0:T(8,128)(2,1)S(1)} %spread.1.grid_ref), custom_call_target="tpu_custom_call" | custom-call | flops 1050000000 | tf_op jit(solution)/shard_map/input_terms/pallas_call | solution.py:61
  92.2 0.9 collective-permute-start.25
  93.1 1.2 collective-permute-start.24
  94.3 1.1 collective-permute-done.19.down_ref
  95.3 0.8 collective-permute-done.18.up_ref
  96.7 1.4 %collective-permute-start.23 = (bf16[28,8,512]{2,1,0:T(8,128)(2,1)S(1)}, bf16[28,8,512]{2,1,0:T(8,128)(2,1)S(1)}, u32[]{:S(2)}, u32[]{:S(2)}) collective-permute-start(bf16[28,8,512]{2,1,0:T(8,128)(2,1)S(1)} %last_hop.3.refs_0_), channel_id=1, source_target_pairs={{8,0},{16,8},{24,16},{28,24},{20,28},{12,20},{4,12},{0,4},{9,1},{1... | collective-permute-start | bytes 688136 | tf_op jit(solution)/shard_map/ppermute | solution.py:323
  98.1 0.7 collective-permute-start.22
  98.7 2.0 %collective-permute-done.25.refs_2_ = bf16[28,8,512]{2,1,0:T(8,128)(2,1)S(1)} collective-permute-done((bf16[28,8,512]{2,1,0:T(8,128)(2,1)S(1)}, bf16[28,8,512]{2,1,0:T(8,128)(2,1)S(1)}, u32[]{:S(2)}, u32[]{:S(2)}) %collective-permute-start.25) | collective-permute-done | bytes 229408 | tf_op jit(solution)/shard_map/ppermute | solution.py:323
  100.8 0.8 collective-permute-done.24.refs_1_
  101.6 1.2 collective-permute-start.28
  102.8 0.8 collective-permute-start.29
  103.6 1.9 %unfold.5.refs_3_ = f32[27,64,1024]{2,1,0:T(8,128)} custom-call(s32[30]{0:T(128)S(1)} %concatenate.9.place_ref.table_ref, bf16[28,8,512]{2,1,0:T(8,128)(2,1)S(1)} %last_hop.2.refs_0_, bf16[28,8,512]{2,1,0:T(8,128)(2,1)S(1)} %collective-permute-done.24.refs_1_, bf16[28,8,512]{2,1,0:T(8,128)(2,1)S(1)} %collective-permute-done.25.refs_2_), custom_call_target="tpu_custom_call" | custom-call | flops 900000000 | tf_op jit(solution)/shard_map/unfold/pallas_call | solution.py:230
  105.7 0.9 collective-permute-done.22.refs_1_
  106.6 1.1 collective-permute-start.26
  107.7 0.9 collective-permute-start.27
  108.6 1.9 %unfold.6.refs_4_ = f32[27,64,1024]{2,1,0:T(8,128)} custom-call(s32[30]{0:T(128)S(1)} %concatenate.9.place_ref.table_ref, bf16[28,8,512]{2,1,0:T(8,128)(2,1)S(1)} %last_hop.3.refs_0_, bf16[28,8,512]{2,1,0:T(8,128)(2,1)S(1)} %collective-permute-done.22.refs_1_, ...), custom_call_target="tpu_custom_call", output_to_operand_aliasing={{}: (4, {})} | custom-call | flops 900000000 | tf_op jit(solution)/shard_map/unfold/pallas_call | solution.py:230
  110.5 1.0 collective-permute-done.28.refs_0_
  111.5 1.8 %collective-permute-start.34 = (bf16[28,8,512]{2,1,0:T(8,128)(2,1)S(1)}, bf16[28,8,512]{2,1,0:T(8,128)(2,1)S(1)}, u32[]{:S(2)}, u32[]{:S(2)}) collective-permute-start(bf16[28,8,512]{2,1,0:T(8,128)(2,1)S(1)} %collective-permute-done.29.refs_1_), channel_id=1, source_target_pairs={{8,0},{16,8},{24,16},{28,24},{20,28},{12,20},{4,12},{0,4},{9,1},{1... | collective-permute-start | bytes 688136 | tf_op jit(solution)/shard_map/ppermute | solution.py:323
  113.6 2.9 %collective-permute-done.26.refs_2_ = bf16[28,8,512]{2,1,0:T(8,128)(2,1)S(1)} collective-permute-done((bf16[28,8,512]{2,1,0:T(8,128)(2,1)S(1)}, bf16[28,8,512]{2,1,0:T(8,128)(2,1)S(1)}, u32[]{:S(2)}, u32[]{:S(2)}) %collective-permute-start.26) | collective-permute-done | bytes 229408 | tf_op jit(solution)/shard_map/ppermute | solution.py:323
  116.5 1.1 collective-permute-start.30
  117.6 0.9 collective-permute-start.31
  118.5 2.0 %unfold.7.refs_4_ = f32[27,64,1024]{2,1,0:T(8,128)} custom-call(s32[30]{0:T(128)S(1)} %concatenate.9.place_ref.table_ref, bf16[28,8,512]{2,1,0:T(8,128)(2,1)S(1)} %collective-permute-done.28.refs_0_, bf16[28,8,512]{2,1,0:T(8,128)(2,1)S(1)} %collective-permute-done.29.refs_1_, ...), custom_call_target="tpu_custom_call", output_to_operand_aliasing={{}: (5, {})} | custom-call | flops 900000000 | tf_op jit(solution)/shard_map/unfold/pallas_call | solution.py:230
  120.6 1.9 %collective-permute-done.30.refs_2_ = bf16[28,8,512]{2,1,0:T(8,128)(2,1)S(1)} collective-permute-done((bf16[28,8,512]{2,1,0:T(8,128)(2,1)S(1)}, bf16[28,8,512]{2,1,0:T(8,128)(2,1)S(1)}, u32[]{:S(2)}, u32[]{:S(2)}) %collective-permute-start.30) | collective-permute-done | bytes 229408 | tf_op jit(solution)/shard_map/ppermute | solution.py:323
  122.5 1.1 collective-permute-done.31.refs_3_
  123.6 0.9 collective-permute-start.36
  124.5 1.2 collective-permute-start.37
  125.7 0.9 collective-permute-start.38
  126.6 1.2 collective-permute-start.39
  127.8 2.0 %unfold.8.refs_2_ = f32[27,64,1024]{2,1,0:T(8,128)} custom-call(s32[30]{0:T(128)S(1)} %concatenate.9.place_ref.table_ref, bf16[28,8,512]{2,1,0:T(8,128)(2,1)S(1)} %collective-permute-done.33.refs_0_, bf16[28,8,512]{2,1,0:T(8,128)(2,1)S(1)} %collective-permute-done.34.refs_1_, ...), custom_call_target="tpu_custom_call", output_to_operand_aliasing={{}: (5, {})} | custom-call | flops 900000000 | tf_op jit(solution)/shard_map/unfold/pallas_call | solution.py:230
  129.9 1.5 %add_convert_fusion = bf16[18,256,128]{2,1,0:T(8,128)(2,1)} fusion(f32[18,256,128]{2,1,0:T(8,128)S(1)} %collective-permute-done.32, f32[18,256,128]{2,1,0:T(8,128)S(1)} %input_terms.7, f32[18,256,128]{2,1,0:T(8,128)S(1)} %collective-permute-done.35), kind=kLoop, calls=%fused_computation | loop fusion | flops 1769472 | bytes 8257536 | tf_op jit(solution)/shard_map/convert_element_type | solution.py:492
  132.3 1.7 %unfold.9 = f32[27,64,1024]{2,1,0:T(8,128)} custom-call(s32[30]{0:T(128)S(1)} %concatenate.9.place_ref.table_ref, bf16[28,8,512]{2,1,0:T(8,128)(2,1)S(1)} %get-tuple-element.311.refs_0_, bf16[28,8,512]{2,1,0:T(8,128)(2,1)S(1)} %get-tuple-element.312.refs_1_, f32[27,64,1024]{2,1,0:T(8,128)} %unfold.8.refs_2_), custom_call_target="tpu_custom_call", output_to_operand_aliasing={{}: (3, {})} | custom-call | flops 900000000 | tf_op jit(solution)/shard_map/unfold/pallas_call | solution.py:230
  (60 shorter events, 8.5 us)
Async XLA Ops:
  0.6 16.2 %collective-permute-start.3 = (bf16[18,256,128]{2,1,0:T(8,128)(2,1)}, bf16[18,256,128]{2,1,0:T(8,128)(2,1)S(1)}, u32[]{:S(2)}, u32[]{:S(2)}) collective-permute-start(bf16[18,256,128]{2,1,0:T(8,128)(2,1)} %bitcast.24), channel_id=1, source_target_pairs={{0,1},{1,0},{2,3},{3,2},{4,5},{5,4},{6,7},{7,6},{8,9},{9,8},{10,11... | collective-permute-start | bytes 3538952 | tf_op jit(solution)/shard_map/ppermute | solution.py:414
  1.1 33.2 %collective-permute-start.2 = (bf16[18,256,128]{2,1,0:T(8,128)(2,1)}, bf16[18,256,128]{2,1,0:T(8,128)(2,1)S(1)}, u32[]{:S(2)}, u32[]{:S(2)}) collective-permute-start(bf16[18,256,128]{2,1,0:T(8,128)(2,1)} %bitcast.25), channel_id=1, source_target_pairs={{0,2},{1,3},{2,0},{3,1},{4,6},{5,7},{6,4},{7,5},{8,10},{9,11},{10,... | collective-permute-start | bytes 3538952 | tf_op jit(solution)/shard_map/ppermute | solution.py:413
  6.0 28.4 %collective-permute-start.1 = (bf16[36,64,128]{2,1,0:T(8,128)(2,1)}, bf16[36,64,128]{2,1,0:T(8,128)(2,1)}, u32[]{:S(2)}, u32[]{:S(2)}) collective-permute-start(bf16[36,64,128]{2,1,0:T(8,128)(2,1)} %get-tuple-element.162), channel_id=1, source_target_pairs={{4,0},{8,4},{12,8},{16,12},{20,16},{24,20},{28,24},{0,28},{5,1},{9... | collective-permute-start | bytes 1769480 | tf_op jit(solution)/shard_map/ppermute | solution.py:409
  10.6 23.8 %collective-permute-start = (bf16[36,64,128]{2,1,0:T(8,128)(2,1)}, bf16[36,64,128]{2,1,0:T(8,128)(2,1)}, u32[]{:S(2)}, u32[]{:S(2)}) collective-permute-start(bf16[36,64,128]{2,1,0:T(8,128)(2,1)} %get-tuple-element.158), channel_id=1, source_target_pairs={{0,4},{4,8},{8,12},{12,16},{16,20},{20,24},{24,28},{28,0},{1,5},{5... | collective-permute-start | bytes 1769480 | tf_op jit(solution)/shard_map/ppermute | solution.py:408
  10.9 5.9 %copy-start.1 = (bf16[256,1,18,128]{3,0,2,1:T(8,128)(2,1)S(1)}, bf16[256,1,18,128]{3,0,2,1:T(8,128)(2,1)}, u32[]{:S(2)}) copy-start(bf16[256,1,18,128]{3,0,2,1:T(8,128)(2,1)} %param.3) | copy-start | bytes 3538948
  16.8 17.6 %copy-start.2 = (bf16[3,64,1,18,128]{4,1,3,2,0:T(8,128)(2,1)S(1)}, bf16[3,64,1,18,128]{4,1,3,2,0:T(8,128)(2,1)}, u32[]{:S(2)}) copy-start(bf16[3,64,1,18,128]{4,1,3,2,0:T(8,128)(2,1)} %param.4) | copy-start | bytes 2654212
  34.4 10.8 %collective-permute-start.4 = (bf16[18,256,128]{2,1,0:T(8,128)(2,1)S(1)}, bf16[18,256,128]{2,1,0:T(8,128)(2,1)S(1)}, u32[]{:S(2)}, u32[]{:S(2)}) collective-permute-start(bf16[18,256,128]{2,1,0:T(8,128)(2,1)S(1)} %collective-permute-done.2.first_ref), channel_id=1, source_target_pairs={{0,1},{1,0},{2,3},{3,2},{4,5},{5,4},{6,7},{7,6},{8,9},{9,8},{10,11... | collective-permute-start | bytes 3538952 | tf_op jit(solution)/shard_map/ppermute | solution.py:425
  42.6 7.4 %collective-permute-start.6 = (bf16[14,8,512]{2,1,0:T(8,128)(2,1)S(1)}, bf16[14,8,512]{2,1,0:T(8,128)(2,1)S(1)}, u32[]{:S(2)}, u32[]{:S(2)}) collective-permute-start(bf16[14,8,512]{2,1,0:T(8,128)(2,1)S(1)} %get-tuple-element.183), channel_id=1, source_target_pairs={{8,0},{16,8},{24,16},{28,24},{20,28},{12,20},{4,12},{0,4},{9,1},{1... | collective-permute-start | bytes 344072 | tf_op jit(solution)/shard_map/ppermute | solution.py:323
  45.1 2.0 %copy-start = (bf16[1728,1024]{0,1:T(8,128)(2,1)S(1)}, bf16[1728,1024]{0,1:T(8,128)(2,1)}, u32[]{:S(2)}) copy-start(bf16[1728,1024]{0,1:T(8,128)(2,1)} %copy.10) | copy-start | bytes 10616836
  45.1 5.4 %collective-permute-start.5 = (bf16[15,8,512]{2,1,0:T(8,128)(2,1)S(1)}, bf16[15,8,512]{2,1,0:T(8,128)(2,1)S(1)}, u32[]{:S(2)}, u32[]{:S(2)}) collective-permute-start(bf16[15,8,512]{2,1,0:T(8,128)(2,1)S(1)} %get-tuple-element.179), channel_id=1, source_target_pairs={{0,8},{8,16},{16,24},{24,28},{28,20},{20,12},{12,4},{4,0},{1,9},{9... | collective-permute-start | bytes 368648 | tf_op jit(solution)/shard_map/ppermute | solution.py:323
  51.0 10.0 %collective-permute-start.9 = (f32[18,256,128]{2,1,0:T(8,128)S(1)}, f32[18,256,128]{2,1,0:T(8,128)S(1)}, u32[]{:S(2)}, u32[]{:S(2)}) collective-permute-start(f32[18,256,128]{2,1,0:T(8,128)S(1)} %input_terms.4), channel_id=1, source_target_pairs={{0,1},{1,0},{2,3},{3,2},{4,5},{5,4},{6,7},{7,6},{8,9},{9,8},{10,11... | collective-permute-start | bytes 7077896 | tf_op jit(solution)/shard_map/ppermute | solution.py:452
  51.1 13.5 %collective-permute-start.12 = (bf16[28,8,512]{2,1,0:T(8,128)(2,1)S(1)}, bf16[28,8,512]{2,1,0:T(8,128)(2,1)S(1)}, u32[]{:S(2)}, u32[]{:S(2)}) collective-permute-start(bf16[28,8,512]{2,1,0:T(8,128)(2,1)S(1)} %get-tuple-element.193), channel_id=1, source_target_pairs={{0,8},{8,16},{16,24},{24,28},{28,20},{20,12},{12,4},{4,0},{1,9},{9... | collective-permute-start | bytes 688136 | tf_op jit(solution)/shard_map/ppermute | solution.py:323
  51.4 13.1 %collective-permute-start.13 = (bf16[28,8,512]{2,1,0:T(8,128)(2,1)S(1)}, bf16[28,8,512]{2,1,0:T(8,128)(2,1)S(1)}, u32[]{:S(2)}, u32[]{:S(2)}) collective-permute-start(bf16[28,8,512]{2,1,0:T(8,128)(2,1)S(1)} %get-tuple-element.216), channel_id=1, source_target_pairs={{8,0},{16,8},{24,16},{28,24},{20,28},{12,20},{4,12},{0,4},{9,1},{1... | collective-permute-start | bytes 688136 | tf_op jit(solution)/shard_map/ppermute | solution.py:323
  58.9 5.2 %collective-permute-start.7 = (bf16[15,8,512]{2,1,0:T(8,128)(2,1)S(1)}, bf16[15,8,512]{2,1,0:T(8,128)(2,1)S(1)}, u32[]{:S(2)}, u32[]{:S(2)}) collective-permute-start(bf16[15,8,512]{2,1,0:T(8,128)(2,1)S(1)} %get-tuple-element.201), channel_id=1, source_target_pairs={{0,8},{8,16},{16,24},{24,28},{28,20},{20,12},{12,4},{4,0},{1,9},{9... | collective-permute-start | bytes 368648 | tf_op jit(solution)/shard_map/ppermute | solution.py:323
  59.3 4.8 %collective-permute-start.8 = (bf16[14,8,512]{2,1,0:T(8,128)(2,1)S(1)}, bf16[14,8,512]{2,1,0:T(8,128)(2,1)S(1)}, u32[]{:S(2)}, u32[]{:S(2)}) collective-permute-start(bf16[14,8,512]{2,1,0:T(8,128)(2,1)S(1)} %get-tuple-element.202), channel_id=1, source_target_pairs={{8,0},{16,8},{24,16},{28,24},{20,28},{12,20},{4,12},{0,4},{9,1},{1... | collective-permute-start | bytes 344072 | tf_op jit(solution)/shard_map/ppermute | solution.py:323
  65.2 55.4 %collective-permute-start.32 = (f32[18,256,128]{2,1,0:T(8,128)S(1)}, f32[18,256,128]{2,1,0:T(8,128)S(1)}, u32[]{:S(2)}, u32[]{:S(2)}) collective-permute-start(f32[18,256,128]{2,1,0:T(8,128)S(1)} %input_terms.5), channel_id=1, source_target_pairs={{0,2},{1,3},{2,0},{3,1},{4,6},{5,7},{6,4},{7,5},{8,10},{9,11},{10,... | collective-permute-start | bytes 7077896 | tf_op jit(solution)/shard_map/ppermute | solution.py:459
  65.8 8.5 %collective-permute-start.11 = (bf16[28,8,512]{2,1,0:T(8,128)(2,1)S(1)}, bf16[28,8,512]{2,1,0:T(8,128)(2,1)S(1)}, u32[]{:S(2)}, u32[]{:S(2)}) collective-permute-start(bf16[28,8,512]{2,1,0:T(8,128)(2,1)S(1)} %get-tuple-element.215), channel_id=1, source_target_pairs={{8,0},{16,8},{24,16},{28,24},{20,28},{12,20},{4,12},{0,4},{9,1},{1... | collective-permute-start | bytes 688136 | tf_op jit(solution)/shard_map/ppermute | solution.py:323
  67.5 8.5 %collective-permute-start.10 = (bf16[28,8,512]{2,1,0:T(8,128)(2,1)S(1)}, bf16[28,8,512]{2,1,0:T(8,128)(2,1)S(1)}, u32[]{:S(2)}, u32[]{:S(2)}) collective-permute-start(bf16[28,8,512]{2,1,0:T(8,128)(2,1)S(1)} %get-tuple-element.214), channel_id=1, source_target_pairs={{0,8},{8,16},{16,24},{24,28},{28,20},{20,12},{12,4},{4,0},{1,9},{9... | collective-permute-start | bytes 688136 | tf_op jit(solution)/shard_map/ppermute | solution.py:323
  67.8 13.1 %collective-permute-start.16 = (bf16[28,8,512]{2,1,0:T(8,128)(2,1)S(1)}, bf16[28,8,512]{2,1,0:T(8,128)(2,1)S(1)}, u32[]{:S(2)}, u32[]{:S(2)}) collective-permute-start(bf16[28,8,512]{2,1,0:T(8,128)(2,1)S(1)} %get-tuple-element.223), channel_id=1, source_target_pairs={{0,8},{8,16},{16,24},{24,28},{28,20},{20,12},{12,4},{4,0},{1,9},{9... | collective-permute-start | bytes 688136 | tf_op jit(solution)/shard_map/ppermute | solution.py:323
  68.9 10.3 %collective-permute-start.17 = (bf16[28,8,512]{2,1,0:T(8,128)(2,1)S(1)}, bf16[28,8,512]{2,1,0:T(8,128)(2,1)S(1)}, u32[]{:S(2)}, u32[]{:S(2)}) collective-permute-start(bf16[28,8,512]{2,1,0:T(8,128)(2,1)S(1)} %get-tuple-element.235), channel_id=1, source_target_pairs={{8,0},{16,8},{24,16},{28,24},{20,28},{12,20},{4,12},{0,4},{9,1},{1... | collective-permute-start | bytes 688136 | tf_op jit(solution)/shard_map/ppermute | solution.py:323
  76.6 8.6 %collective-permute-start.15 = (bf16[28,8,512]{2,1,0:T(8,128)(2,1)S(1)}, bf16[28,8,512]{2,1,0:T(8,128)(2,1)S(1)}, u32[]{:S(2)}, u32[]{:S(2)}) collective-permute-start(bf16[28,8,512]{2,1,0:T(8,128)(2,1)S(1)} %get-tuple-element.234), channel_id=1, source_target_pairs={{8,0},{16,8},{24,16},{28,24},{20,28},{12,20},{4,12},{0,4},{9,1},{1... | collective-permute-start | bytes 688136 | tf_op jit(solution)/shard_map/ppermute | solution.py:323
  77.6 8.5 %collective-permute-start.14 = (bf16[28,8,512]{2,1,0:T(8,128)(2,1)S(1)}, bf16[28,8,512]{2,1,0:T(8,128)(2,1)S(1)}, u32[]{:S(2)}, u32[]{:S(2)}) collective-permute-start(bf16[28,8,512]{2,1,0:T(8,128)(2,1)S(1)} %get-tuple-element.233), channel_id=1, source_target_pairs={{0,8},{8,16},{16,24},{24,28},{28,20},{20,12},{12,4},{4,0},{1,9},{9... | collective-permute-start | bytes 688136 | tf_op jit(solution)/shard_map/ppermute | solution.py:323
  81.6 10.1 %collective-permute-start.21 = (bf16[28,8,512]{2,1,0:T(8,128)(2,1)S(1)}, bf16[28,8,512]{2,1,0:T(8,128)(2,1)S(1)}, u32[]{:S(2)}, u32[]{:S(2)}) collective-permute-start(bf16[28,8,512]{2,1,0:T(8,128)(2,1)S(1)} %get-tuple-element.254), channel_id=1, source_target_pairs={{8,0},{16,8},{24,16},{28,24},{20,28},{12,20},{4,12},{0,4},{9,1},{1... | collective-permute-start | bytes 688136 | tf_op jit(solution)/shard_map/ppermute | solution.py:323
  82.5 9.2 %collective-permute-start.20 = (bf16[28,8,512]{2,1,0:T(8,128)(2,1)S(1)}, bf16[28,8,512]{2,1,0:T(8,128)(2,1)S(1)}, u32[]{:S(2)}, u32[]{:S(2)}) collective-permute-start(bf16[28,8,512]{2,1,0:T(8,128)(2,1)S(1)} %get-tuple-element.242), channel_id=1, source_target_pairs={{0,8},{8,16},{16,24},{24,28},{28,20},{20,12},{12,4},{4,0},{1,9},{9... | collective-permute-start | bytes 688136 | tf_op jit(solution)/shard_map/ppermute | solution.py:323
  86.8 8.6 %collective-permute-start.19 = (bf16[28,8,512]{2,1,0:T(8,128)(2,1)S(1)}, bf16[28,8,512]{2,1,0:T(8,128)(2,1)S(1)}, u32[]{:S(2)}, u32[]{:S(2)}) collective-permute-start(bf16[28,8,512]{2,1,0:T(8,128)(2,1)S(1)} %get-tuple-element.253), channel_id=1, source_target_pairs={{8,0},{16,8},{24,16},{28,24},{20,28},{12,20},{4,12},{0,4},{9,1},{1... | collective-permute-start | bytes 688136 | tf_op jit(solution)/shard_map/ppermute | solution.py:323
  87.6 8.6 %collective-permute-start.18 = (bf16[28,8,512]{2,1,0:T(8,128)(2,1)S(1)}, bf16[28,8,512]{2,1,0:T(8,128)(2,1)S(1)}, u32[]{:S(2)}, u32[]{:S(2)}) collective-permute-start(bf16[28,8,512]{2,1,0:T(8,128)(2,1)S(1)} %get-tuple-element.249), channel_id=1, source_target_pairs={{0,8},{8,16},{16,24},{24,28},{28,20},{20,12},{12,4},{4,0},{1,9},{9... | collective-permute-start | bytes 688136 | tf_op jit(solution)/shard_map/ppermute | solution.py:323
  92.2 8.6 %collective-permute-start.25 = (bf16[28,8,512]{2,1,0:T(8,128)(2,1)S(1)}, bf16[28,8,512]{2,1,0:T(8,128)(2,1)S(1)}, u32[]{:S(2)}, u32[]{:S(2)}) collective-permute-start(bf16[28,8,512]{2,1,0:T(8,128)(2,1)S(1)} %last_hop.2.refs_0_), channel_id=1, source_target_pairs={{8,0},{16,8},{24,16},{28,24},{20,28},{12,20},{4,12},{0,4},{9,1},{1... | collective-permute-start | bytes 688136 | tf_op jit(solution)/shard_map/ppermute | solution.py:323
  93.1 8.5 %collective-permute-start.24 = (bf16[28,8,512]{2,1,0:T(8,128)(2,1)S(1)}, bf16[28,8,512]{2,1,0:T(8,128)(2,1)S(1)}, u32[]{:S(2)}, u32[]{:S(2)}) collective-permute-start(bf16[28,8,512]{2,1,0:T(8,128)(2,1)S(1)} %last_hop.2.refs_0_), channel_id=1, source_target_pairs={{0,8},{8,16},{16,24},{24,28},{28,20},{20,12},{12,4},{4,0},{1,9},{9... | collective-permute-start | bytes 688136 | tf_op jit(solution)/shard_map/ppermute | solution.py:323
  96.7 9.0 %collective-permute-start.23 = (bf16[28,8,512]{2,1,0:T(8,128)(2,1)S(1)}, bf16[28,8,512]{2,1,0:T(8,128)(2,1)S(1)}, u32[]{:S(2)}, u32[]{:S(2)}) collective-permute-start(bf16[28,8,512]{2,1,0:T(8,128)(2,1)S(1)} %last_hop.3.refs_0_), channel_id=1, source_target_pairs={{8,0},{16,8},{24,16},{28,24},{20,28},{12,20},{4,12},{0,4},{9,1},{1... | collective-permute-start | bytes 688136 | tf_op jit(solution)/shard_map/ppermute | solution.py:323
  98.1 8.5 %collective-permute-start.22 = (bf16[28,8,512]{2,1,0:T(8,128)(2,1)S(1)}, bf16[28,8,512]{2,1,0:T(8,128)(2,1)S(1)}, u32[]{:S(2)}, u32[]{:S(2)}) collective-permute-start(bf16[28,8,512]{2,1,0:T(8,128)(2,1)S(1)} %last_hop.3.refs_0_), channel_id=1, source_target_pairs={{0,8},{8,16},{16,24},{24,28},{28,20},{20,12},{12,4},{4,0},{1,9},{9... | collective-permute-start | bytes 688136 | tf_op jit(solution)/shard_map/ppermute | solution.py:323
  101.6 9.9 %collective-permute-start.28 = (bf16[28,8,512]{2,1,0:T(8,128)(2,1)S(1)}, bf16[28,8,512]{2,1,0:T(8,128)(2,1)S(1)}, u32[]{:S(2)}, u32[]{:S(2)}) collective-permute-start(bf16[28,8,512]{2,1,0:T(8,128)(2,1)S(1)} %collective-permute-done.24.refs_1_), channel_id=1, source_target_pairs={{0,8},{8,16},{16,24},{24,28},{28,20},{20,12},{12,4},{4,0},{1,9},{9... | collective-permute-start | bytes 688136 | tf_op jit(solution)/shard_map/ppermute | solution.py:323
  102.8 8.7 %collective-permute-start.29 = (bf16[28,8,512]{2,1,0:T(8,128)(2,1)S(1)}, bf16[28,8,512]{2,1,0:T(8,128)(2,1)S(1)}, u32[]{:S(2)}, u32[]{:S(2)}) collective-permute-start(bf16[28,8,512]{2,1,0:T(8,128)(2,1)S(1)} %collective-permute-done.25.refs_2_), channel_id=1, source_target_pairs={{8,0},{16,8},{24,16},{28,24},{20,28},{12,20},{4,12},{0,4},{9,1},{1... | collective-permute-start | bytes 688136 | tf_op jit(solution)/shard_map/ppermute | solution.py:323
  106.6 9.8 %collective-permute-start.26 = (bf16[28,8,512]{2,1,0:T(8,128)(2,1)S(1)}, bf16[28,8,512]{2,1,0:T(8,128)(2,1)S(1)}, u32[]{:S(2)}, u32[]{:S(2)}) collective-permute-start(bf16[28,8,512]{2,1,0:T(8,128)(2,1)S(1)} %collective-permute-done.22.refs_1_), channel_id=1, source_target_pairs={{0,8},{8,16},{16,24},{24,28},{28,20},{20,12},{12,4},{4,0},{1,9},{9... | collective-permute-start | bytes 688136 | tf_op jit(solution)/shard_map/ppermute | solution.py:323
  107.7 8.7 %collective-permute-start.27 = (bf16[28,8,512]{2,1,0:T(8,128)(2,1)S(1)}, bf16[28,8,512]{2,1,0:T(8,128)(2,1)S(1)}, u32[]{:S(2)}, u32[]{:S(2)}) collective-permute-start(bf16[28,8,512]{2,1,0:T(8,128)(2,1)S(1)} %collective-permute-done.23.refs_2_), channel_id=1, source_target_pairs={{8,0},{16,8},{24,16},{28,24},{20,28},{12,20},{4,12},{0,4},{9,1},{1... | collective-permute-start | bytes 688136 | tf_op jit(solution)/shard_map/ppermute | solution.py:323
  111.5 9.0 %collective-permute-start.34 = (bf16[28,8,512]{2,1,0:T(8,128)(2,1)S(1)}, bf16[28,8,512]{2,1,0:T(8,128)(2,1)S(1)}, u32[]{:S(2)}, u32[]{:S(2)}) collective-permute-start(bf16[28,8,512]{2,1,0:T(8,128)(2,1)S(1)} %collective-permute-done.29.refs_1_), channel_id=1, source_target_pairs={{8,0},{16,8},{24,16},{28,24},{20,28},{12,20},{4,12},{0,4},{9,1},{1... | collective-permute-start | bytes 688136 | tf_op jit(solution)/shard_map/ppermute | solution.py:323
  113.4 7.2 %collective-permute-start.33 = (bf16[28,8,512]{2,1,0:T(8,128)(2,1)S(1)}, bf16[28,8,512]{2,1,0:T(8,128)(2,1)S(1)}, u32[]{:S(2)}, u32[]{:S(2)}) collective-permute-start(bf16[28,8,512]{2,1,0:T(8,128)(2,1)S(1)} %collective-permute-done.28.refs_0_), channel_id=1, source_target_pairs={{0,8},{8,16},{16,24},{24,28},{28,20},{20,12},{12,4},{4,0},{1,9},{9... | collective-permute-start | bytes 688136 | tf_op jit(solution)/shard_map/ppermute | solution.py:323
  116.5 6.0 %collective-permute-start.30 = (bf16[28,8,512]{2,1,0:T(8,128)(2,1)S(1)}, bf16[28,8,512]{2,1,0:T(8,128)(2,1)S(1)}, u32[]{:S(2)}, u32[]{:S(2)}) collective-permute-start(bf16[28,8,512]{2,1,0:T(8,128)(2,1)S(1)} %collective-permute-done.26.refs_2_), channel_id=1, source_target_pairs={{0,8},{8,16},{16,24},{24,28},{28,20},{20,12},{12,4},{4,0},{1,9},{9... | collective-permute-start | bytes 688136 | tf_op jit(solution)/shard_map/ppermute | solution.py:323
  117.6 6.0 %collective-permute-start.31 = (bf16[28,8,512]{2,1,0:T(8,128)(2,1)S(1)}, bf16[28,8,512]{2,1,0:T(8,128)(2,1)S(1)}, u32[]{:S(2)}, u32[]{:S(2)}) collective-permute-start(bf16[28,8,512]{2,1,0:T(8,128)(2,1)S(1)} %collective-permute-done.27.refs_3_), channel_id=1, source_target_pairs={{8,0},{16,8},{24,16},{28,24},{20,28},{12,20},{4,12},{0,4},{9,1},{1... | collective-permute-start | bytes 688136 | tf_op jit(solution)/shard_map/ppermute | solution.py:323
  123.6 6.3 %collective-permute-start.35 = (f32[18,256,128]{2,1,0:T(8,128)S(1)}, f32[18,256,128]{2,1,0:T(8,128)S(1)}, u32[]{:S(2)}, u32[]{:S(2)}) collective-permute-start(f32[18,256,128]{2,1,0:T(8,128)S(1)} %input_terms.6), channel_id=1, source_target_pairs={{0,1},{1,0},{2,3},{3,2},{4,5},{5,4},{6,7},{7,6},{8,9},{9,8},{10,11... | collective-permute-start | bytes 7077896 | tf_op jit(solution)/shard_map/ppermute | solution.py:490
  123.6 8.6 %collective-permute-start.36 = (bf16[14,8,512]{2,1,0:T(8,128)(2,1)S(1)}, bf16[14,8,512]{2,1,0:T(8,128)(2,1)S(1)}, u32[]{:S(2)}, u32[]{:S(2)}) collective-permute-start(bf16[14,8,512]{2,1,0:T(8,128)(2,1)S(1)} %slice.12), channel_id=1, source_target_pairs={{0,8},{8,16},{16,24},{24,28},{28,20},{20,12},{12,4},{4,0},{1,9},{9... | collective-permute-start | bytes 344072 | tf_op jit(solution)/shard_map/ppermute | solution.py:323
  124.5 7.7 %collective-permute-start.37 = (bf16[14,8,512]{2,1,0:T(8,128)(2,1)S(1)}, bf16[14,8,512]{2,1,0:T(8,128)(2,1)S(1)}, u32[]{:S(2)}, u32[]{:S(2)}) collective-permute-start(bf16[14,8,512]{2,1,0:T(8,128)(2,1)S(1)} %slice.13), channel_id=1, source_target_pairs={{8,0},{16,8},{24,16},{28,24},{20,28},{12,20},{4,12},{0,4},{9,1},{1... | collective-permute-start | bytes 344072 | tf_op jit(solution)/shard_map/ppermute | solution.py:323
  125.7 6.0 %collective-permute-start.38 = (bf16[14,8,512]{2,1,0:T(8,128)(2,1)S(1)}, bf16[14,8,512]{2,1,0:T(8,128)(2,1)S(1)}, u32[]{:S(2)}, u32[]{:S(2)}) collective-permute-start(bf16[14,8,512]{2,1,0:T(8,128)(2,1)S(1)} %slice.14), channel_id=1, source_target_pairs={{0,8},{8,16},{16,24},{24,28},{28,20},{20,12},{12,4},{4,0},{1,9},{9... | collective-permute-start | bytes 344072 | tf_op jit(solution)/shard_map/ppermute | solution.py:323
  126.6 5.6 %collective-permute-start.39 = (bf16[14,8,512]{2,1,0:T(8,128)(2,1)S(1)}, bf16[14,8,512]{2,1,0:T(8,128)(2,1)S(1)}, u32[]{:S(2)}, u32[]{:S(2)}) collective-permute-start(bf16[14,8,512]{2,1,0:T(8,128)(2,1)S(1)} %slice.15), channel_id=1, source_target_pairs={{8,0},{16,8},{24,16},{28,24},{20,28},{12,20},{4,12},{0,4},{9,1},{1... | collective-permute-start | bytes 344072 | tf_op jit(solution)/shard_map/ppermute | solution.py:323

commit v3 on v2

--- a/solution.py
+++ b/solution.py
@@ -93,7 +93,8 @@
     )(in_hbm(cot))
 
 
-def spread_kernel(cot_ref, left_ref, right_ref, out_ref):
+def spread_kernel(cot_ref, left_ref, right_ref, weight_ref, out_ref):
+    del weight_ref
     cols, chans, rows = cot_ref.shape[1:]
     lane = lax.broadcasted_iota(jnp.int32, (chans, rows), 1)
     start = 0
@@ -123,10 +124,10 @@
         start += dilation
 
 
-def spread(cot, left, right):
+def spread(cot, left, right, weight_rows):
     branches, cols, chans, rows = cot.shape
     shape = jax.ShapeDtypeStruct((branches * TAPS * chans, cols * rows), jnp.bfloat16)
-    return direct(spread_kernel, [shape], [cot, left, right], "spread")[0]
+    return direct(spread_kernel, [shape], [cot, left, right, weight_rows], "spread")[0]
 
 
 def flatten_kernel(place_ref, first_ref, second_ref, out_ref):
@@ -410,6 +411,7 @@
 
     to_core = [(i, i ^ 1) for i in range(4)]
     to_x = [(i, i ^ 2) for i in range(4)]
+    feat = order.gate(feat)[0]
     far = lax.ppermute(feat, "ch", to_x)
     near = lax.ppermute(feat, "ch", to_core)
 
@@ -421,7 +423,7 @@
     weight_rows = order(jnp.transpose, weights.reshape(-1, total))
     flat_near = order(flatten, table, feat, near)
     left, right, far = order.gate(left, right, far)
-    grid = order(spread, cot, left, right)
+    grid = order(spread, cot, left, right, weight_rows)
     far_near = lax.ppermute(far, "ch", to_core)
 
     def terms_of(which, spans, *added):

time: 134 us -> 134 us (level)
    ppermute x16, starting transfers between devices: 20.6 us -> 17.1 us  [send(): lax.ppermute(down, 'lon', self.behind)]
    ppermute x16, starting transfers between devices: 12.7 us -> 15.9 us  [send(): lax.ppermute(up, 'lon', self.ahead)]
    ppermute x1, starting transfers between devices: 0.01 us -> 1.52 us  [local(): lax.ppermute(tails, 'lon', [(i, (i + 1) % count) for i in range(count)])]
    ppermute x1, starting transfers between devices: 4.56 us -> 3.2 us  [local(): lax.ppermute(heads, 'lon', [((i + 1) % count, i) for i in range(count)])]
  transfers between devices with their start and end apart: 40 -> 40, of which waited for: 21 -> 19; matrix products, arithmetic and copies ran while one was open for 6% -> 6% of each run, Pallas kernels for 31% -> 29%
where the time goes in v3:
time: 134 us
  Pallas kernels  43.8 us (33%)
  starting transfers between devices  41.3 us (31%)
  waiting for transfers between devices  40 us (30%)
  local copies, waits for them, and re-layouts  6.09 us (5%)
  other arithmetic  1.69 us (1%)
    pallas_call x19, Pallas kernels, direct(): pl.pallas_call(kernel, in_specs=([] if table is None else [smem]) + [vmem...  32 us
    ppermute x1, waiting for transfers between devices, local(): lax.ppermute(heads, 'lon', [((i + 1) % count, i) for i in range(count)])  17.5 us
    ppermute x16, starting transfers between devices, send(): lax.ppermute(down, 'lon', self.behind)  17.1 us
    ppermute x16, starting transfers between devices, send(): lax.ppermute(up, 'lon', self.ahead)  15.9 us
    ppermute x16, waiting for transfers between devices, send(): lax.ppermute(up, 'lon', self.ahead)  12.6 us
    ppermute x16, waiting for transfers between devices, send(): lax.ppermute(down, 'lon', self.behind)  9.84 us
    pallas_call x5, Pallas kernels, unfold(): pl.pallas_call(functools.partial(unfold_kernel, norm, places), in_specs=[...  9.48 us
    optimization_barrier x1, local copies, waits for them, and re-layouts, gate(): return lax.optimization_barrier(values + self.last)[:len(values)]  5.87 us
  transfers between devices with their start and end apart: 40, of which 19 were waited for; matrix products, arithmetic and copies ran while one was open for 6% of the time, Pallas kernels for 29%

profile of v3, /device:TPU:0, one launch (start us, length us, event | category | flops | bytes accessed | tf_op | source)
XLA Modules:
  0.0 134.0 jit_solution(7508278183157614196)
XLA Ops:
  0.6 2.3 %edges.1 = (bf16[36,64,128]{2,1,0:T(8,128)(2,1)}, bf16[36,64,128]{2,1,0:T(8,128)(2,1)}) custom-call(bf16[3,18,64,128]{3,2,1,0:T(8,128)(2,1)} %bitcast.28), custom_call_target="tpu_custom_call" | custom-call | flops 300000000 | tf_op jit(solution)/shard_map/edges/pallas_call | solution.py:84
  3.4 2.5 %collective-permute-start.2 = (bf16[18,256,128]{2,1,0:T(8,128)(2,1)}, bf16[18,256,128]{2,1,0:T(8,128)(2,1)S(1)}, u32[]{:S(2)}, u32[]{:S(2)}) collective-permute-start(bf16[18,256,128]{2,1,0:T(8,128)(2,1)} %bitcast.26), channel_id=1, source_target_pairs={{0,2},{1,3},{2,0},{3,1},{4,6},{5,7},{6,4},{7,5},{8,10},{9,11},{10,... | collective-permute-start | bytes 3538952 | tf_op jit(solution)/shard_map/ppermute | solution.py:415
  5.9 1.5 %collective-permute-start = (bf16[36,64,128]{2,1,0:T(8,128)(2,1)}, bf16[36,64,128]{2,1,0:T(8,128)(2,1)}, u32[]{:S(2)}, u32[]{:S(2)}) collective-permute-start(bf16[36,64,128]{2,1,0:T(8,128)(2,1)} %get-tuple-element.160), channel_id=1, source_target_pairs={{0,4},{4,8},{8,12},{12,16},{16,20},{20,24},{24,28},{28,0},{1,5},{5... | collective-permute-start | bytes 1769480 | tf_op jit(solution)/shard_map/ppermute | solution.py:409
  7.4 3.2 %collective-permute-start.1 = (bf16[36,64,128]{2,1,0:T(8,128)(2,1)}, bf16[36,64,128]{2,1,0:T(8,128)(2,1)}, u32[]{:S(2)}, u32[]{:S(2)}) collective-permute-start(bf16[36,64,128]{2,1,0:T(8,128)(2,1)} %get-tuple-element.164), channel_id=1, source_target_pairs={{4,0},{8,4},{12,8},{16,12},{20,16},{24,20},{28,24},{0,28},{5,1},{9... | collective-permute-start | bytes 1769480 | tf_op jit(solution)/shard_map/ppermute | solution.py:410
  11.0 5.9 %copy.10 = bf16[1728,1024]{0,1:T(8,128)(2,1)} copy(bf16[1728,1024]{1,0:T(8,128)(2,1)} %bitcast.31) | data formatting | bytes 7077888 | tf_op jit(solution)/shard_map/optimization_barrier | solution.py:301
  16.9 1.2 flatten.2.feat_ref
  18.1 17.5 %collective-permute-done.1.right_ref = bf16[36,64,128]{2,1,0:T(8,128)(2,1)} collective-permute-done((bf16[36,64,128]{2,1,0:T(8,128)(2,1)}, bf16[36,64,128]{2,1,0:T(8,128)(2,1)}, u32[]{:S(2)}, u32[]{:S(2)}) %collective-permute-start.1) | collective-permute-done | bytes 589856 | tf_op jit(solution)/shard_map/ppermute | solution.py:410
  35.6 2.5 %spread.1.grid_ref = bf16[1728,2304]{1,0:T(8,128)(2,1)S(1)} custom-call(bf16[3,18,64,128]{3,2,1,0:T(8,128)(2,1)S(1)} %bitcast.29, bf16[36,64,128]{2,1,0:T(8,128)(2,1)} %collective-permute-done.left_ref, bf16[36,64,128]{2,1,0:T(8,128)(2,1)} %collective-permute-done.1.right_ref, bf16[1024,1728]{1,0:T(8,128)(2,1)S(1)} %bitcast.20), custom_call_target="tpu_custom_call" | custom-call | flops 600000000 | tf_op jit(solution)/shard_map/spread/pallas_call | solution.py:61
  38.1 5.6 %kernel_terms.2 = (f32[8,27,8,512]{3,2,1,0:T(8,128)S(1)}, f32[1,8,512]{2,1,0:T(8,128)S(1)}) custom-call(s32[30]{0:T(128)S(1)} %concatenate.9.place_ref.table_ref, bf16[1728,2304]{1,0:T(8,128)(2,1)S(1)} %spread.1.grid_ref, bf16[2304,512]{1,0:T(8,128)(2,1)S(1)} %flatten.2.feat_ref), custom_call_target="tpu_custom_call" | custom-call | flops 1800000000 | tf_op jit(solution)/shard_map/kernel_terms/pallas_call | solution.py:61
  44.1 1.8 %collective-permute-start.5 = (bf16[15,8,512]{2,1,0:T(8,128)(2,1)S(1)}, bf16[15,8,512]{2,1,0:T(8,128)(2,1)S(1)}, u32[]{:S(2)}, u32[]{:S(2)}) collective-permute-start(bf16[15,8,512]{2,1,0:T(8,128)(2,1)S(1)} %get-tuple-element.183), channel_id=1, source_target_pairs={{0,8},{8,16},{16,24},{24,28},{28,20},{20,12},{12,4},{4,0},{1,9},{9... | collective-permute-start | bytes 368648 | tf_op jit(solution)/shard_map/ppermute | solution.py:324
  45.9 1.2 flatten.3.feat_ref
  47.1 2.8 %input_terms.4 = f32[18,256,128]{2,1,0:T(8,128)S(1)} custom-call(s32[30]{0:T(128)S(1)} %concatenate.9.place_ref.table_ref, bf16[1024,1728]{1,0:T(8,128)(2,1)S(1)} %bitcast.21, bf16[1728,2304]{1,0:T(8,128)(2,1)S(1)} %spread.1.grid_ref), custom_call_target="tpu_custom_call" | custom-call | flops 1050000000 | tf_op jit(solution)/shard_map/input_terms/pallas_call | solution.py:61
  50.5 1.4 %collective-permute-start.12 = (bf16[28,8,512]{2,1,0:T(8,128)(2,1)S(1)}, bf16[28,8,512]{2,1,0:T(8,128)(2,1)S(1)}, u32[]{:S(2)}, u32[]{:S(2)}) collective-permute-start(bf16[28,8,512]{2,1,0:T(8,128)(2,1)S(1)} %get-tuple-element.197), channel_id=1, source_target_pairs={{0,8},{8,16},{16,24},{24,28},{28,20},{20,12},{12,4},{4,0},{1,9},{9... | collective-permute-start | bytes 688136 | tf_op jit(solution)/shard_map/ppermute | solution.py:324
  51.9 0.7 collective-permute-start.13
  52.6 5.6 %kernel_terms.3 = (f32[8,27,8,512]{3,2,1,0:T(8,128)S(1)}, f32[1,8,512]{2,1,0:T(8,128)S(1)}) custom-call(s32[30]{0:T(128)S(1)} %concatenate.9.place_ref.table_ref, bf16[1728,2304]{1,0:T(8,128)(2,1)S(1)} %spread.1.grid_ref, bf16[2304,512]{1,0:T(8,128)(2,1)S(1)} %flatten.3.feat_ref), custom_call_target="tpu_custom_call" | custom-call | flops 1800000000 | tf_op jit(solution)/shard_map/kernel_terms/pallas_call | solution.py:61
  58.3 1.4 %collective-permute-start.7 = (bf16[15,8,512]{2,1,0:T(8,128)(2,1)S(1)}, bf16[15,8,512]{2,1,0:T(8,128)(2,1)S(1)}, u32[]{:S(2)}, u32[]{:S(2)}) collective-permute-start(bf16[15,8,512]{2,1,0:T(8,128)(2,1)S(1)} %get-tuple-element.205), channel_id=1, source_target_pairs={{0,8},{8,16},{16,24},{24,28},{28,20},{20,12},{12,4},{4,0},{1,9},{9... | collective-permute-start | bytes 368648 | tf_op jit(solution)/shard_map/ppermute | solution.py:324
  59.7 0.7 collective-permute-start.8
  60.4 2.8 %input_terms.5 = f32[18,256,128]{2,1,0:T(8,128)S(1)} custom-call(s32[30]{0:T(128)S(1)} %concatenate.9.place_ref.table_ref, bf16[1024,1728]{1,0:T(8,128)(2,1)S(1)} %bitcast.22, bf16[1728,2304]{1,0:T(8,128)(2,1)S(1)} %spread.1.grid_ref, f32[18,256,128]{2,1,0:T(8,128)S(1)} %collective-permute-done.9.refs_0_), custom_call_target="tpu_custom_call" | custom-call | flops 1050000000 | tf_op jit(solution)/shard_map/input_terms/pallas_call | solution.py:61
  63.3 1.3 collective-permute-done.8.down_ref
  65.0 0.6 next_hop.8
  66.2 0.7 collective-permute-start.11
  66.9 1.4 %collective-permute-start.10 = (bf16[28,8,512]{2,1,0:T(8,128)(2,1)S(1)}, bf16[28,8,512]{2,1,0:T(8,128)(2,1)S(1)}, u32[]{:S(2)}, u32[]{:S(2)}) collective-permute-start(bf16[28,8,512]{2,1,0:T(8,128)(2,1)S(1)} %get-tuple-element.218), channel_id=1, source_target_pairs={{0,8},{8,16},{16,24},{24,28},{28,20},{20,12},{12,4},{4,0},{1,9},{9... | collective-permute-start | bytes 688136 | tf_op jit(solution)/shard_map/ppermute | solution.py:324
  68.3 1.5 %collective-permute-start.16 = (bf16[28,8,512]{2,1,0:T(8,128)(2,1)S(1)}, bf16[28,8,512]{2,1,0:T(8,128)(2,1)S(1)}, u32[]{:S(2)}, u32[]{:S(2)}) collective-permute-start(bf16[28,8,512]{2,1,0:T(8,128)(2,1)S(1)} %get-tuple-element.227), channel_id=1, source_target_pairs={{0,8},{8,16},{16,24},{24,28},{28,20},{20,12},{12,4},{4,0},{1,9},{9... | collective-permute-start | bytes 688136 | tf_op jit(solution)/shard_map/ppermute | solution.py:324
  70.3 2.8 %input_terms.6 = f32[18,256,128]{2,1,0:T(8,128)S(1)} custom-call(s32[30]{0:T(128)S(1)} %concatenate.9.place_ref.table_ref, bf16[1024,1728]{1,0:T(8,128)(2,1)S(1)} %bitcast.23, bf16[1728,2304]{1,0:T(8,128)(2,1)S(1)} %spread.1.grid_ref), custom_call_target="tpu_custom_call" | custom-call | flops 1050000000 | tf_op jit(solution)/shard_map/input_terms/pallas_call | solution.py:61
  73.1 1.4 %collective-permute-done.11.down_ref = bf16[28,8,512]{2,1,0:T(8,128)(2,1)S(1)} collective-permute-done((bf16[28,8,512]{2,1,0:T(8,128)(2,1)S(1)}, bf16[28,8,512]{2,1,0:T(8,128)(2,1)S(1)}, u32[]{:S(2)}, u32[]{:S(2)}) %collective-permute-start.11) | collective-permute-done | bytes 229408 | tf_op jit(solution)/shard_map/ppermute | solution.py:324
  74.6 0.9 collective-permute-done.10.up_ref
  76.1 1.2 collective-permute-start.15
  77.3 0.8 collective-permute-start.14
  78.1 1.3 %collective-permute-done.17.down_ref = bf16[28,8,512]{2,1,0:T(8,128)(2,1)S(1)} collective-permute-done((bf16[28,8,512]{2,1,0:T(8,128)(2,1)S(1)}, bf16[28,8,512]{2,1,0:T(8,128)(2,1)S(1)}, u32[]{:S(2)}, u32[]{:S(2)}) %collective-permute-start.17) | collective-permute-done | bytes 229408 | tf_op jit(solution)/shard_map/ppermute | solution.py:324
  79.5 0.9 collective-permute-done.16.up_ref
  81.0 1.2 collective-permute-start.21
  82.2 0.8 collective-permute-start.20
  83.1 1.6 %collective-permute-done.15.down_ref = bf16[28,8,512]{2,1,0:T(8,128)(2,1)S(1)} collective-permute-done((bf16[28,8,512]{2,1,0:T(8,128)(2,1)S(1)}, bf16[28,8,512]{2,1,0:T(8,128)(2,1)S(1)}, u32[]{:S(2)}, u32[]{:S(2)}) %collective-permute-start.15) | collective-permute-done | bytes 229408 | tf_op jit(solution)/shard_map/ppermute | solution.py:324
  84.7 0.7 collective-permute-done.14.up_ref
  86.0 1.3 collective-permute-start.19
  87.3 0.8 collective-permute-start.18
  88.1 2.8 %input_terms.7 = f32[18,256,128]{2,1,0:T(8,128)S(1)} custom-call(s32[30]{0:T(128)S(1)} %concatenate.9.place_ref.table_ref, bf16[1024,1728]{1,0:T(8,128)(2,1)S(1)} %bitcast.24, bf16[1728,2304]{1,0:T(8,128)(2,1)S(1)} %spread.1.grid_ref), custom_call_target="tpu_custom_call" | custom-call | flops 1050000000 | tf_op jit(solution)/shard_map/input_terms/pallas_call | solution.py:61
  91.4 1.3 collective-permute-start.25
  92.8 0.8 collective-permute-start.24
  93.5 1.1 collective-permute-done.19.down_ref
  94.6 1.3 collective-permute-done.18.up_ref
  96.3 1.8 %collective-permute-start.23 = (bf16[28,8,512]{2,1,0:T(8,128)(2,1)S(1)}, bf16[28,8,512]{2,1,0:T(8,128)(2,1)S(1)}, u32[]{:S(2)}, u32[]{:S(2)}) collective-permute-start(bf16[28,8,512]{2,1,0:T(8,128)(2,1)S(1)} %last_hop.3.refs_0_), channel_id=1, source_target_pairs={{8,0},{16,8},{24,16},{28,24},{20,28},{12,20},{4,12},{0,4},{9,1},{1... | collective-permute-start | bytes 688136 | tf_op jit(solution)/shard_map/ppermute | solution.py:324
  98.4 1.6 %collective-permute-done.25.refs_2_ = bf16[28,8,512]{2,1,0:T(8,128)(2,1)S(1)} collective-permute-done((bf16[28,8,512]{2,1,0:T(8,128)(2,1)S(1)}, bf16[28,8,512]{2,1,0:T(8,128)(2,1)S(1)}, u32[]{:S(2)}, u32[]{:S(2)}) %collective-permute-start.25) | collective-permute-done | bytes 229408 | tf_op jit(solution)/shard_map/ppermute | solution.py:324
  100.0 1.3 collective-permute-done.24.refs_1_
  101.3 0.8 collective-permute-start.28
  102.1 1.3 collective-permute-start.29
  103.3 1.9 %unfold.5.refs_3_ = f32[27,64,1024]{2,1,0:T(8,128)} custom-call(s32[30]{0:T(128)S(1)} %concatenate.9.place_ref.table_ref, bf16[28,8,512]{2,1,0:T(8,128)(2,1)S(1)} %last_hop.2.refs_0_, bf16[28,8,512]{2,1,0:T(8,128)(2,1)S(1)} %collective-permute-done.24.refs_1_, bf16[28,8,512]{2,1,0:T(8,128)(2,1)S(1)} %collective-permute-done.25.refs_2_), custom_call_target="tpu_custom_call" | custom-call | flops 900000000 | tf_op jit(solution)/shard_map/unfold/pallas_call | solution.py:231
  105.2 1.4 %collective-permute-done.22.refs_1_ = bf16[28,8,512]{2,1,0:T(8,128)(2,1)S(1)} collective-permute-done((bf16[28,8,512]{2,1,0:T(8,128)(2,1)S(1)}, bf16[28,8,512]{2,1,0:T(8,128)(2,1)S(1)}, u32[]{:S(2)}, u32[]{:S(2)}) %collective-permute-start.22) | collective-permute-done | bytes 229408 | tf_op jit(solution)/shard_map/ppermute | solution.py:324
  107.0 1.7 %collective-permute-start.27 = (bf16[28,8,512]{2,1,0:T(8,128)(2,1)S(1)}, bf16[28,8,512]{2,1,0:T(8,128)(2,1)S(1)}, u32[]{:S(2)}, u32[]{:S(2)}) collective-permute-start(bf16[28,8,512]{2,1,0:T(8,128)(2,1)S(1)} %collective-permute-done.23.refs_2_), channel_id=1, source_target_pairs={{8,0},{16,8},{24,16},{28,24},{20,28},{12,20},{4,12},{0,4},{9,1},{1... | collective-permute-start | bytes 688136 | tf_op jit(solution)/shard_map/ppermute | solution.py:324
  108.7 1.9 %unfold.6.refs_4_ = f32[27,64,1024]{2,1,0:T(8,128)} custom-call(s32[30]{0:T(128)S(1)} %concatenate.9.place_ref.table_ref, bf16[28,8,512]{2,1,0:T(8,128)(2,1)S(1)} %last_hop.3.refs_0_, bf16[28,8,512]{2,1,0:T(8,128)(2,1)S(1)} %collective-permute-done.22.refs_1_, ...), custom_call_target="tpu_custom_call", output_to_operand_aliasing={{}: (4, {})} | custom-call | flops 900000000 | tf_op jit(solution)/shard_map/unfold/pallas_call | solution.py:231
  110.5 1.0 collective-permute-done.28.refs_0_
  111.6 1.5 %collective-permute-start.34 = (bf16[28,8,512]{2,1,0:T(8,128)(2,1)S(1)}, bf16[28,8,512]{2,1,0:T(8,128)(2,1)S(1)}, u32[]{:S(2)}, u32[]{:S(2)}) collective-permute-start(bf16[28,8,512]{2,1,0:T(8,128)(2,1)S(1)} %collective-permute-done.29.refs_1_), channel_id=1, source_target_pairs={{8,0},{16,8},{24,16},{28,24},{20,28},{12,20},{4,12},{0,4},{9,1},{1... | collective-permute-start | bytes 688136 | tf_op jit(solution)/shard_map/ppermute | solution.py:324
  113.6 2.9 %collective-permute-done.26.refs_2_ = bf16[28,8,512]{2,1,0:T(8,128)(2,1)S(1)} collective-permute-done((bf16[28,8,512]{2,1,0:T(8,128)(2,1)S(1)}, bf16[28,8,512]{2,1,0:T(8,128)(2,1)S(1)}, u32[]{:S(2)}, u32[]{:S(2)}) %collective-permute-start.26) | collective-permute-done | bytes 229408 | tf_op jit(solution)/shard_map/ppermute | solution.py:324
  116.8 1.7 %collective-permute-start.31 = (bf16[28,8,512]{2,1,0:T(8,128)(2,1)S(1)}, bf16[28,8,512]{2,1,0:T(8,128)(2,1)S(1)}, u32[]{:S(2)}, u32[]{:S(2)}) collective-permute-start(bf16[28,8,512]{2,1,0:T(8,128)(2,1)S(1)} %collective-permute-done.27.refs_3_), channel_id=1, source_target_pairs={{8,0},{16,8},{24,16},{28,24},{20,28},{12,20},{4,12},{0,4},{9,1},{1... | collective-permute-start | bytes 688136 | tf_op jit(solution)/shard_map/ppermute | solution.py:324
  118.5 2.0 %unfold.7.refs_4_ = f32[27,64,1024]{2,1,0:T(8,128)} custom-call(s32[30]{0:T(128)S(1)} %concatenate.9.place_ref.table_ref, bf16[28,8,512]{2,1,0:T(8,128)(2,1)S(1)} %collective-permute-done.28.refs_0_, bf16[28,8,512]{2,1,0:T(8,128)(2,1)S(1)} %collective-permute-done.29.refs_1_, ...), custom_call_target="tpu_custom_call", output_to_operand_aliasing={{}: (5, {})} | custom-call | flops 900000000 | tf_op jit(solution)/shard_map/unfold/pallas_call | solution.py:231
  120.6 1.9 %collective-permute-done.30.refs_2_ = bf16[28,8,512]{2,1,0:T(8,128)(2,1)S(1)} collective-permute-done((bf16[28,8,512]{2,1,0:T(8,128)(2,1)S(1)}, bf16[28,8,512]{2,1,0:T(8,128)(2,1)S(1)}, u32[]{:S(2)}, u32[]{:S(2)}) %collective-permute-start.30) | collective-permute-done | bytes 229408 | tf_op jit(solution)/shard_map/ppermute | solution.py:324
  122.9 1.5 %collective-permute-start.36 = (bf16[14,8,512]{2,1,0:T(8,128)(2,1)S(1)}, bf16[14,8,512]{2,1,0:T(8,128)(2,1)S(1)}, u32[]{:S(2)}, u32[]{:S(2)}) collective-permute-start(bf16[14,8,512]{2,1,0:T(8,128)(2,1)S(1)} %slice.12), channel_id=1, source_target_pairs={{0,8},{8,16},{16,24},{24,28},{28,20},{20,12},{12,4},{4,0},{1,9},{9... | collective-permute-start | bytes 344072 | tf_op jit(solution)/shard_map/ppermute | solution.py:324
  124.3 0.6 collective-permute-start.37
  125.0 1.5 %collective-permute-start.38 = (bf16[14,8,512]{2,1,0:T(8,128)(2,1)S(1)}, bf16[14,8,512]{2,1,0:T(8,128)(2,1)S(1)}, u32[]{:S(2)}, u32[]{:S(2)}) collective-permute-start(bf16[14,8,512]{2,1,0:T(8,128)(2,1)S(1)} %slice.14), channel_id=1, source_target_pairs={{0,8},{8,16},{16,24},{24,28},{28,20},{20,12},{12,4},{4,0},{1,9},{9... | collective-permute-start | bytes 344072 | tf_op jit(solution)/shard_map/ppermute | solution.py:324
  126.4 0.6 collective-permute-start.39
  127.1 2.0 %unfold.8.refs_2_ = f32[27,64,1024]{2,1,0:T(8,128)} custom-call(s32[30]{0:T(128)S(1)} %concatenate.9.place_ref.table_ref, bf16[28,8,512]{2,1,0:T(8,128)(2,1)S(1)} %collective-permute-done.33.refs_0_, bf16[28,8,512]{2,1,0:T(8,128)(2,1)S(1)} %collective-permute-done.34.refs_1_, ...), custom_call_target="tpu_custom_call", output_to_operand_aliasing={{}: (5, {})} | custom-call | flops 900000000 | tf_op jit(solution)/shard_map/unfold/pallas_call | solution.py:231
  129.1 1.5 %add_convert_fusion = bf16[18,256,128]{2,1,0:T(8,128)(2,1)} fusion(f32[18,256,128]{2,1,0:T(8,128)S(1)} %collective-permute-done.32, f32[18,256,128]{2,1,0:T(8,128)S(1)} %input_terms.7, f32[18,256,128]{2,1,0:T(8,128)S(1)} %collective-permute-done.35), kind=kLoop, calls=%fused_computation | loop fusion | flops 1769472 | bytes 8257536 | tf_op jit(solution)/shard_map/convert_element_type | solution.py:494
  130.9 1.1 collective-permute-done.39
  132.1 1.7 %unfold.9 = f32[27,64,1024]{2,1,0:T(8,128)} custom-call(s32[30]{0:T(128)S(1)} %concatenate.9.place_ref.table_ref, bf16[28,8,512]{2,1,0:T(8,128)(2,1)S(1)} %get-tuple-element.315.refs_0_, bf16[28,8,512]{2,1,0:T(8,128)(2,1)S(1)} %get-tuple-element.316.refs_1_, f32[27,64,1024]{2,1,0:T(8,128)} %unfold.8.refs_2_), custom_call_target="tpu_custom_call", output_to_operand_aliasing={{}: (3, {})} | custom-call | flops 900000000 | tf_op jit(solution)/shard_map/unfold/pallas_call | solution.py:231
  (60 shorter events, 8.7 us)
Async XLA Ops:
  2.9 13.9 %collective-permute-start.3 = (bf16[18,256,128]{2,1,0:T(8,128)(2,1)}, bf16[18,256,128]{2,1,0:T(8,128)(2,1)S(1)}, u32[]{:S(2)}, u32[]{:S(2)}) collective-permute-start(bf16[18,256,128]{2,1,0:T(8,128)(2,1)} %bitcast.25), channel_id=1, source_target_pairs={{0,1},{1,0},{2,3},{3,2},{4,5},{5,4},{6,7},{7,6},{8,9},{9,8},{10,11... | collective-permute-start | bytes 3538952 | tf_op jit(solution)/shard_map/ppermute | solution.py:416
  3.4 32.2 %collective-permute-start.2 = (bf16[18,256,128]{2,1,0:T(8,128)(2,1)}, bf16[18,256,128]{2,1,0:T(8,128)(2,1)S(1)}, u32[]{:S(2)}, u32[]{:S(2)}) collective-permute-start(bf16[18,256,128]{2,1,0:T(8,128)(2,1)} %bitcast.26), channel_id=1, source_target_pairs={{0,2},{1,3},{2,0},{3,1},{4,6},{5,7},{6,4},{7,5},{8,10},{9,11},{10,... | collective-permute-start | bytes 3538952 | tf_op jit(solution)/shard_map/ppermute | solution.py:415
  5.9 29.7 %collective-permute-start = (bf16[36,64,128]{2,1,0:T(8,128)(2,1)}, bf16[36,64,128]{2,1,0:T(8,128)(2,1)}, u32[]{:S(2)}, u32[]{:S(2)}) collective-permute-start(bf16[36,64,128]{2,1,0:T(8,128)(2,1)} %get-tuple-element.160), channel_id=1, source_target_pairs={{0,4},{4,8},{8,12},{12,16},{16,20},{20,24},{24,28},{28,0},{1,5},{5... | collective-permute-start | bytes 1769480 | tf_op jit(solution)/shard_map/ppermute | solution.py:409
  7.4 28.1 %collective-permute-start.1 = (bf16[36,64,128]{2,1,0:T(8,128)(2,1)}, bf16[36,64,128]{2,1,0:T(8,128)(2,1)}, u32[]{:S(2)}, u32[]{:S(2)}) collective-permute-start(bf16[36,64,128]{2,1,0:T(8,128)(2,1)} %get-tuple-element.164), channel_id=1, source_target_pairs={{4,0},{8,4},{12,8},{16,12},{20,16},{24,20},{28,24},{0,28},{5,1},{9... | collective-permute-start | bytes 1769480 | tf_op jit(solution)/shard_map/ppermute | solution.py:410
  11.0 5.9 %copy-start.1 = (bf16[256,1,18,128]{3,0,2,1:T(8,128)(2,1)S(1)}, bf16[256,1,18,128]{3,0,2,1:T(8,128)(2,1)}, u32[]{:S(2)}) copy-start(bf16[256,1,18,128]{3,0,2,1:T(8,128)(2,1)} %param.3) | copy-start | bytes 3538948
  16.8 18.7 %copy-start = (bf16[1728,1024]{0,1:T(8,128)(2,1)S(1)}, bf16[1728,1024]{0,1:T(8,128)(2,1)}, u32[]{:S(2)}) copy-start(bf16[1728,1024]{0,1:T(8,128)(2,1)} %copy.10) | copy-start | bytes 10616836
  16.9 18.7 %copy-start.2 = (bf16[3,64,1,18,128]{4,1,3,2,0:T(8,128)(2,1)S(1)}, bf16[3,64,1,18,128]{4,1,3,2,0:T(8,128)(2,1)}, u32[]{:S(2)}) copy-start(bf16[3,64,1,18,128]{4,1,3,2,0:T(8,128)(2,1)} %param.4) | copy-start | bytes 2654212
  35.5 10.3 %collective-permute-start.4 = (bf16[18,256,128]{2,1,0:T(8,128)(2,1)S(1)}, bf16[18,256,128]{2,1,0:T(8,128)(2,1)S(1)}, u32[]{:S(2)}, u32[]{:S(2)}) collective-permute-start(bf16[18,256,128]{2,1,0:T(8,128)(2,1)S(1)} %collective-permute-done.2.first_ref), channel_id=1, source_target_pairs={{0,1},{1,0},{2,3},{3,2},{4,5},{5,4},{6,7},{7,6},{8,9},{9,8},{10,11... | collective-permute-start | bytes 3538952 | tf_op jit(solution)/shard_map/ppermute | solution.py:427
  43.8 6.1 %collective-permute-start.6 = (bf16[14,8,512]{2,1,0:T(8,128)(2,1)S(1)}, bf16[14,8,512]{2,1,0:T(8,128)(2,1)S(1)}, u32[]{:S(2)}, u32[]{:S(2)}) collective-permute-start(bf16[14,8,512]{2,1,0:T(8,128)(2,1)S(1)} %get-tuple-element.187), channel_id=1, source_target_pairs={{8,0},{16,8},{24,16},{28,24},{20,28},{12,20},{4,12},{0,4},{9,1},{1... | collective-permute-start | bytes 344072 | tf_op jit(solution)/shard_map/ppermute | solution.py:324
  44.1 5.8 %collective-permute-start.5 = (bf16[15,8,512]{2,1,0:T(8,128)(2,1)S(1)}, bf16[15,8,512]{2,1,0:T(8,128)(2,1)S(1)}, u32[]{:S(2)}, u32[]{:S(2)}) collective-permute-start(bf16[15,8,512]{2,1,0:T(8,128)(2,1)S(1)} %get-tuple-element.183), channel_id=1, source_target_pairs={{0,8},{8,16},{16,24},{24,28},{28,20},{20,12},{12,4},{4,0},{1,9},{9... | collective-permute-start | bytes 368648 | tf_op jit(solution)/shard_map/ppermute | solution.py:324
  50.4 10.0 %collective-permute-start.9 = (f32[18,256,128]{2,1,0:T(8,128)S(1)}, f32[18,256,128]{2,1,0:T(8,128)S(1)}, u32[]{:S(2)}, u32[]{:S(2)}) collective-permute-start(f32[18,256,128]{2,1,0:T(8,128)S(1)} %input_terms.4), channel_id=1, source_target_pairs={{0,1},{1,0},{2,3},{3,2},{4,5},{5,4},{6,7},{7,6},{8,9},{9,8},{10,11... | collective-permute-start | bytes 7077896 | tf_op jit(solution)/shard_map/ppermute | solution.py:454
  50.5 14.5 %collective-permute-start.12 = (bf16[28,8,512]{2,1,0:T(8,128)(2,1)S(1)}, bf16[28,8,512]{2,1,0:T(8,128)(2,1)S(1)}, u32[]{:S(2)}, u32[]{:S(2)}) collective-permute-start(bf16[28,8,512]{2,1,0:T(8,128)(2,1)S(1)} %get-tuple-element.197), channel_id=1, source_target_pairs={{0,8},{8,16},{16,24},{24,28},{28,20},{20,12},{12,4},{4,0},{1,9},{9... | collective-permute-start | bytes 688136 | tf_op jit(solution)/shard_map/ppermute | solution.py:324
  51.9 13.1 %collective-permute-start.13 = (bf16[28,8,512]{2,1,0:T(8,128)(2,1)S(1)}, bf16[28,8,512]{2,1,0:T(8,128)(2,1)S(1)}, u32[]{:S(2)}, u32[]{:S(2)}) collective-permute-start(bf16[28,8,512]{2,1,0:T(8,128)(2,1)S(1)} %get-tuple-element.220), channel_id=1, source_target_pairs={{8,0},{16,8},{24,16},{28,24},{20,28},{12,20},{4,12},{0,4},{9,1},{1... | collective-permute-start | bytes 688136 | tf_op jit(solution)/shard_map/ppermute | solution.py:324
  58.3 6.2 %collective-permute-start.7 = (bf16[15,8,512]{2,1,0:T(8,128)(2,1)S(1)}, bf16[15,8,512]{2,1,0:T(8,128)(2,1)S(1)}, u32[]{:S(2)}, u32[]{:S(2)}) collective-permute-start(bf16[15,8,512]{2,1,0:T(8,128)(2,1)S(1)} %get-tuple-element.205), channel_id=1, source_target_pairs={{0,8},{8,16},{16,24},{24,28},{28,20},{20,12},{12,4},{4,0},{1,9},{9... | collective-permute-start | bytes 368648 | tf_op jit(solution)/shard_map/ppermute | solution.py:324
  59.7 4.8 %collective-permute-start.8 = (bf16[14,8,512]{2,1,0:T(8,128)(2,1)S(1)}, bf16[14,8,512]{2,1,0:T(8,128)(2,1)S(1)}, u32[]{:S(2)}, u32[]{:S(2)}) collective-permute-start(bf16[14,8,512]{2,1,0:T(8,128)(2,1)S(1)} %get-tuple-element.206), channel_id=1, source_target_pairs={{8,0},{16,8},{24,16},{28,24},{20,28},{12,20},{4,12},{0,4},{9,1},{1... | collective-permute-start | bytes 344072 | tf_op jit(solution)/shard_map/ppermute | solution.py:324
  65.6 54.9 %collective-permute-start.32 = (f32[18,256,128]{2,1,0:T(8,128)S(1)}, f32[18,256,128]{2,1,0:T(8,128)S(1)}, u32[]{:S(2)}, u32[]{:S(2)}) collective-permute-start(f32[18,256,128]{2,1,0:T(8,128)S(1)} %input_terms.5), channel_id=1, source_target_pairs={{0,2},{1,3},{2,0},{3,1},{4,6},{5,7},{6,4},{7,5},{8,10},{9,11},{10,... | collective-permute-start | bytes 7077896 | tf_op jit(solution)/shard_map/ppermute | solution.py:461
  66.2 8.3 %collective-permute-start.11 = (bf16[28,8,512]{2,1,0:T(8,128)(2,1)S(1)}, bf16[28,8,512]{2,1,0:T(8,128)(2,1)S(1)}, u32[]{:S(2)}, u32[]{:S(2)}) collective-permute-start(bf16[28,8,512]{2,1,0:T(8,128)(2,1)S(1)} %get-tuple-element.219), channel_id=1, source_target_pairs={{8,0},{16,8},{24,16},{28,24},{20,28},{12,20},{4,12},{0,4},{9,1},{1... | collective-permute-start | bytes 688136 | tf_op jit(solution)/shard_map/ppermute | solution.py:324
  66.9 8.5 %collective-permute-start.10 = (bf16[28,8,512]{2,1,0:T(8,128)(2,1)S(1)}, bf16[28,8,512]{2,1,0:T(8,128)(2,1)S(1)}, u32[]{:S(2)}, u32[]{:S(2)}) collective-permute-start(bf16[28,8,512]{2,1,0:T(8,128)(2,1)S(1)} %get-tuple-element.218), channel_id=1, source_target_pairs={{0,8},{8,16},{16,24},{24,28},{28,20},{20,12},{12,4},{4,0},{1,9},{9... | collective-permute-start | bytes 688136 | tf_op jit(solution)/shard_map/ppermute | solution.py:324
  68.3 12.1 %collective-permute-start.16 = (bf16[28,8,512]{2,1,0:T(8,128)(2,1)S(1)}, bf16[28,8,512]{2,1,0:T(8,128)(2,1)S(1)}, u32[]{:S(2)}, u32[]{:S(2)}) collective-permute-start(bf16[28,8,512]{2,1,0:T(8,128)(2,1)S(1)} %get-tuple-element.227), channel_id=1, source_target_pairs={{0,8},{8,16},{16,24},{24,28},{28,20},{20,12},{12,4},{4,0},{1,9},{9... | collective-permute-start | bytes 688136 | tf_op jit(solution)/shard_map/ppermute | solution.py:324
  69.7 9.8 %collective-permute-start.17 = (bf16[28,8,512]{2,1,0:T(8,128)(2,1)S(1)}, bf16[28,8,512]{2,1,0:T(8,128)(2,1)S(1)}, u32[]{:S(2)}, u32[]{:S(2)}) collective-permute-start(bf16[28,8,512]{2,1,0:T(8,128)(2,1)S(1)} %get-tuple-element.239), channel_id=1, source_target_pairs={{8,0},{16,8},{24,16},{28,24},{20,28},{12,20},{4,12},{0,4},{9,1},{1... | collective-permute-start | bytes 688136 | tf_op jit(solution)/shard_map/ppermute | solution.py:324
  76.1 8.6 %collective-permute-start.15 = (bf16[28,8,512]{2,1,0:T(8,128)(2,1)S(1)}, bf16[28,8,512]{2,1,0:T(8,128)(2,1)S(1)}, u32[]{:S(2)}, u32[]{:S(2)}) collective-permute-start(bf16[28,8,512]{2,1,0:T(8,128)(2,1)S(1)} %get-tuple-element.238), channel_id=1, source_target_pairs={{8,0},{16,8},{24,16},{28,24},{20,28},{12,20},{4,12},{0,4},{9,1},{1... | collective-permute-start | bytes 688136 | tf_op jit(solution)/shard_map/ppermute | solution.py:324
  77.3 8.1 %collective-permute-start.14 = (bf16[28,8,512]{2,1,0:T(8,128)(2,1)S(1)}, bf16[28,8,512]{2,1,0:T(8,128)(2,1)S(1)}, u32[]{:S(2)}, u32[]{:S(2)}) collective-permute-start(bf16[28,8,512]{2,1,0:T(8,128)(2,1)S(1)} %get-tuple-element.237), channel_id=1, source_target_pairs={{0,8},{8,16},{16,24},{24,28},{28,20},{20,12},{12,4},{4,0},{1,9},{9... | collective-permute-start | bytes 688136 | tf_op jit(solution)/shard_map/ppermute | solution.py:324
  81.0 9.9 %collective-permute-start.21 = (bf16[28,8,512]{2,1,0:T(8,128)(2,1)S(1)}, bf16[28,8,512]{2,1,0:T(8,128)(2,1)S(1)}, u32[]{:S(2)}, u32[]{:S(2)}) collective-permute-start(bf16[28,8,512]{2,1,0:T(8,128)(2,1)S(1)} %get-tuple-element.258), channel_id=1, source_target_pairs={{8,0},{16,8},{24,16},{28,24},{20,28},{12,20},{4,12},{0,4},{9,1},{1... | collective-permute-start | bytes 688136 | tf_op jit(solution)/shard_map/ppermute | solution.py:324
  82.2 8.7 %collective-permute-start.20 = (bf16[28,8,512]{2,1,0:T(8,128)(2,1)S(1)}, bf16[28,8,512]{2,1,0:T(8,128)(2,1)S(1)}, u32[]{:S(2)}, u32[]{:S(2)}) collective-permute-start(bf16[28,8,512]{2,1,0:T(8,128)(2,1)S(1)} %get-tuple-element.246), channel_id=1, source_target_pairs={{0,8},{8,16},{16,24},{24,28},{28,20},{20,12},{12,4},{4,0},{1,9},{9... | collective-permute-start | bytes 688136 | tf_op jit(solution)/shard_map/ppermute | solution.py:324
  86.0 8.6 %collective-permute-start.19 = (bf16[28,8,512]{2,1,0:T(8,128)(2,1)S(1)}, bf16[28,8,512]{2,1,0:T(8,128)(2,1)S(1)}, u32[]{:S(2)}, u32[]{:S(2)}) collective-permute-start(bf16[28,8,512]{2,1,0:T(8,128)(2,1)S(1)} %get-tuple-element.257), channel_id=1, source_target_pairs={{8,0},{16,8},{24,16},{28,24},{20,28},{12,20},{4,12},{0,4},{9,1},{1... | collective-permute-start | bytes 688136 | tf_op jit(solution)/shard_map/ppermute | solution.py:324
  87.3 8.5 %collective-permute-start.18 = (bf16[28,8,512]{2,1,0:T(8,128)(2,1)S(1)}, bf16[28,8,512]{2,1,0:T(8,128)(2,1)S(1)}, u32[]{:S(2)}, u32[]{:S(2)}) collective-permute-start(bf16[28,8,512]{2,1,0:T(8,128)(2,1)S(1)} %get-tuple-element.253), channel_id=1, source_target_pairs={{0,8},{8,16},{16,24},{24,28},{28,20},{20,12},{12,4},{4,0},{1,9},{9... | collective-permute-start | bytes 688136 | tf_op jit(solution)/shard_map/ppermute | solution.py:324
  91.4 8.6 %collective-permute-start.25 = (bf16[28,8,512]{2,1,0:T(8,128)(2,1)S(1)}, bf16[28,8,512]{2,1,0:T(8,128)(2,1)S(1)}, u32[]{:S(2)}, u32[]{:S(2)}) collective-permute-start(bf16[28,8,512]{2,1,0:T(8,128)(2,1)S(1)} %last_hop.2.refs_0_), channel_id=1, source_target_pairs={{8,0},{16,8},{24,16},{28,24},{20,28},{12,20},{4,12},{0,4},{9,1},{1... | collective-permute-start | bytes 688136 | tf_op jit(solution)/shard_map/ppermute | solution.py:324
  92.8 8.5 %collective-permute-start.24 = (bf16[28,8,512]{2,1,0:T(8,128)(2,1)S(1)}, bf16[28,8,512]{2,1,0:T(8,128)(2,1)S(1)}, u32[]{:S(2)}, u32[]{:S(2)}) collective-permute-start(bf16[28,8,512]{2,1,0:T(8,128)(2,1)S(1)} %last_hop.2.refs_0_), channel_id=1, source_target_pairs={{0,8},{8,16},{16,24},{24,28},{28,20},{20,12},{12,4},{4,0},{1,9},{9... | collective-permute-start | bytes 688136 | tf_op jit(solution)/shard_map/ppermute | solution.py:324
  96.3 8.8 %collective-permute-start.23 = (bf16[28,8,512]{2,1,0:T(8,128)(2,1)S(1)}, bf16[28,8,512]{2,1,0:T(8,128)(2,1)S(1)}, u32[]{:S(2)}, u32[]{:S(2)}) collective-permute-start(bf16[28,8,512]{2,1,0:T(8,128)(2,1)S(1)} %last_hop.3.refs_0_), channel_id=1, source_target_pairs={{8,0},{16,8},{24,16},{28,24},{20,28},{12,20},{4,12},{0,4},{9,1},{1... | collective-permute-start | bytes 688136 | tf_op jit(solution)/shard_map/ppermute | solution.py:324
  98.1 8.5 %collective-permute-start.22 = (bf16[28,8,512]{2,1,0:T(8,128)(2,1)S(1)}, bf16[28,8,512]{2,1,0:T(8,128)(2,1)S(1)}, u32[]{:S(2)}, u32[]{:S(2)}) collective-permute-start(bf16[28,8,512]{2,1,0:T(8,128)(2,1)S(1)} %last_hop.3.refs_0_), channel_id=1, source_target_pairs={{0,8},{8,16},{16,24},{24,28},{28,20},{20,12},{12,4},{4,0},{1,9},{9... | collective-permute-start | bytes 688136 | tf_op jit(solution)/shard_map/ppermute | solution.py:324
  101.3 10.3 %collective-permute-start.28 = (bf16[28,8,512]{2,1,0:T(8,128)(2,1)S(1)}, bf16[28,8,512]{2,1,0:T(8,128)(2,1)S(1)}, u32[]{:S(2)}, u32[]{:S(2)}) collective-permute-start(bf16[28,8,512]{2,1,0:T(8,128)(2,1)S(1)} %collective-permute-done.24.refs_1_), channel_id=1, source_target_pairs={{0,8},{8,16},{16,24},{24,28},{28,20},{20,12},{12,4},{4,0},{1,9},{9... | collective-permute-start | bytes 688136 | tf_op jit(solution)/shard_map/ppermute | solution.py:324
  102.1 9.5 %collective-permute-start.29 = (bf16[28,8,512]{2,1,0:T(8,128)(2,1)S(1)}, bf16[28,8,512]{2,1,0:T(8,128)(2,1)S(1)}, u32[]{:S(2)}, u32[]{:S(2)}) collective-permute-start(bf16[28,8,512]{2,1,0:T(8,128)(2,1)S(1)} %collective-permute-done.25.refs_2_), channel_id=1, source_target_pairs={{8,0},{16,8},{24,16},{28,24},{20,28},{12,20},{4,12},{0,4},{9,1},{1... | collective-permute-start | bytes 688136 | tf_op jit(solution)/shard_map/ppermute | solution.py:324
  106.6 9.8 %collective-permute-start.26 = (bf16[28,8,512]{2,1,0:T(8,128)(2,1)S(1)}, bf16[28,8,512]{2,1,0:T(8,128)(2,1)S(1)}, u32[]{:S(2)}, u32[]{:S(2)}) collective-permute-start(bf16[28,8,512]{2,1,0:T(8,128)(2,1)S(1)} %collective-permute-done.22.refs_1_), channel_id=1, source_target_pairs={{0,8},{8,16},{16,24},{24,28},{28,20},{20,12},{12,4},{4,0},{1,9},{9... | collective-permute-start | bytes 688136 | tf_op jit(solution)/shard_map/ppermute | solution.py:324
  107.0 9.5 %collective-permute-start.27 = (bf16[28,8,512]{2,1,0:T(8,128)(2,1)S(1)}, bf16[28,8,512]{2,1,0:T(8,128)(2,1)S(1)}, u32[]{:S(2)}, u32[]{:S(2)}) collective-permute-start(bf16[28,8,512]{2,1,0:T(8,128)(2,1)S(1)} %collective-permute-done.23.refs_2_), channel_id=1, source_target_pairs={{8,0},{16,8},{24,16},{28,24},{20,28},{12,20},{4,12},{0,4},{9,1},{1... | collective-permute-start | bytes 688136 | tf_op jit(solution)/shard_map/ppermute | solution.py:324
  111.6 9.0 %collective-permute-start.34 = (bf16[28,8,512]{2,1,0:T(8,128)(2,1)S(1)}, bf16[28,8,512]{2,1,0:T(8,128)(2,1)S(1)}, u32[]{:S(2)}, u32[]{:S(2)}) collective-permute-start(bf16[28,8,512]{2,1,0:T(8,128)(2,1)S(1)} %collective-permute-done.29.refs_1_), channel_id=1, source_target_pairs={{8,0},{16,8},{24,16},{28,24},{20,28},{12,20},{4,12},{0,4},{9,1},{1... | collective-permute-start | bytes 688136 | tf_op jit(solution)/shard_map/ppermute | solution.py:324
  113.0 7.5 %collective-permute-start.33 = (bf16[28,8,512]{2,1,0:T(8,128)(2,1)S(1)}, bf16[28,8,512]{2,1,0:T(8,128)(2,1)S(1)}, u32[]{:S(2)}, u32[]{:S(2)}) collective-permute-start(bf16[28,8,512]{2,1,0:T(8,128)(2,1)S(1)} %collective-permute-done.28.refs_0_), channel_id=1, source_target_pairs={{0,8},{8,16},{16,24},{24,28},{28,20},{20,12},{12,4},{4,0},{1,9},{9... | collective-permute-start | bytes 688136 | tf_op jit(solution)/shard_map/ppermute | solution.py:324
  116.5 6.0 %collective-permute-start.30 = (bf16[28,8,512]{2,1,0:T(8,128)(2,1)S(1)}, bf16[28,8,512]{2,1,0:T(8,128)(2,1)S(1)}, u32[]{:S(2)}, u32[]{:S(2)}) collective-permute-start(bf16[28,8,512]{2,1,0:T(8,128)(2,1)S(1)} %collective-permute-done.26.refs_2_), channel_id=1, source_target_pairs={{0,8},{8,16},{16,24},{24,28},{28,20},{20,12},{12,4},{4,0},{1,9},{9... | collective-permute-start | bytes 688136 | tf_op jit(solution)/shard_map/ppermute | solution.py:324
  116.8 6.0 %collective-permute-start.31 = (bf16[28,8,512]{2,1,0:T(8,128)(2,1)S(1)}, bf16[28,8,512]{2,1,0:T(8,128)(2,1)S(1)}, u32[]{:S(2)}, u32[]{:S(2)}) collective-permute-start(bf16[28,8,512]{2,1,0:T(8,128)(2,1)S(1)} %collective-permute-done.27.refs_3_), channel_id=1, source_target_pairs={{8,0},{16,8},{24,16},{28,24},{20,28},{12,20},{4,12},{0,4},{9,1},{1... | collective-permute-start | bytes 688136 | tf_op jit(solution)/shard_map/ppermute | solution.py:324
  122.8 6.3 %collective-permute-start.35 = (f32[18,256,128]{2,1,0:T(8,128)S(1)}, f32[18,256,128]{2,1,0:T(8,128)S(1)}, u32[]{:S(2)}, u32[]{:S(2)}) collective-permute-start(f32[18,256,128]{2,1,0:T(8,128)S(1)} %input_terms.6), channel_id=1, source_target_pairs={{0,1},{1,0},{2,3},{3,2},{4,5},{5,4},{6,7},{7,6},{8,9},{9,8},{10,11... | collective-permute-start | bytes 7077896 | tf_op jit(solution)/shard_map/ppermute | solution.py:492
  122.9 9.2 %collective-permute-start.36 = (bf16[14,8,512]{2,1,0:T(8,128)(2,1)S(1)}, bf16[14,8,512]{2,1,0:T(8,128)(2,1)S(1)}, u32[]{:S(2)}, u32[]{:S(2)}) collective-permute-start(bf16[14,8,512]{2,1,0:T(8,128)(2,1)S(1)} %slice.12), channel_id=1, source_target_pairs={{0,8},{8,16},{16,24},{24,28},{28,20},{20,12},{12,4},{4,0},{1,9},{9... | collective-permute-start | bytes 344072 | tf_op jit(solution)/shard_map/ppermute | solution.py:324
  124.3 7.7 %collective-permute-start.37 = (bf16[14,8,512]{2,1,0:T(8,128)(2,1)S(1)}, bf16[14,8,512]{2,1,0:T(8,128)(2,1)S(1)}, u32[]{:S(2)}, u32[]{:S(2)}) collective-permute-start(bf16[14,8,512]{2,1,0:T(8,128)(2,1)S(1)} %slice.13), channel_id=1, source_target_pairs={{8,0},{16,8},{24,16},{28,24},{20,28},{12,20},{4,12},{0,4},{9,1},{1... | collective-permute-start | bytes 344072 | tf_op jit(solution)/shard_map/ppermute | solution.py:324
  125.0 6.0 %collective-permute-start.38 = (bf16[14,8,512]{2,1,0:T(8,128)(2,1)S(1)}, bf16[14,8,512]{2,1,0:T(8,128)(2,1)S(1)}, u32[]{:S(2)}, u32[]{:S(2)}) collective-permute-start(bf16[14,8,512]{2,1,0:T(8,128)(2,1)S(1)} %slice.14), channel_id=1, source_target_pairs={{0,8},{8,16},{16,24},{24,28},{28,20},{20,12},{12,4},{4,0},{1,9},{9... | collective-permute-start | bytes 344072 | tf_op jit(solution)/shard_map/ppermute | solution.py:324
  126.4 5.6 %collective-permute-start.39 = (bf16[14,8,512]{2,1,0:T(8,128)(2,1)S(1)}, bf16[14,8,512]{2,1,0:T(8,128)(2,1)S(1)}, u32[]{:S(2)}, u32[]{:S(2)}) collective-permute-start(bf16[14,8,512]{2,1,0:T(8,128)(2,1)S(1)} %slice.15), channel_id=1, source_target_pairs={{8,0},{16,8},{24,16},{28,24},{20,28},{12,20},{4,12},{0,4},{9,1},{1... | collective-permute-start | bytes 344072 | tf_op jit(solution)/shard_map/ppermute | solution.py:324
